TPU v7x, 32 devices: a whole 2x2x4 slice. The times are simulated.
32 devices in a mesh: seq: 4 (over y, x), dp: 8 (over z, core).
Axes of the slice: x: 2, y: 2, z: 4, core: 2. Of those that a mesh axis runs over, the one named last changes fastest.
Arguments:
- inputs: bfloat16 [16, 1024, 2048], P('dp', 'seq'), may hold values from -6 to 6
- counts: int32 [8], P('dp'), may hold values from 1 to 2, as said below
- cotangent: bfloat16 [16, 1024, 2048], P('dp', 'seq'), may hold values from -6 to 6
- stretch: bfloat16 [2048], P(('seq', 'dp')), may hold values from 0.099609375 to 1.8984375
- offset: bfloat16 [2048], P(('seq', 'dp')), may hold values from -1.5 to 1.5
- inward: bfloat16 [2048, 6144], P(('seq', 'dp')), may hold values from -0.1875 to 0.1875
- outward: bfloat16 [2048, 2048], P(('seq', 'dp')), may hold values from -0.25 to 0.25
- dilation: bfloat16 [2048], P(('seq', 'dp')), may hold values from 0.099609375 to 1.8984375
- translation: bfloat16 [2048], P(('seq', 'dp')), may hold values from -1.5 to 1.5
- upward: bfloat16 [2048, 8192], P(('seq', 'dp')), may hold values from -0.125 to 0.125
- downward: bfloat16 [8192, 2048], P(('seq', 'dp')), may hold values from -0.0625 to 0.0625
Outputs:
- outputs: bfloat16 [16, 1024, 2048], P('dp', 'seq')
- input_delta: float32 [16, 1024, 2048], P('dp', 'seq')
- stretch_delta: float32 [2048], P(('seq', 'dp'))
- offset_delta: float32 [2048], P(('seq', 'dp'))
- inward_delta: float32 [2048, 6144], P(('seq', 'dp'))
- outward_delta: float32 [2048, 2048], P(('seq', 'dp'))
- dilation_delta: float32 [2048], P(('seq', 'dp'))
- translation_delta: float32 [2048], P(('seq', 'dp'))
- upward_delta: float32 [2048, 8192], P(('seq', 'dp'))
- downward_delta: float32 [8192, 2048], P(('seq', 'dp'))
Inputs may be any that keep to these rules, and one draw needn't show every extreme that they name: Slots 0 to counts - 1 of a group hold sequences, later slots of the group none; some group uses all 2 slots and some other group only one.
All inputs are finite; a program needn't handle non-finite values.
Results may differ from a plain program's by a relative error of at most 0.013.
The roundings to bfloat16 on the way count: a program that leaves them out, or rounds other values in their place, can miss the bound.
Values may be sent and summed in bfloat16 or wider, within the bound.
A program may use at most 768 MiB of HBM per device.

v0:
```python
import math

import jax
import jax.numpy as jnp
from jax import lax
from jax.sharding import PartitionSpec as P

HEADS = 16


EPSILON = 1e-05
MASKED = -1e30


def layer_norm(values, gain, shift):
    average = jnp.mean(values, axis=-1, keepdims=True)
    centered = values - average
    variance = jnp.mean(centered * centered, axis=-1, keepdims=True)
    return centered * lax.rsqrt(variance + EPSILON) * gain + shift


def smooth_gate(values):
    return jax.nn.gelu(values, approximate=True)


def contract_rows(left, right):
    return lax.dot_general(
        left, right, (((0,), (0,)), ((), ())), preferred_element_type=jnp.float32
    )


def contract_cols(left, right):
    return lax.dot_general(
        left, right, (((1,), (1,)), ((), ())), preferred_element_type=jnp.float32
    )


def attention_probs(query_heads, key_heads, causal, scaling):
    logits = (
        jnp.einsum("sqhd,skhd->shqk", query_heads, key_heads, preferred_element_type=jnp.float32)
        * scaling
    )
    masked = jnp.where(causal[None, None], logits, MASKED)
    return jax.nn.softmax(masked, axis=-1)


def forward(
    inputs, counts, stretch, offset, inward, outward, dilation, translation, upward, downward
):
    full_stretch, full_offset, matrix_in, matrix_out = (
        lax.all_gather(stretch, ("seq", "dp"), axis=0, tiled=True),
        lax.all_gather(offset, ("seq", "dp"), axis=0, tiled=True),
        lax.all_gather(inward, ("seq", "dp"), axis=0, tiled=True),
        lax.all_gather(outward, ("seq", "dp"), axis=0, tiled=True),
    )
    slot_count, block_rows, model_width = inputs.shape
    head_size = model_width // HEADS
    scaling = 1.0 / math.sqrt(head_size)
    live_slots = (jnp.arange(slot_count) < counts[0]).astype(jnp.float32)
    live_rows = jnp.repeat(live_slots, block_rows)[:, None]
    residual = inputs.astype(jnp.float32).reshape(slot_count * block_rows, model_width)
    normed_low = layer_norm(
        residual, full_stretch.astype(jnp.float32), full_offset.astype(jnp.float32)
    ).astype(jnp.bfloat16)
    projected = jnp.dot(normed_low, matrix_in, preferred_element_type=jnp.float32).astype(
        jnp.bfloat16
    )
    keys_values = lax.all_gather(
        projected[:, model_width:].reshape(slot_count, block_rows, 2 * model_width),
        "seq",
        axis=1,
        tiled=True,
    )
    length = keys_values.shape[1]
    query_place = lax.axis_index("seq") * block_rows + jnp.arange(block_rows)
    causal = jnp.arange(length)[None, :] <= query_place[:, None]
    query_heads = projected[:, :model_width].reshape(slot_count, block_rows, HEADS, head_size)
    key_heads = keys_values[:, :, :model_width].reshape(slot_count, length, HEADS, head_size)
    value_heads = keys_values[:, :, model_width:].reshape(slot_count, length, HEADS, head_size)
    weights_low = attention_probs(query_heads, key_heads, causal, scaling).astype(jnp.bfloat16)
    mixture = jnp.einsum(
        "shqk,skhd->sqhd", weights_low, value_heads, preferred_element_type=jnp.float32
    )
    attended = mixture.reshape(slot_count * block_rows, model_width).astype(jnp.bfloat16)
    middle = residual + jnp.dot(attended, matrix_out, preferred_element_type=jnp.float32)
    full_dilation, full_translation, matrix_up, matrix_down = (
        lax.all_gather(dilation, ("seq", "dp"), axis=0, tiled=True),
        lax.all_gather(translation, ("seq", "dp"), axis=0, tiled=True),
        lax.all_gather(upward, ("seq", "dp"), axis=0, tiled=True),
        lax.all_gather(downward, ("seq", "dp"), axis=0, tiled=True),
    )
    normed_two = layer_norm(
        middle, full_dilation.astype(jnp.float32), full_translation.astype(jnp.float32)
    ).astype(jnp.bfloat16)
    expanded = jnp.dot(normed_two, matrix_up, preferred_element_type=jnp.float32)
    hidden_low = smooth_gate(expanded).astype(jnp.bfloat16)
    result = middle + jnp.dot(hidden_low, matrix_down, preferred_element_type=jnp.float32)
    outputs = (result * live_rows).astype(jnp.bfloat16).reshape(slot_count, block_rows, model_width)
    stored = (
        residual,
        live_rows,
        full_stretch,
        full_offset,
        matrix_in,
        matrix_out,
        normed_low,
        projected,
        keys_values,
        causal,
        attended,
        middle,
        full_dilation,
        full_translation,
        matrix_up,
        matrix_down,
        normed_two,
        expanded,
        hidden_low,
    )
    return (outputs, stored)


def per_device(
    inputs,
    counts,
    cotangent,
    stretch,
    offset,
    inward,
    outward,
    dilation,
    translation,
    upward,
    downward,
):
    outputs, stored = forward(
        inputs, counts, stretch, offset, inward, outward, dilation, translation, upward, downward
    )
    fresh = lax.optimization_barrier(
        (inputs, counts, stretch, offset, inward, outward, dilation, translation, upward, downward)
    )
    stored = forward(*fresh)[1]
    (
        residual,
        live_rows,
        full_stretch,
        full_offset,
        matrix_in,
        matrix_out,
        normed_low,
        projected,
        keys_values,
        causal,
        attended,
        middle,
        full_dilation,
        full_translation,
        matrix_up,
        matrix_down,
        normed_two,
        expanded,
        hidden_low,
    ) = stored
    slot_count, block_rows, model_width = inputs.shape
    head_size = model_width // HEADS
    scaling = 1.0 / math.sqrt(head_size)
    length = keys_values.shape[1]
    upstream = (
        cotangent.astype(jnp.float32).reshape(slot_count * block_rows, model_width) * live_rows
    )
    upstream_low = upstream.astype(jnp.bfloat16)
    down_term = contract_rows(hidden_low, upstream_low)
    downward_delta = lax.psum_scatter(down_term, ("seq", "dp"), scatter_dimension=0, tiled=True)
    hidden_back = contract_cols(upstream_low, matrix_down)
    gate_value, gate_pull = jax.vjp(smooth_gate, expanded)
    expanded_back = gate_pull(hidden_back)[0].astype(jnp.bfloat16)
    up_term = contract_rows(normed_two, expanded_back)
    normed_two_back = contract_cols(expanded_back, matrix_up)
    norm_value, norm_pull = jax.vjp(
        layer_norm, middle, full_dilation.astype(jnp.float32), full_translation.astype(jnp.float32)
    )
    middle_norm_back, dilation_term, translation_term = norm_pull(normed_two_back)
    dilation_delta, translation_delta, upward_delta = (
        lax.psum_scatter(dilation_term, ("seq", "dp"), scatter_dimension=0, tiled=True),
        lax.psum_scatter(translation_term, ("seq", "dp"), scatter_dimension=0, tiled=True),
        lax.psum_scatter(up_term, ("seq", "dp"), scatter_dimension=0, tiled=True),
    )
    middle_back = upstream + middle_norm_back
    middle_low = middle_back.astype(jnp.bfloat16)
    out_term = contract_rows(attended, middle_low)
    attended_back = contract_cols(middle_low, matrix_out).astype(jnp.bfloat16)
    heads_back = attended_back.reshape(slot_count, block_rows, HEADS, head_size)
    query_heads = projected[:, :model_width].reshape(slot_count, block_rows, HEADS, head_size)
    key_heads = keys_values[:, :, :model_width].reshape(slot_count, length, HEADS, head_size)
    value_heads = keys_values[:, :, model_width:].reshape(slot_count, length, HEADS, head_size)
    probs = attention_probs(query_heads, key_heads, causal, scaling)
    weights_low = probs.astype(jnp.bfloat16)
    prob_back = jnp.einsum(
        "sqhd,skhd->shqk", heads_back, value_heads, preferred_element_type=jnp.float32
    )
    value_term = jnp.einsum(
        "shqk,sqhd->skhd", weights_low, heads_back, preferred_element_type=jnp.float32
    )
    logit_back = probs * (prob_back - jnp.sum(probs * prob_back, axis=-1, keepdims=True))
    logit_low = logit_back.astype(jnp.bfloat16)
    query_back = (
        jnp.einsum("shqk,skhd->sqhd", logit_low, key_heads, preferred_element_type=jnp.float32)
        * scaling
    )
    key_term = (
        jnp.einsum("shqk,sqhd->skhd", logit_low, query_heads, preferred_element_type=jnp.float32)
        * scaling
    )
    key_delta, value_delta = (
        lax.psum_scatter(
            key_term.reshape(slot_count, length, model_width),
            "seq",
            scatter_dimension=1,
            tiled=True,
        ),
        lax.psum_scatter(
            value_term.reshape(slot_count, length, model_width),
            "seq",
            scatter_dimension=1,
            tiled=True,
        ),
    )
    total_rows = slot_count * block_rows
    projected_back = jnp.concatenate(
        [
            query_back.reshape(total_rows, model_width),
            key_delta.reshape(total_rows, model_width),
            value_delta.reshape(total_rows, model_width),
        ],
        axis=1,
    ).astype(jnp.bfloat16)
    in_term = contract_rows(normed_low, projected_back)
    normed_back = contract_cols(projected_back, matrix_in)
    first_value, first_pull = jax.vjp(
        layer_norm, residual, full_stretch.astype(jnp.float32), full_offset.astype(jnp.float32)
    )
    residual_norm_back, stretch_term, offset_term = first_pull(normed_back)
    stretch_delta, offset_delta, inward_delta, outward_delta = (
        lax.psum_scatter(stretch_term, ("seq", "dp"), scatter_dimension=0, tiled=True),
        lax.psum_scatter(offset_term, ("seq", "dp"), scatter_dimension=0, tiled=True),
        lax.psum_scatter(in_term, ("seq", "dp"), scatter_dimension=0, tiled=True),
        lax.psum_scatter(out_term, ("seq", "dp"), scatter_dimension=0, tiled=True),
    )
    input_delta = (middle_back + residual_norm_back).reshape(slot_count, block_rows, model_width)
    return (
        outputs,
        input_delta,
        stretch_delta,
        offset_delta,
        inward_delta,
        outward_delta,
        dilation_delta,
        translation_delta,
        upward_delta,
        downward_delta,
    )


def solution(mesh):
    in_specs = (
        P("dp", "seq", None),
        P("dp"),
        P("dp", "seq", None),
        P(("seq", "dp")),
        P(("seq", "dp")),
        P(("seq", "dp"), None),
        P(("seq", "dp"), None),
        P(("seq", "dp")),
        P(("seq", "dp")),
        P(("seq", "dp"), None),
        P(("seq", "dp"), None),
    )
    out_specs = (
        P("dp", "seq", None),
        P("dp", "seq", None),
        P(("seq", "dp")),
        P(("seq", "dp")),
        P(("seq", "dp"), None),
        P(("seq", "dp"), None),
        P(("seq", "dp")),
        P(("seq", "dp")),
        P(("seq", "dp"), None),
        P(("seq", "dp"), None),
    )
    return jax.shard_map(
        per_device, mesh=mesh, in_specs=in_specs, out_specs=out_specs, check_vma=False
    )
```

profile of v0, /device:TPU:0, one launch (start us, length us, event | category | flops | bytes accessed | tf_op | source)
XLA Modules:
  0.0 3950.9 jit_solution(18179705334635023295)
XLA Ops:
  15.5 43.5 %all-reduce.13 = (bf16[2048]{0:T(1024)(128)(2,1)}, bf16[2048]{0:T(1024)(128)(2,1)}, bf16[2048]{0:T(1024)(128)(2,1)}, bf16[2048]{0:T(1024)(128)(2,1)}, bf16[2048]...) all-reduce(bf16[2048]{0:T(1024)(128)(2,1)S(1)} %dynamic-update-slic, ...), channel_id=1, replica_groups=mesh['seq'=4,'dp'=8] {'seq','dp'}, use_global_device_ids=true, to_apply=%add.1 | all-reduce | flops 16384 | bytes 65536
  65.1 104.8 %all-gather.23.cloned.1.call-done = bf16[2048,6144]{1,0:T(8,128)(2,1)} async-done(((bf16[64,6144]{1,0:T(8,128)(2,1)}), bf16[2048,6144]{1,0:T(8,128)(2,1)}) %all-gather.23.cloned.1.call-update) | async-done | bytes 25165840 | tf_op jit(solution)/shard_map/all_gather | solution.py:53
  213.3 152.5 %all-gather.21.cloned.1.call-done = bf16[8192,2048]{1,0:T(8,128)(2,1)} async-done(((bf16[256,2048]{1,0:T(8,128)(2,1)}), bf16[8192,2048]{1,0:T(8,128)(2,1)}) %all-gather.21.cloned.1.call-update) | async-done | bytes 33554448 | tf_op jit(solution)/shard_map/all_gather | solution.py:90
  391.9 131.3 %all-gather.25.cloned.1.call-done = bf16[2,1024,4096]{1,2,0:T(8,128)(2,1)} async-done(((bf16[2,256,4096]{1,2,0:T(8,128)(2,1)}), bf16[2,1024,4096]{1,2,0:T(8,128)(2,1)}) %all-gather.25.cloned.1.call-update) | async-done | bytes 16777232 | tf_op jit(solution)/shard_map/all_gather | solution.py:68
  574.3 29.1 all-gather.27.cloned.1.call-done
  613.9 185.8 %all-gather.29.cloned.1.call-done = bf16[2048,8192]{1,0:T(8,128)(2,1)} async-done(((bf16[64,8192]{1,0:T(8,128)(2,1)}), bf16[2048,8192]{1,0:T(8,128)(2,1)}) %all-gather.29.cloned.1.call-update) | async-done | bytes 33554448 | tf_op jit(solution)/shard_map/all_gather | solution.py:89
  799.7 38.0 fusion.10
  837.7 27.3 multiply_reduce_fusion.1
  946.5 29.7 multiply_convert_fusion
  1074.6 36.0 reduce-scatter.9.cloned.1.call-done
  1114.5 153.1 %reduce-scatter.7.cloned.1.call-done = f32[2,256,2048]{2,1,0:T(8,128)} async-done(((f32[2,1024,2048]{2,1,0:T(8,128)}), f32[2,256,2048]{2,1,0:T(8,128)}) %reduce-scatter.7.cloned.1.call-update) | async-done | bytes 4194320 | tf_op jit(solution)/shard_map/reduce_scatter | solution.py:215
  1297.3 32.2 fusion.110
  1331.1 33.7 fusion.26
  1367.9 58.8 %all-gather.13.cloned.1.call-done = bf16[2,1024,4096]{1,2,0:T(8,128)(2,1)} async-done(((bf16[2,256,4096]{1,2,0:T(8,128)(2,1)}), bf16[2,1024,4096]{1,2,0:T(8,128)(2,1)}) %all-gather.13.cloned.1.call-update) | async-done | bytes 16777232 | tf_op jit(solution)/shard_map/all_gather | solution.py:68
  1480.2 26.7 all-gather.15.cloned.1.call-done
  1517.3 186.1 %all-gather.17.cloned.1.call-done = bf16[2048,8192]{1,0:T(8,128)(2,1)} async-done(((bf16[64,8192]{1,0:T(8,128)(2,1)}), bf16[2048,8192]{1,0:T(8,128)(2,1)}) %all-gather.17.cloned.1.call-update) | async-done | bytes 33554448 | tf_op jit(solution)/shard_map/all_gather | solution.py:89
  1703.4 28.4 fusion.69
  1731.7 167.5 %all-gather.19.cloned.1.call-done = bf16[8192,2048]{1,0:T(8,128)(2,1)} async-done(((bf16[256,2048]{1,0:T(8,128)(2,1)}), bf16[8192,2048]{1,0:T(8,128)(2,1)}) %all-gather.19.cloned.1.call-update) | async-done | bytes 33554448 | tf_op jit(solution)/shard_map/all_gather | solution.py:90
  1899.2 34.3 multiply_convert_fusion.4
  1959.8 41.0 %all-reduce.12 = (f32[2048]{0:T(1024)S(1)}, f32[2048]{0:T(1024)S(1)}, f32[2048]{0:T(1024)S(1)}, f32[2048]{0:T(1024)S(1)}) all-reduce(f32[2048]{0:T(1024)S(1)} %get-tuple-element.32, f32[2048]{0:T(1024)S(1)} %get-tuple-element.35, f32[2048]{0:T(1024)S(1)} %copy-done.39, ...), channel_id=4, replica_groups=mesh['seq'=4,'dp'=8] {'seq','dp'}, use_global_device_ids=true, to_apply=%region_20.21.clone | all-reduce | flops 8192 | bytes 65536
  2009.9 78.1 %reduce-scatter.13.cloned.1.call-done = f32[64,2048]{1,0:T(8,128)} async-done(((f32[2048,2048]{1,0:T(8,128)}), f32[64,2048]{1,0:T(8,128)}) %reduce-scatter.13.cloned.1.call-update) | async-done | bytes 524304 | tf_op jit(solution)/shard_map/reduce_scatter | solution.py:247
  2088.0 436.1 %reduce-scatter.11.cloned.1.call-done = f32[64,6144]{1,0:T(8,128)} async-done(((f32[2048,6144]{1,0:T(8,128)}), f32[64,6144]{1,0:T(8,128)}) %reduce-scatter.11.cloned.1.call-update) | async-done | bytes 1572880 | tf_op jit(solution)/shard_map/reduce_scatter | solution.py:246
  2524.1 711.2 %reduce-scatter.15.cloned.1.call-done = f32[64,8192]{1,0:T(8,128)} async-done(((f32[2048,8192]{1,0:T(8,128)}), f32[64,8192]{1,0:T(8,128)}) %reduce-scatter.15.cloned.1.call-update) | async-done | bytes 2097168 | tf_op jit(solution)/shard_map/reduce_scatter | solution.py:186
  3235.3 708.7 %reduce-scatter.17.cloned.1.call-done = f32[256,2048]{1,0:T(8,128)} async-done(((f32[8192,2048]{1,0:T(8,128)}), f32[256,2048]{1,0:T(8,128)}) %reduce-scatter.17.cloned.1.call-update) | async-done | bytes 2097168 | tf_op jit(solution)/shard_map/reduce_scatter | solution.py:173
  (227 shorter events, 461.6 us)
Async XLA Ops:
  7.2 53.8 %copy-start = (bf16[2,256,2048]{2,1,0:T(8,128)(2,1)S(1)}, bf16[2,256,2048]{2,1,0:T(8,128)(2,1)}, u32[]{:S(2)}) copy-start(bf16[2,256,2048]{2,1,0:T(8,128)(2,1)} %param.11) | copy-start | bytes 6291460
  7.2 162.7 %all-gather.23.cloned.1.call-start = ((), (), s32[]{:S(2)}) async-start(), calls=%async_computation.12 | async-start | bytes 25952256 | tf_op jit(solution)/shard_map/all_gather | solution.py:53
  7.9 357.9 %all-gather.21.cloned.1.call-start = ((), (), s32[]{:S(2)}) async-start(), calls=%async_computation.11 | async-start | bytes 34603008 | tf_op jit(solution)/shard_map/all_gather | solution.py:90
  8.7 514.5 %all-gather.25.cloned.1.call-start = ((), (), s32[]{:S(2)}) async-start(), calls=%async_computation.13 | async-start | bytes 20971520 | tf_op jit(solution)/shard_map/all_gather | solution.py:68
  198.7 404.7 %all-gather.27.cloned.1.call-start = ((), (), s32[]{:S(2)}) async-start(), calls=%async_computation.14 | async-start | bytes 8650752 | tf_op jit(solution)/shard_map/all_gather | solution.py:54
  199.3 600.4 %all-gather.29.cloned.1.call-start = ((), (), s32[]{:S(2)}) async-start(), calls=%async_computation.15 | async-start | bytes 34603008 | tf_op jit(solution)/shard_map/all_gather | solution.py:89
  199.9 814.8 %all-gather.11.cloned.1.call-start = ((), (), s32[]{:S(2)}) async-start(), calls=%async_computation.6 | async-start | bytes 25952256 | tf_op jit(solution)/shard_map/all_gather | solution.py:53
  200.5 910.1 %reduce-scatter.9.cloned.1.call-start = ((), (), s32[]{:S(2)}) async-start(), calls=%async_computation.17 | async-start | bytes 20971520 | tf_op jit(solution)/shard_map/reduce_scatter | solution.py:221
  201.4 663.6 %copy-start.16 = (f32[2048]{0:T(1024)}, f32[2048]{0:T(1024)S(1)}, u32[]{:S(2)}) copy-start(f32[2048]{0:T(1024)S(1)} %convert_element_type.133) | copy-start | bytes 24580
  201.5 598.2 %copy-start.22 = (f32[2048]{0:T(1024)}, f32[2048]{0:T(1024)S(1)}, u32[]{:S(2)}) copy-start(f32[2048]{0:T(1024)S(1)} %convert_element_type.134) | copy-start | bytes 24580
  201.7 333.2 %copy-start.24 = (pred[256,1024]{1,0:T(8,128)(4,1)}, pred[256,1024]{1,0:T(8,128)(4,1)S(1)}, u32[]{:S(2)}) copy-start(pred[256,1024]{1,0:T(8,128)(4,1)S(1)} %iota_compare_fusion) | copy-start | bytes 786436
  611.4 253.6 %copy-start.18 = (f32[512]{0:T(512)}, f32[512]{0:T(512)S(1)}, u32[]{:S(2)}) copy-start(f32[512]{0:T(512)S(1)} %broadcast_multiply_fusion.1) | copy-start | bytes 6148
  613.9 251.1 %copy-start.20 = (f32[512]{0:T(512)}, f32[512]{0:T(512)S(1)}, u32[]{:S(2)}) copy-start(f32[512]{0:T(512)S(1)} %fusion.92) | copy-start | bytes 6148
  919.5 348.1 %reduce-scatter.7.cloned.1.call-start = ((), (), s32[]{:S(2)}) async-start(), calls=%async_computation.16 | async-start | bytes 20971520 | tf_op jit(solution)/shard_map/reduce_scatter | solution.py:215
  1009.9 416.8 %all-gather.13.cloned.1.call-start = ((), (), s32[]{:S(2)}) async-start(), calls=%async_computation.7 | async-start | bytes 20971520 | tf_op jit(solution)/shard_map/all_gather | solution.py:68
  1044.3 462.7 %all-gather.15.cloned.1.call-start = ((), (), s32[]{:S(2)}) async-start(), calls=%async_computation.8 | async-start | bytes 8650752 | tf_op jit(solution)/shard_map/all_gather | solution.py:54
  1044.9 658.5 %all-gather.17.cloned.1.call-start = ((), (), s32[]{:S(2)}) async-start(), calls=%async_computation.9 | async-start | bytes 34603008 | tf_op jit(solution)/shard_map/all_gather | solution.py:89
  1045.6 853.6 %all-gather.19.cloned.1.call-start = ((), (), s32[]{:S(2)}) async-start(), calls=%async_computation.10 | async-start | bytes 34603008 | tf_op jit(solution)/shard_map/all_gather | solution.py:90
  1046.2 1041.8 %reduce-scatter.13.cloned.1.call-start = ((), (), s32[]{:S(2)}) async-start(), calls=%async_computation.19 | async-start | bytes 17301504 | tf_op jit(solution)/shard_map/reduce_scatter | solution.py:247
  1056.4 1467.6 %reduce-scatter.11.cloned.1.call-start = ((), (), s32[]{:S(2)}) async-start(), calls=%async_computation.18 | async-start | bytes 51904512 | tf_op jit(solution)/shard_map/reduce_scatter | solution.py:246
  1114.5 156.9 %copy-start.8 = (bf16[512,2048]{1,0:T(8,128)(2,1)S(1)}, bf16[512,2048]{1,0:T(8,128)(2,1)}, u32[]{:S(2)}) copy-start(bf16[512,2048]{1,0:T(8,128)(2,1)} %fusion.49) | copy-start | bytes 6291460
  1296.6 1938.7 %reduce-scatter.15.cloned.1.call-start = ((), (), s32[]{:S(2)}) async-start(), calls=%async_computation.20 | async-start | bytes 69206016 | tf_op jit(solution)/shard_map/reduce_scatter | solution.py:186
  1329.5 2614.5 %reduce-scatter.17.cloned.1.call-start = ((), (), s32[]{:S(2)}) async-start(), calls=%async_computation.21 | async-start | bytes 69206016 | tf_op jit(solution)/shard_map/reduce_scatter | solution.py:173
  1367.9 70.6 %copy-start.25 = (pred[256,1024]{1,0:T(8,128)(4,1)S(1)}, pred[256,1024]{1,0:T(8,128)(4,1)}, u32[]{:S(2)}) copy-start(pred[256,1024]{1,0:T(8,128)(4,1)} %copy-done.24) | copy-start | bytes 786436
  (37 other events, 363.4 us)
Sparse Core Ops, SparseCore 0:
  11.0 158.7 all-gather.22
  172.8 192.9 all-gather.20
  367.7 155.4 all-gather.24
  526.0 77.3 all-gather.26
  606.3 193.3 all-gather.28
  802.5 152.9 all-gather.10
  958.6 152.0 reduce-scatter.8
  1113.7 153.8 reduce-scatter.6
  1269.4 157.2 all-gather.12
  1429.5 77.3 all-gather.14
  1510.0 193.3 all-gather.16
  1706.2 192.9 all-gather.18
  1902.1 185.8 reduce-scatter.12
  2094.8 429.1 reduce-scatter.10
  2526.8 708.3 reduce-scatter.14
  3238.1 705.8 reduce-scatter.16
where the time goes:
time: 3960 us; the launch traced here: 3950 us
  waiting for transfers between devices  3170 us (80%)
  matrix products  483 us (12%)
  local copies, waits for them, and re-layouts  132 us (3%)
  blocking collectives  84.5 us (2%)
  other arithmetic  64.8 us (2%)
    reduce_scatter x1, waiting for transfers between devices, per_device(): lax.psum_scatter(up_term, ('seq', 'dp'), scatter_dimension=0, tiled=True)  711 us
    reduce_scatter x1, waiting for transfers between devices, per_device(): lax.psum_scatter(down_term, ('seq', 'dp'), scatter_dimension=0, tiled=True)  709 us
    reduce_scatter x1, waiting for transfers between devices, per_device(): lax.psum_scatter(in_term, ('seq', 'dp'), scatter_dimension=0, tiled=True)  436 us
    all_gather x2, waiting for transfers between devices, forward(): lax.all_gather(upward, ('seq', 'dp'), axis=0, tiled=True)  372 us
    all_gather x2, waiting for transfers between devices, forward(): lax.all_gather(downward, ('seq', 'dp'), axis=0, tiled=True)  320 us
    all_gather x2, waiting for transfers between devices, forward(): lax.all_gather(projected[:, model_width:].reshape(slot_count, block_rows,...  190 us
    reduce_scatter x1, waiting for transfers between devices, per_device(): lax.psum_scatter(key_term.reshape(slot_count, length, model_width), 'seq'...  153 us
    all_gather x2, waiting for transfers between devices, forward(): lax.all_gather(inward, ('seq', 'dp'), axis=0, tiled=True)  105 us
  transfers between devices with their start and end apart: 16, of which 15 were waited for; matrix products, arithmetic and copies ran while one was open for 17% of the time, Pallas kernels for 0%

commit v1 on v0

v1 whole, which is shorter than its diff:
```python
import math

import jax
import jax.numpy as jnp
from jax import lax
from jax.sharding import PartitionSpec as P

HEADS = 16
EPSILON = 1e-05
MASKED = -1e30
BF = jnp.bfloat16
F32 = jnp.float32


def norm_parts(values):
    average = jnp.mean(values, axis=-1, keepdims=True)
    centered = values - average
    root = lax.rsqrt(jnp.mean(centered * centered, axis=-1, keepdims=True) + EPSILON)
    return centered * root, root


def norm_back(flow, unit, root, gain):
    scaled = flow * gain
    first = jnp.mean(scaled, axis=-1, keepdims=True)
    second = jnp.mean(scaled * unit, axis=-1, keepdims=True)
    return root * (scaled - first - unit * second), jnp.sum(flow * unit, axis=0), jnp.sum(flow, axis=0)


def smooth_gate(values):
    return jax.nn.gelu(values, approximate=True)


def rows_product(left, right):
    return lax.dot_general(left, right, (((0,), (0,)), ((), ())), preferred_element_type=F32)


def cols_product(left, right):
    return lax.dot_general(left, right, (((1,), (1,)), ((), ())), preferred_element_type=F32)


def product(left, right):
    return jnp.dot(left, right, preferred_element_type=F32)


def swap_over_seq(pieces, count):
    me = lax.axis_index("seq")
    result = jnp.zeros_like(pieces)
    own = lax.dynamic_index_in_dim(pieces, me, 0, keepdims=True)
    result = lax.dynamic_update_index_in_dim(result, own, me, 0)
    for step in range(1, count):
        if count & (count - 1) == 0:
            target, source = me ^ step, me ^ step
            pairs = [(i, i ^ step) for i in range(count)]
        else:
            target, source = (me + step) % count, (me - step) % count
            pairs = [(i, (i + step) % count) for i in range(count)]
        sent = lax.dynamic_index_in_dim(pieces, target, 0, keepdims=True)
        got = lax.ppermute(sent, "seq", pairs)
        result = lax.dynamic_update_index_in_dim(result, got, source, 0)
    return result


def probabilities(query, key, scaling):
    logits = jnp.einsum("sqhd,skhd->shqk", query, key, preferred_element_type=F32) * scaling
    length = logits.shape[-1]
    causal = jnp.arange(length)[None, :] <= jnp.arange(length)[:, None]
    return jax.nn.softmax(jnp.where(causal[None, None], logits, MASKED), axis=-1)


def make_layer(seq, dp):
    def scatter_seq(values, slots):
        shaped = values.astype(BF).reshape(slots, -1, values.shape[-1])
        got = lax.psum_scatter(shaped, "seq", scatter_dimension=1, tiled=True)
        return got.reshape(-1, values.shape[-1]).astype(F32)

    def gather_seq(values, slots):
        shaped = values.reshape(slots, -1, values.shape[-1])
        return lax.all_gather(shaped, "seq", axis=1, tiled=True).reshape(-1, values.shape[-1])

    def gather_columns(shard, thirds):
        rows, columns = shard.shape
        width = columns // (thirds * seq)
        pieces = shard.reshape(rows, thirds, seq, width).transpose(2, 0, 1, 3).reshape(seq, rows, thirds * width)
        swapped = swap_over_seq(pieces, seq)
        return lax.all_gather(swapped, "dp", axis=1, tiled=True).reshape(-1, thirds * width)

    def scatter_columns(term, thirds):
        total, width = term.shape
        rows = total // (seq * dp)
        summed = lax.psum_scatter(
            term.astype(BF).reshape(seq, dp * rows, width), "dp", scatter_dimension=1, tiled=True
        )
        swapped = swap_over_seq(summed, seq)
        shaped = swapped.reshape(seq, rows, thirds, width // thirds).transpose(1, 2, 0, 3)
        return shaped.reshape(rows, seq * width).astype(F32)

    def scatter_rows(term):
        return lax.psum_scatter(term.astype(BF), "dp", scatter_dimension=0, tiled=True).astype(F32)

    def layer(
        inputs, counts, cotangent, stretch, offset, inward, outward, dilation, translation, upward, downward
    ):
        slots, block, model = inputs.shape
        head_size = model // HEADS
        heads = HEADS // seq
        scaling = 1.0 / math.sqrt(head_size)
        local_rows = slots * block
        length = block * seq
        total = slots * length
        live = jnp.repeat((jnp.arange(slots) < counts[0]).astype(F32), block)[:, None]
        residual = inputs.reshape(local_rows, model)
        everything = gather_seq(residual, slots)
        small = jnp.stack([stretch, offset, dilation, translation]).astype(F32)
        small = lax.all_gather(small, ("seq", "dp"), axis=1, tiled=True)
        gain_one, shift_one, gain_two, shift_two = small[0], small[1], small[2], small[3]
        matrix_in = gather_columns(inward, 3)
        matrix_out = lax.all_gather(outward, "dp", axis=0, tiled=True)
        matrix_up = gather_columns(upward, 1)
        matrix_down = lax.all_gather(downward, "dp", axis=0, tiled=True)
        upstream = (cotangent.astype(F32).reshape(local_rows, model) * live).astype(BF)
        upstream_all = gather_seq(upstream, slots)

        unit_all, _ = norm_parts(everything.astype(F32))
        normed = (unit_all * gain_one + shift_one).astype(BF)
        projected = product(normed, matrix_in).astype(BF)
        query, key, value = (
            projected[:, i * heads * head_size : (i + 1) * heads * head_size].reshape(slots, length, heads, head_size)
            for i in range(3)
        )
        probs = probabilities(query, key, scaling)
        weights = probs.astype(BF)
        mixture = jnp.einsum("shqk,skhd->sqhd", weights, value, preferred_element_type=F32)
        attended = mixture.reshape(total, heads * head_size).astype(BF)
        middle = residual.astype(F32) + scatter_seq(product(attended, matrix_out), slots)
        unit_two, root_two = norm_parts(middle)
        normed_two = gather_seq((unit_two * gain_two + shift_two).astype(BF), slots)
        expanded = product(normed_two, matrix_up)
        hidden = smooth_gate(expanded).astype(BF)
        result = middle + scatter_seq(product(hidden, matrix_down), slots)
        outputs = (result * live).astype(BF).reshape(slots, block, model)

        downward_delta = scatter_rows(rows_product(hidden, upstream_all))
        hidden_back = cols_product(upstream_all, matrix_down)
        expanded_back = jax.vjp(smooth_gate, expanded)[1](hidden_back)[0].astype(BF)
        upward_delta = scatter_columns(rows_product(normed_two, expanded_back), 1)
        two_back = scatter_seq(cols_product(expanded_back, matrix_up), slots)
        middle_flow, dilation_term, translation_term = norm_back(two_back, unit_two, root_two, gain_two)
        middle_back = upstream.astype(F32) + middle_flow
        middle_low = gather_seq(middle_back.astype(BF), slots)
        outward_delta = scatter_rows(rows_product(attended, middle_low))
        heads_back = cols_product(middle_low, matrix_out).astype(BF).reshape(slots, length, heads, head_size)

        prob_back = jnp.einsum("sqhd,skhd->shqk", heads_back, value, preferred_element_type=F32)
        value_back = jnp.einsum("shqk,sqhd->skhd", weights, heads_back, preferred_element_type=F32)
        logit_back = (probs * (prob_back - jnp.sum(probs * prob_back, axis=-1, keepdims=True))).astype(BF)
        query_back = jnp.einsum("shqk,skhd->sqhd", logit_back, key, preferred_element_type=F32) * scaling
        key_back = jnp.einsum("shqk,sqhd->skhd", logit_back, query, preferred_element_type=F32) * scaling
        projected_back = jnp.concatenate(
            [part.astype(BF).reshape(total, heads * head_size) for part in (query_back, key_back, value_back)], axis=1
        )
        inward_delta = scatter_columns(rows_product(normed, projected_back), 3)
        one_back = scatter_seq(cols_product(projected_back, matrix_in), slots)
        unit_one, root_one = norm_parts(residual.astype(F32))
        input_flow, stretch_term, offset_term = norm_back(one_back, unit_one, root_one, gain_one)
        terms = jnp.stack([stretch_term, offset_term, dilation_term, translation_term])
        deltas = lax.psum_scatter(terms, ("seq", "dp"), scatter_dimension=1, tiled=True)
        input_delta = (middle_back + input_flow).reshape(slots, block, model)
        return (
            outputs,
            input_delta,
            deltas[0],
            deltas[1],
            inward_delta,
            outward_delta,
            deltas[2],
            deltas[3],
            upward_delta,
            downward_delta,
        )

    return layer


def solution(mesh):
    tokens, vector, matrix = P("dp", "seq", None), P(("seq", "dp")), P(("seq", "dp"), None)
    return jax.shard_map(
        make_layer(mesh.shape["seq"], mesh.shape["dp"]),
        mesh=mesh,
        in_specs=(tokens, P("dp"), tokens, vector, vector, matrix, matrix, vector, vector, matrix, matrix),
        out_specs=(tokens, tokens, vector, vector, matrix, matrix, vector, vector, matrix, matrix),
        check_vma=False,
    )
```

time: 3960 us -> 1560 us (0.39)
  waiting for transfers between devices: 3170 us -> 955 us
  matrix products: 483 us -> 340 us
  blocking collectives: 84.5 us -> 41.3 us
    reduce_scatter x6 -> x8, waiting for transfers between devices: 2120 us -> 356 us  [the longest x4 299 us: scatter_seq(): got = lax.psum_scatter(shaped, 'seq', scatter_dimension=1, tiled=True)]
    all_gather x10 -> x8, waiting for transfers between devices: 1040 us -> 426 us  [the longest x4 231 us: gather_seq(): lax.all_gather(shaped, 'seq', axis=1, tiled=True)]
    unnamed x16 -> x18, waiting for transfers between devices: 4.82 us -> 131 us
    dot_general x21 -> x17, matrix products: 442 us -> 320 us  [the longest x4 88.7 us: product(): return jnp.dot(left, right, preferred_element_type=F32)]
    unnamed x2 -> x0, blocking collectives: 84.5 us -> none
    ppermute x0 -> x12, waiting for transfers between devices: none -> 42.5 us  [swap_over_seq(): got = lax.ppermute(sent, 'seq', pairs)]
    all_gather x0 -> x1, blocking collectives: none -> 41.3 us  [layer(): small = lax.all_gather(small, ('seq', 'dp'), axis=1, tiled=True)]
  transfers between devices with their start and end apart: 16 -> 29, of which waited for: 15 -> 20; matrix products, arithmetic and copies ran while one was open for 17% -> 28% of each run, Pallas kernels for 0% -> 0%
where the time goes in v1:
time: 1560 us; the launch traced here: 1550 us
  waiting for transfers between devices  955 us (61%)
  matrix products  340 us (22%)
  local copies, waits for them, and re-layouts  97.7 us (6%)
  other arithmetic  85 us (5%)
  blocking collectives  41.3 us (3%)
  starting transfers between devices  17.1 us (1%)
  between operations  15.9 us (1%)
    reduce_scatter x4, waiting for transfers between devices, scatter_seq(): got = lax.psum_scatter(shaped, 'seq', scatter_dimension=1, tiled=True)  299 us
    all_gather x4, waiting for transfers between devices, gather_seq(): lax.all_gather(shaped, 'seq', axis=1, tiled=True)  231 us
    unnamed x18, waiting for transfers between devices  131 us
    all_gather x2, waiting for transfers between devices, gather_columns(): lax.all_gather(swapped, 'dp', axis=1, tiled=True)  111 us
    dot_general x4, matrix products, product(): return jnp.dot(left, right, preferred_element_type=F32)  88.7 us
    all_gather x1, waiting for transfers between devices, layer(): matrix_down = lax.all_gather(downward, 'dp', axis=0, tiled=True)  83.6 us
    dot_general x4, matrix products, rows_product(): lax.dot_general(left, right, (((0,), (0,)), ((), ())), preferred_element_...  78.8 us
    dot_general x4, matrix products, cols_product(): lax.dot_general(left, right, (((1,), (1,)), ((), ())), preferred_element_...  75 us
  transfers between devices with their start and end apart: 29, of which 20 were waited for; matrix products, arithmetic and copies ran while one was open for 28% of the time, Pallas kernels for 0%

profile of v1, /device:TPU:0, one launch (start us, length us, event | category | flops | bytes accessed | tf_op | source)
XLA Modules:
  0.0 1552.7 jit_solution(13752615539026847849)
XLA Ops:
  31.5 41.3 %all-gather = f32[32,64,4]{1,2,0:T(4,128)S(1)} all-gather(f32[1,64,4]{1,2,0:T(4,128)S(1)} %convert_bitcast_fusion.2), channel_id=1, replica_groups=mesh['seq'=4,'dp'=8] {'seq','dp'}, dimensions={0}, use_global_device_ids=true | all-gather | bytes 33792 | tf_op jit(solution)/shard_map/all_gather | solution.py:114
  73.0 29.8 %all-gather.10.cloned.1.call-done = bf16[2,1024,2048]{2,1,0:T(8,128)(2,1)} async-done(((bf16[2,256,2048]{2,1,0:T(8,128)(2,1)}), bf16[2,1024,2048]{2,1,0:T(8,128)(2,1)}) %all-gather.10.cloned.1.call-update) | async-done | bytes 8388624 | tf_op jit(solution)/shard_map/all_gather | solution.py:78
  117.0 52.7 %all-gather.12.cloned.1.call-done = bf16[4,512,1536]{2,1,0:T(8,128)(2,1)} async-done(((bf16[4,64,1536]{2,1,0:T(8,128)(2,1)}), bf16[4,512,1536]{2,1,0:T(8,128)(2,1)}) %all-gather.12.cloned.1.call-update) | async-done | bytes 6291472 | tf_op jit(solution)/shard_map/all_gather | solution.py:85
  203.2 20.2 %fusion.64 = (f32[2,4,1024]{2,1,0:T(4,128)S(1)}, f32[2,4,1024,1024]{2,3,1,0:T(8,128)}) fusion(pred[1024,1024]{0,1:T(8,128)(4,1)S(1)} %iota_compare_fusion, bf16[2,1024,4,128]{1,3,2,0:T(8,128)(2,1)} %copy.93, bf16[2,1024,4,128]{1,3,2,0:T(8,128)(2,1)S(1)} %copy.90), kind=kOutput, calls=%fused_computation.148 | convolution fusion | flops 2181039104 | bytes 38830080 | tf_op jit(solution)/shard_map/sub | solution.py:67
  288.4 61.3 %reduce-scatter.12.cloned.1.call-done = bf16[2,256,2048]{2,1,0:T(8,128)(2,1)} async-done(((bf16[2,1024,2048]{2,1,0:T(8,128)(2,1)}), bf16[2,256,2048]{2,1,0:T(8,128)(2,1)}) %reduce-scatter.12.cloned.1.call-update) | async-done | bytes 2097168 | tf_op jit(solution)/shard_map/reduce_scatter | solution.py:73
  355.5 84.3 %all-gather.22.cloned.1.call-done = bf16[2,1024,2048]{2,1,0:T(8,128)(2,1)} async-done(((bf16[2,256,2048]{2,1,0:T(8,128)(2,1)}), bf16[2,1024,2048]{2,1,0:T(8,128)(2,1)}) %all-gather.22.cloned.1.call-update) | async-done | bytes 8388624 | tf_op jit(solution)/shard_map/all_gather | solution.py:78
  439.7 83.6 %all-gather.20.cloned.1.call-done = bf16[2048,2048]{1,0:T(8,128)(2,1)} async-done(((bf16[256,2048]{1,0:T(8,128)(2,1)}), bf16[2048,2048]{1,0:T(8,128)(2,1)}) %all-gather.20.cloned.1.call-update) | async-done | bytes 8388624 | tf_op jit(solution)/shard_map/all_gather | solution.py:119
  523.4 24.5 %fusion.65 = f32[2048,2048]{1,0:T(8,128)} fusion(bf16[2048,2048]{1,0:T(8,128)(2,1)} %bitcast.185, bf16[2048,2048]{1,0:T(8,128)(2,1)} %all-gather.20.cloned.1.call-done), kind=kOutput, calls=%fused_computation.149 | convolution fusion | flops 17179869184 | bytes 33554432 | tf_op jit(solution)/shard_map/dot_general | solution.py:38
  547.9 58.4 %all-gather.18.cloned.1.call-done = bf16[4,512,2048]{2,1,0:T(8,128)(2,1)} async-done(((bf16[4,64,2048]{2,1,0:T(8,128)(2,1)}), bf16[4,512,2048]{2,1,0:T(8,128)(2,1)}) %all-gather.18.cloned.1.call-update) | async-done | bytes 8388624 | tf_op jit(solution)/shard_map/all_gather | solution.py:85
  606.3 88.7 %all-gather.16.cloned.1.call-done = bf16[2,1024,2048]{2,1,0:T(8,128)(2,1)} async-done(((bf16[2,256,2048]{2,1,0:T(8,128)(2,1)}), bf16[2,1024,2048]{2,1,0:T(8,128)(2,1)}) %all-gather.16.cloned.1.call-update) | async-done | bytes 8388624 | tf_op jit(solution)/shard_map/all_gather | solution.py:78
  695.0 36.4 %fusion.8 = (bf16[2048,2048]{1,0:T(8,128)(2,1)}, f32[2048,2048]{1,0:T(8,128)}) fusion(f32[2048,2048]{1,0:T(8,128)} %fusion.65, bf16[2048,2048]{1,0:T(8,128)(2,1)} %bitcast.189, bf16[2048,2048]{1,0:T(8,128)(2,1)} %bitcast.191), kind=kOutput, calls=%fused_computation.14 | convolution fusion | flops 17263755264 | bytes 58720256 | tf_op jit(solution)/shard_map/dot_general | solution.py:42
  731.4 21.9 %convolution_convert_fusion.3 = bf16[2048,2048]{1,0:T(8,128)(2,1)} fusion(bf16[2048,2048]{1,0:T(8,128)(2,1)} %get-tuple-element.56, bf16[2048,2048]{1,0:T(8,128)(2,1)S(1)} %bitcast.192), kind=kOutput, calls=%fused_computation.35 | convolution fusion | flops 17184063488 | bytes 25165824 | tf_op jit(solution)/shard_map/dot_general | solution.py:38
  753.4 86.5 %reduce-scatter.16.cloned.1.call-done = bf16[2,256,2048]{2,1,0:T(8,128)(2,1)} async-done(((bf16[2,1024,2048]{2,1,0:T(8,128)(2,1)}), bf16[2,256,2048]{2,1,0:T(8,128)(2,1)}) %reduce-scatter.16.cloned.1.call-update) | async-done | bytes 2097168 | tf_op jit(solution)/shard_map/reduce_scatter | solution.py:73
  849.3 23.7 %convolution_convert_fusion.1 = bf16[2048,2048]{1,0:T(8,128)(2,1)} fusion(bf16[2048,2048]{1,0:T(8,128)(2,1)} %bitcast.190, bf16[2048,2048]{1,0:T(8,128)(2,1)} %get-tuple-element.56), kind=kOutput, calls=%fused_computation.33 | convolution fusion | flops 17184063488 | bytes 25165824 | tf_op jit(solution)/shard_map/dot_general | solution.py:34
  882.6 26.1 %convolution_convert_fusion = bf16[2048,2048]{1,0:T(8,128)(2,1)} fusion(bf16[2048,2048]{1,0:T(8,128)(2,1)} %bitcast.186, f32[2048,2048]{1,0:T(8,128)} %get-tuple-element.57), kind=kOutput, calls=%fused_computation.32 | convolution fusion | flops 17221812224 | bytes 33554432 | tf_op jit(solution)/shard_map/dot_general | solution.py:34
  908.7 28.3 %all-gather.24.cloned.1.call-done = bf16[2,1024,2048]{2,1,0:T(8,128)(2,1)} async-done(((bf16[2,256,2048]{2,1,0:T(8,128)(2,1)}), bf16[2,1024,2048]{2,1,0:T(8,128)(2,1)}) %all-gather.24.cloned.1.call-update) | async-done | bytes 8388624 | tf_op jit(solution)/shard_map/all_gather | solution.py:78
  971.5 25.5 %multiply_reduce_fusion = (f32[2,4,1024]{2,1,0:T(4,128)S(1)}, f32[2,4,1024,1024]{2,3,1,0:T(8,128)}) fusion(f32[2,4,1024,1024]{2,3,1,0:T(8,128)} %get-tuple-element.55, f32[2,4,1024]{2,1,0:T(4,128)S(1)} %copy-done.41, bf16[2,1024,4,128]{1,3,2,0:T(8,128)(2,1)} %copy.96, bf16[2,1024,4,128]{3,2,1,0:T(4,128)(2,1)S(1)} %copy-done.20), kind=kOutput, calls=%fused_computation.2 | convolution fusion | flops 2172641280 | bytes 71368704 | tf_op jit(solution)/shard_map/sqhd,skhd->shqk/dot_general | solution.py:153
  997.1 28.6 %multiply_convert_fusion = bf16[2,4,1024,1024]{2,3,1,0:T(8,128)(2,1)} fusion(f32[2,4,1024,1024]{2,3,1,0:T(8,128)} %get-tuple-element.59, f32[2,4,1024]{2,1,0:T(4,128)S(1)} %get-tuple-element.58, f32[2,4,1024,1024]{2,3,1,0:T(8,128)} %get-tuple-element.55, f32[2,4,1024]{2,1,0:T(4,128)S(1)} %copy-done.41), kind=kLoop, calls=%fused_computation.1 | loop fusion | flops 33554432 | bytes 83951616 | tf_op jit(solution)/shard_map/convert_element_type | solution.py:155
  1060.1 19.7 %convolution_convert_fusion.7 = bf16[2048,1536]{1,0:T(8,128)(2,1)} fusion(bf16[2048,2048]{1,0:T(8,128)(2,1)} %fusion.12, bf16[2048,1536]{1,0:T(8,128)(2,1)S(1)} %bitcast_dynamic-update-slice_fusion), kind=kOutput, calls=%fused_computation.39 | convolution fusion | flops 12888047616 | bytes 20971520 | tf_op jit(solution)/shard_map/dot_general | solution.py:34
  1110.2 26.0 %convolution_convert_fusion.4 = bf16[2048,2048]{1,0:T(8,128)(2,1)} fusion(bf16[2048,2048]{1,0:T(8,128)(2,1)} %all-gather.20.cloned.1.call-done, f32[2048,2048]{1,0:T(8,128)} %get-tuple-element.57), kind=kOutput, calls=%fused_computation.36 | convolution fusion | flops 17221812224 | bytes 33554432 | tf_op jit(solution)/shard_map/dot_general | solution.py:42
  1148.4 41.2 %reduce-scatter.20.cloned.1.call-done = bf16[4,64,1536]{2,1,0:T(8,128)(2,1)} async-done(((bf16[4,512,1536]{2,1,0:T(8,128)(2,1)}), bf16[4,64,1536]{2,1,0:T(8,128)(2,1)}) %reduce-scatter.20.cloned.1.call-update) | async-done | bytes 786448 | tf_op jit(solution)/shard_map/reduce_scatter | solution.py:90
  1249.0 66.6 %reduce-scatter.18.cloned.1.call-done = bf16[2,256,2048]{2,1,0:T(8,128)(2,1)} async-done(((bf16[2,1024,2048]{2,1,0:T(8,128)(2,1)}), bf16[2,256,2048]{2,1,0:T(8,128)(2,1)}) %reduce-scatter.18.cloned.1.call-update) | async-done | bytes 2097168 | tf_op jit(solution)/shard_map/reduce_scatter | solution.py:73
  1320.5 84.8 %reduce-scatter.14.cloned.1.call-done = bf16[2,256,2048]{2,1,0:T(8,128)(2,1)} async-done(((bf16[2,1024,2048]{2,1,0:T(8,128)(2,1)}), bf16[2,256,2048]{2,1,0:T(8,128)(2,1)}) %reduce-scatter.14.cloned.1.call-update) | async-done | bytes 2097168 | tf_op jit(solution)/shard_map/reduce_scatter | solution.py:73
  1413.8 128.8 %reduce-scatter.28.cloned.1.call-done = f32[64,4]{1,0:T(8,128)} async-done(((f32[2048,4]{1,0:T(8,128)}), f32[64,4]{1,0:T(8,128)}) %reduce-scatter.28.cloned.1.call-update) | async-done | bytes 1040
  (285 shorter events, 347.8 us)
Async XLA Ops:
  7.2 95.6 %all-gather.10.cloned.1.call-start = ((), (), s32[]{:S(2)}) async-start(), calls=%async_computation.9 | async-start | bytes 10485760 | tf_op jit(solution)/shard_map/all_gather | solution.py:78
  7.9 161.8 %all-gather.12.cloned.1.call-start = ((), (), s32[]{:S(2)}) async-start(), calls=%async_computation.10 | async-start | bytes 7077888 | tf_op jit(solution)/shard_map/all_gather | solution.py:85
  30.4 213.8 %all-gather.14.cloned.1.call-start = ((), (), s32[]{:S(2)}) async-start(), calls=%async_computation.11 | async-start | bytes 2359296 | tf_op jit(solution)/shard_map/all_gather | solution.py:117
  31.1 318.6 %reduce-scatter.12.cloned.1.call-start = ((), (), s32[]{:S(2)}) async-start(), calls=%async_computation.12 | async-start | bytes 10485760 | tf_op jit(solution)/shard_map/reduce_scatter | solution.py:73
  253.2 186.5 %all-gather.22.cloned.1.call-start = ((), (), s32[]{:S(2)}) async-start(), calls=%async_computation.17 | async-start | bytes 10485760 | tf_op jit(solution)/shard_map/all_gather | solution.py:78
  256.8 266.6 %all-gather.20.cloned.1.call-start = ((), (), s32[]{:S(2)}) async-start(), calls=%async_computation.15 | async-start | bytes 9437184 | tf_op jit(solution)/shard_map/all_gather | solution.py:119
  257.4 348.9 %all-gather.18.cloned.1.call-start = ((), (), s32[]{:S(2)}) async-start(), calls=%async_computation.14 | async-start | bytes 9437184 | tf_op jit(solution)/shard_map/all_gather | solution.py:85
  260.6 14.8 collective-permute-start.3
  262.3 15.4 collective-permute-start.4
  264.0 23.4 %collective-permute-start.5 = (bf16[1,64,2048]{2,1,0:T(8,128)(2,1)S(1)}, bf16[1,64,2048]{2,1,0:T(8,128)(2,1)S(1)}, u32[]{:S(2)}, u32[]{:S(2)}) collective-permute-start(bf16[1,64,2048]{2,1,0:T(8,128)(2,1)S(1)} %bitcast.158), channel_id=1, source_target_pairs={{0,24},{8,16},{16,8},{24,0},{1,25},{9,17},{17,9},{25,1},{2,26},{10... | collective-permute-start | bytes 786440 | tf_op jit(solution)/shard_map/ppermute | solution.py:58
  288.3 406.7 %all-gather.16.cloned.1.call-start = ((), (), s32[]{:S(2)}) async-start(), calls=%async_computation.13 | async-start | bytes 10485760 | tf_op jit(solution)/shard_map/all_gather | solution.py:78
  355.4 484.5 %reduce-scatter.16.cloned.1.call-start = ((), (), s32[]{:S(2)}) async-start(), calls=%async_computation.18 | async-start | bytes 10485760 | tf_op jit(solution)/shard_map/reduce_scatter | solution.py:73
  753.4 183.7 %all-gather.24.cloned.1.call-start = ((), (), s32[]{:S(2)}) async-start(), calls=%async_computation.19 | async-start | bytes 10485760 | tf_op jit(solution)/shard_map/all_gather | solution.py:78
  849.2 287.3 %reduce-scatter.24.cloned.1.call-start = ((), (), s32[]{:S(2)}) async-start(), calls=%async_computation.23 | async-start | bytes 9437184 | tf_op jit(solution)/shard_map/reduce_scatter | solution.py:90
  873.1 272.6 %reduce-scatter.26.cloned.1.call-start = ((), (), s32[]{:S(2)}) async-start(), calls=%async_computation.24 | async-start | bytes 9437184 | tf_op jit(solution)/shard_map/reduce_scatter | solution.py:98
  908.7 281.0 %reduce-scatter.20.cloned.1.call-start = ((), (), s32[]{:S(2)}) async-start(), calls=%async_computation.21 | async-start | bytes 7077888 | tf_op jit(solution)/shard_map/reduce_scatter | solution.py:90
  1079.8 146.7 %reduce-scatter.22.cloned.1.call-start = ((), (), s32[]{:S(2)}) async-start(), calls=%async_computation.22 | async-start | bytes 2359296 | tf_op jit(solution)/shard_map/reduce_scatter | solution.py:98
  1090.7 224.8 %reduce-scatter.18.cloned.1.call-start = ((), (), s32[]{:S(2)}) async-start(), calls=%async_computation.20 | async-start | bytes 10485760 | tf_op jit(solution)/shard_map/reduce_scatter | solution.py:73
  1110.2 295.1 %reduce-scatter.14.cloned.1.call-start = ((), (), s32[]{:S(2)}) async-start(), calls=%async_computation.16 | async-start | bytes 10485760 | tf_op jit(solution)/shard_map/reduce_scatter | solution.py:73
  1136.3 406.3 %reduce-scatter.28.cloned.1.call-start = ((), (), s32[]{:S(2)}) async-start(), calls=%async_computation.25 | async-start | bytes 1081344
  1137.9 55.3 %collective-permute-start.11 = (bf16[1,64,2048]{2,1,0:T(8,128)(2,1)S(1)}, bf16[1,64,2048]{2,1,0:T(8,128)(2,1)}, u32[]{:S(2)}, u32[]{:S(2)}) collective-permute-start(bf16[1,64,2048]{2,1,0:T(8,128)(2,1)S(1)} %get-tuple-element.26), channel_id=1, source_target_pairs={{0,24},{8,16},{16,8},{24,0},{1,25},{9,17},{17,9},{25,1},{2,26},{10... | collective-permute-start | bytes 786440 | tf_op jit(solution)/shard_map/ppermute | solution.py:58
  1139.9 54.7 %collective-permute-start.10 = (bf16[1,64,2048]{2,1,0:T(8,128)(2,1)S(1)}, bf16[1,64,2048]{2,1,0:T(8,128)(2,1)}, u32[]{:S(2)}, u32[]{:S(2)}) collective-permute-start(bf16[1,64,2048]{2,1,0:T(8,128)(2,1)S(1)} %get-tuple-element.27), channel_id=1, source_target_pairs={{0,16},{8,24},{16,0},{24,8},{1,17},{9,25},{17,1},{25,9},{2,18},{10... | collective-permute-start | bytes 786440 | tf_op jit(solution)/shard_map/ppermute | solution.py:58
  1140.9 55.0 %collective-permute-start.9 = (bf16[1,64,2048]{2,1,0:T(8,128)(2,1)S(1)}, bf16[1,64,2048]{2,1,0:T(8,128)(2,1)S(1)}, u32[]{:S(2)}, u32[]{:S(2)}) collective-permute-start(bf16[1,64,2048]{2,1,0:T(8,128)(2,1)S(1)} %get-tuple-element.28), channel_id=1, source_target_pairs={{0,8},{8,0},{16,24},{24,16},{1,9},{9,1},{17,25},{25,17},{2,10},{10... | collective-permute-start | bytes 786440 | tf_op jit(solution)/shard_map/ppermute | solution.py:58
  1191.7 39.5 %collective-permute-start.6 = (bf16[1,64,1536]{2,1,0:T(8,128)(2,1)}, bf16[1,64,1536]{2,1,0:T(8,128)(2,1)}, u32[]{:S(2)}, u32[]{:S(2)}) collective-permute-start(bf16[1,64,1536]{2,1,0:T(8,128)(2,1)} %get-tuple-element.36), channel_id=1, source_target_pairs={{0,8},{8,0},{16,24},{24,16},{1,9},{9,1},{17,25},{25,17},{2,10},{10... | collective-permute-start | bytes 589832 | tf_op jit(solution)/shard_map/ppermute | solution.py:58
  (67 other events, 2681.5 us)
Sparse Core Ops, SparseCore 0:
  9.9 92.8 all-gather.9
  105.0 64.6 all-gather.11
  171.3 27.7 all-gather.13
  253.3 96.2 reduce-scatter.11
  352.1 87.5 all-gather.21
  441.3 82.0 all-gather.19
  525.6 80.5 all-gather.17
  608.8 86.1 all-gather.15
  753.5 86.4 reduce-scatter.15
  849.4 87.6 all-gather.23
  939.3 89.5 reduce-scatter.23
  1031.1 87.9 reduce-scatter.25
  1121.4 68.1 reduce-scatter.19
  1192.3 34.0 reduce-scatter.21
  1229.4 86.1 reduce-scatter.17
  1318.8 86.4 reduce-scatter.13
  1407.3 135.1 reduce-scatter.27

commit v2 on v1

v2 whole, which is shorter than its diff:
```python
import functools
import math

import jax
import jax.numpy as jnp
from jax import lax
from jax.experimental import pallas as pl
from jax.experimental.pallas import tpu as pltpu
from jax.sharding import PartitionSpec as P

HEADS = 16
EPSILON = 1e-05
MASKED = -1e30
BF = jnp.bfloat16
F32 = jnp.float32
MESH = pl.DeviceIdType.MESH


def norm_parts(values):
    average = jnp.mean(values, axis=-1, keepdims=True)
    centered = values - average
    root = lax.rsqrt(jnp.mean(centered * centered, axis=-1, keepdims=True) + EPSILON)
    return centered * root, root


def norm_back(flow, unit, root, gain):
    scaled = flow * gain
    first = jnp.mean(scaled, axis=-1, keepdims=True)
    second = jnp.mean(scaled * unit, axis=-1, keepdims=True)
    return root * (scaled - first - unit * second), jnp.sum(flow * unit, axis=0), jnp.sum(flow, axis=0)


def smooth_gate(values):
    return jax.nn.gelu(values, approximate=True)


def rows_product(left, right):
    return lax.dot_general(left, right, (((0,), (0,)), ((), ())), preferred_element_type=F32)


def cols_product(left, right):
    return lax.dot_general(left, right, (((1,), (1,)), ((), ())), preferred_element_type=F32)


def product(left, right):
    return jnp.dot(left, right, preferred_element_type=F32)


def after(values, event):
    return lax.optimization_barrier((values, event))[0]


def greet(seq, dp, me_seq, me_dp):
    barrier = pltpu.get_barrier_semaphore()
    for step in range(1, seq):
        pl.semaphore_signal(barrier, inc=1, device_id=(lax.rem(me_seq + step, seq), me_dp), device_id_type=MESH)
    for step in range(1, dp):
        pl.semaphore_signal(barrier, inc=1, device_id=(me_seq, lax.rem(me_dp + step, dp)), device_id_type=MESH)
    pl.semaphore_wait(barrier, seq + dp - 2)


def opening_kernel(seq, dp, pieces, small, swapped, params, own, send, recv, send_small, recv_small, send_row, recv_row):
    me_seq, me_dp = lax.axis_index("seq"), lax.axis_index("dp")
    greet(seq, dp, me_seq, me_dp)
    keep = [
        pltpu.make_async_copy(small, params.at[me_dp, me_seq], own.at[0]),
        pltpu.make_async_copy(pieces.at[me_seq], swapped.at[me_seq], own.at[1]),
    ]
    for copy in keep:
        copy.start()
    tiny, large, rows = [], [], []
    for step in range(1, seq):
        target = lax.rem(me_seq + step, seq)
        tiny.append(
            pltpu.make_async_remote_copy(
                small, params.at[me_dp, me_seq], send_small.at[step], recv_small.at[step], (target, me_dp), MESH
            )
        )
        tiny[-1].start()
    for step in range(1, seq):
        target = lax.rem(me_seq + step, seq)
        large.append(
            pltpu.make_async_remote_copy(
                pieces.at[target], swapped.at[me_seq], send.at[step], recv.at[step], (target, me_dp), MESH
            )
        )
        large[-1].start()
    keep[0].wait()
    for copy in tiny:
        copy.wait()
    for step in range(1, dp):
        target = lax.rem(me_dp + step, dp)
        rows.append(
            pltpu.make_async_remote_copy(
                params.at[me_dp], params.at[me_dp], send_row.at[step], recv_row.at[step], (me_seq, target), MESH
            )
        )
        rows[-1].start()
    keep[1].wait()
    for copy in rows + large:
        copy.wait()


def opening(seq, dp, pieces, small):
    anywhere = pl.BlockSpec(memory_space=pl.ANY)
    return pl.pallas_call(
        functools.partial(opening_kernel, seq, dp),
        out_shape=(
            jax.ShapeDtypeStruct(pieces.shape, pieces.dtype),
            jax.ShapeDtypeStruct((dp, seq) + small.shape, small.dtype),
        ),
        in_specs=[anywhere, anywhere],
        out_specs=(anywhere, anywhere),
        scratch_shapes=[pltpu.SemaphoreType.DMA((2,))]
        + [pltpu.SemaphoreType.DMA((seq,))] * 4
        + [pltpu.SemaphoreType.DMA((dp,))] * 2,
        compiler_params=pltpu.CompilerParams(collective_id=1, has_side_effects=True),
        name="opening",
    )(pieces, small)


def closing_kernel(seq, dp, terms, total, over_seq, partial, over_dp, send, recv, send_row, recv_row):
    me_seq, me_dp = lax.axis_index("seq"), lax.axis_index("dp")
    greet(seq, dp, me_seq, me_dp)
    copies = []
    for step in range(1, seq):
        target = lax.rem(me_seq + step, seq)
        copies.append(
            pltpu.make_async_remote_copy(
                terms.at[target], over_seq.at[step], send.at[step], recv.at[step], (target, me_dp), MESH
            )
        )
        copies[-1].start()
    value = terms[me_seq]
    for step, copy in enumerate(copies):
        copy.wait()
        value = value + over_seq[step + 1]
    partial[...] = value
    copies = []
    for step in range(1, dp):
        target = lax.rem(me_dp + step, dp)
        copies.append(
            pltpu.make_async_remote_copy(
                partial.at[target], over_dp.at[step], send_row.at[step], recv_row.at[step], (me_seq, target), MESH
            )
        )
        copies[-1].start()
    value = partial[me_dp]
    for step, copy in enumerate(copies):
        copy.wait()
        value = value + over_dp[step + 1]
    total[...] = value


def closing(seq, dp, terms):
    tile = terms.shape[2:]
    inside = pl.BlockSpec(memory_space=pltpu.VMEM)
    return pl.pallas_call(
        functools.partial(closing_kernel, seq, dp),
        out_shape=jax.ShapeDtypeStruct(tile, F32),
        in_specs=[inside],
        out_specs=inside,
        scratch_shapes=[
            pltpu.VMEM(terms.shape, F32),
            pltpu.VMEM(terms.shape[1:], F32),
            pltpu.VMEM(terms.shape[1:], F32),
        ]
        + [pltpu.SemaphoreType.DMA((seq,))] * 2
        + [pltpu.SemaphoreType.DMA((dp,))] * 2,
        compiler_params=pltpu.CompilerParams(collective_id=2, has_side_effects=True),
        name="closing",
    )(terms)


def head_parts(ref, where, part, size):
    return [ref[where[place], 0, :, part * size : (part + 1) * size] for place in range(ref.shape[0])]


def diagonal(block):
    return lax.broadcasted_iota(jnp.int32, (block, block), 1) <= lax.broadcasted_iota(jnp.int32, (block, block), 0)


def masked_exp(query, keys, scaling):
    logits = cols_product(query, keys) * scaling
    block, length = logits.shape
    last = jnp.where(diagonal(block), logits[:, length - block :], MASKED)
    logits = last if length == block else jnp.concatenate([logits[:, : length - block], last], axis=1)
    raised = jnp.exp(logits - jnp.max(logits, axis=-1, keepdims=True))
    return raised, jnp.sum(raised, axis=-1, keepdims=True)


def attend_kernel(scaling, where, joint, attended):
    seq, _, block, size = attended.shape
    keys = jnp.concatenate(head_parts(joint, where, 1, size))
    values = jnp.concatenate(head_parts(joint, where, 2, size))
    for place in range(seq):
        length = (place + 1) * block
        query = joint[where[place], 0, :, :size]
        raised, sums = masked_exp(query, keys[:length], scaling)
        weights = (raised * (1.0 / sums)).astype(BF)
        attended[where[place], 0] = product(weights, values[:length]).astype(BF)


def attend(where, joint, size, scaling):
    seq, slots, block, width = joint.shape
    heads = width // (3 * size)
    return pl.pallas_call(
        functools.partial(attend_kernel, scaling),
        out_shape=jax.ShapeDtypeStruct((seq, slots, block, heads * size), BF),
        grid=(slots, heads),
        in_specs=[
            pl.BlockSpec(memory_space=pltpu.SMEM),
            pl.BlockSpec((seq, 1, block, 3 * size), lambda slot, head: (0, slot, 0, head)),
        ],
        out_specs=pl.BlockSpec((seq, 1, block, size), lambda slot, head: (0, slot, 0, head)),
        compiler_params=pltpu.CompilerParams(vmem_limit_bytes=48 << 20),
        name="attend",
    )(where, joint)


def attend_back_kernel(scaling, where, joint, flow, joint_back, key_sum, value_sum):
    seq, _, block, size = flow.shape
    keys = jnp.concatenate(head_parts(joint, where, 1, size))
    values = jnp.concatenate(head_parts(joint, where, 2, size))
    for place in reversed(range(seq)):
        length = (place + 1) * block
        spot = where[place]
        query = joint[spot, 0, :, :size]
        flow_here = flow[spot, 0]
        raised, sums = masked_exp(query, keys[:length], scaling)
        probs = raised * (1.0 / sums)
        weights = probs.astype(BF)
        prob_back = cols_product(flow_here, values[:length])
        mean_back = jnp.sum(probs * prob_back, axis=-1, keepdims=True)
        logit_back = (probs * (prob_back - mean_back)).astype(BF)
        joint_back[spot, 0, :, :size] = (product(logit_back, keys[:length]) * scaling).astype(BF)
        key_term = rows_product(logit_back, query) * scaling
        value_term = rows_product(weights, flow_here)
        if place == seq - 1:
            key_sum[...] = key_term
            value_sum[...] = value_term
        else:
            key_sum[:length] += key_term
            value_sum[:length] += value_term
    for place in range(seq):
        rows = slice(place * block, (place + 1) * block)
        joint_back[where[place], 0, :, size : 2 * size] = key_sum[rows].astype(BF)
        joint_back[where[place], 0, :, 2 * size :] = value_sum[rows].astype(BF)


def attend_back(where, joint, flow, size, scaling):
    seq, slots, block, width = joint.shape
    heads = width // (3 * size)
    wide = pl.BlockSpec((seq, 1, block, 3 * size), lambda slot, head: (0, slot, 0, head))
    return pl.pallas_call(
        functools.partial(attend_back_kernel, scaling),
        out_shape=jax.ShapeDtypeStruct(joint.shape, BF),
        grid=(slots, heads),
        in_specs=[
            pl.BlockSpec(memory_space=pltpu.SMEM),
            wide,
            pl.BlockSpec((seq, 1, block, size), lambda slot, head: (0, slot, 0, head)),
        ],
        out_specs=wide,
        scratch_shapes=[pltpu.VMEM((seq * block, size), F32)] * 2,
        compiler_params=pltpu.CompilerParams(vmem_limit_bytes=48 << 20),
        name="attend_back",
    )(where, joint, flow)


def swap_over_seq(pieces, count):
    me = lax.axis_index("seq")
    result = jnp.zeros_like(pieces)
    own = lax.dynamic_index_in_dim(pieces, me, 0, keepdims=True)
    result = lax.dynamic_update_index_in_dim(result, own, me, 0)
    for step in range(1, count):
        if count & (count - 1) == 0:
            target, source = me ^ step, me ^ step
            pairs = [(i, i ^ step) for i in range(count)]
        else:
            target, source = (me + step) % count, (me - step) % count
            pairs = [(i, (i + step) % count) for i in range(count)]
        sent = lax.dynamic_index_in_dim(pieces, target, 0, keepdims=True)
        got = lax.ppermute(sent, "seq", pairs)
        result = lax.dynamic_update_index_in_dim(result, got, source, 0)
    return result


def make_layer(seq, dp):
    xor = seq & (seq - 1) == 0

    def shift(values, step):
        pairs = [(i, i ^ step if xor else (i + step) % seq) for i in range(seq)]
        return lax.ppermute(values, "seq", pairs)

    def gather_seq(block):
        if seq != 4:
            return [block] + [shift(block, step) for step in range(1, seq)]
        half = block.shape[0] // 2
        near, far = shift(block, 1), shift(block, 2)
        corner = [shift(near[:half], 2), shift(far[half:], 1)]
        return [block, near, far, jnp.concatenate(corner)]

    def scatter_seq(make):
        if seq != 4:
            sent = [shift(make(step).astype(BF), step if xor else seq - step).astype(F32) for step in range(1, seq)]
            return make(0) + sum(sent)
        corner = make(3).astype(BF)
        half = corner.shape[0] // 2
        by_near, by_far = shift(corner[:half], 1), shift(corner[half:], 2)
        near = lax.optimization_barrier(make(1).astype(BF))
        far = lax.optimization_barrier(make(2).astype(BF))
        near_first, far_last = shift(near[:half], 1), shift(far[half:], 2)
        near_last = shift((near[half:].astype(F32) + by_far.astype(F32)).astype(BF), 1)
        far_first = shift((far[:half].astype(F32) + by_near.astype(F32)).astype(BF), 2)
        first = near_first.astype(F32) + far_first.astype(F32)
        last = near_last.astype(F32) + far_last.astype(F32)
        return make(0) + jnp.concatenate([first, last])

    def column_pieces(shard, thirds, groups):
        rows, columns = shard.shape
        shaped = shard.reshape(rows, thirds, seq, groups, -1).transpose(2, 0, 3, 1, 4)
        return shaped.reshape(seq, rows, columns // seq)

    def gather_columns(swapped):
        return lax.all_gather(swapped, "dp", axis=1, tiled=True).reshape(-1, swapped.shape[2])

    def scatter_columns(term, thirds, groups):
        total, width = term.shape
        rows = total // (seq * dp)
        summed = lax.psum_scatter(
            term.astype(BF).reshape(seq, dp * rows, width), "dp", scatter_dimension=1, tiled=True
        )
        swapped = swap_over_seq(summed, seq)
        shaped = swapped.reshape(seq, rows, groups, thirds, -1).transpose(1, 3, 0, 2, 4)
        return shaped.reshape(rows, seq * width).astype(F32)

    def scatter_rows(term):
        return lax.psum_scatter(term.astype(BF), "dp", scatter_dimension=0, tiled=True).astype(F32)

    def layer(
        inputs, counts, cotangent, stretch, offset, inward, outward, dilation, translation, upward, downward
    ):
        slots, block, model = inputs.shape
        head_size = model // HEADS
        heads = HEADS // seq
        scaling = 1.0 / math.sqrt(head_size)
        local_rows = slots * block
        total = seq * local_rows
        live = jnp.repeat((jnp.arange(slots) < counts[0]).astype(F32), block)[:, None]
        residual = inputs.reshape(local_rows, model)
        small = jnp.stack([stretch, offset, dilation, translation]).astype(F32).reshape(-1)
        taken = small.shape[0]
        small = jnp.pad(small, (0, -taken % 1024)).reshape(-1, 128)
        swapped_in, small = opening(seq, dp, column_pieces(inward, 3, heads), small)
        small = small.reshape(dp, seq, -1)[:, :, :taken].reshape(dp, seq, 4, -1).transpose(2, 1, 0, 3).reshape(4, model)
        gain_one, shift_one, gain_two, shift_two = small[0], small[1], small[2], small[3]
        matrix_in = gather_columns(swapped_in)
        blocks = gather_seq(after(residual, swapped_in))
        matrix_out = lax.all_gather(after(outward, matrix_in), "dp", axis=0, tiled=True)
        swapped_up = swap_over_seq(after(column_pieces(upward, 1, 1), blocks[-1]), seq)
        matrix_up = gather_columns(swapped_up)
        matrix_down = lax.all_gather(after(downward, matrix_up), "dp", axis=0, tiled=True)
        upstream = (cotangent.astype(F32).reshape(local_rows, model) * live).astype(BF)
        upstream_all = jnp.concatenate(gather_seq(after(upstream, swapped_up)))

        def piece(values, step):
            return values[step * local_rows : (step + 1) * local_rows]

        def norm_one(values):
            return (norm_parts(values.astype(F32))[0] * gain_one + shift_one).astype(BF)

        normed = [norm_one(part) for part in blocks]
        projected = jnp.concatenate([product(part, matrix_in).astype(BF) for part in normed])
        normed = jnp.concatenate(normed)

        me = lax.axis_index("seq")
        where = me ^ jnp.arange(seq) if xor else (me + seq - jnp.arange(seq)) % seq
        joint = projected.reshape(seq, slots, block, -1)
        attended = attend(where, joint, head_size, scaling).reshape(total, heads * head_size)
        middle = residual.astype(F32) + scatter_seq(lambda step: product(piece(attended, step), matrix_out))
        unit_two, root_two = norm_parts(middle)
        normed_two = gather_seq((unit_two * gain_two + shift_two).astype(BF))
        expanded = [product(part, matrix_up) for part in normed_two]
        normed_two = jnp.concatenate(normed_two)
        hidden = [smooth_gate(part).astype(BF) for part in expanded]
        def gate_back(step):
            flow = cols_product(piece(upstream_all, step), matrix_down)
            return jax.vjp(smooth_gate, expanded[step])[1](flow)[0].astype(BF)

        expanded_back = [gate_back(step) for step in range(seq)]
        two_back = scatter_seq(lambda step: cols_product(expanded_back[step], matrix_up))
        expanded_back = jnp.concatenate(expanded_back)
        downward_delta = scatter_rows(rows_product(jnp.concatenate(hidden), upstream_all))
        upward_delta = scatter_columns(rows_product(normed_two, expanded_back), 1, 1)
        middle_flow, dilation_term, translation_term = norm_back(two_back, unit_two, root_two, gain_two)
        middle_back = upstream.astype(F32) + middle_flow
        middle_low = gather_seq(middle_back.astype(BF))
        heads_back = jnp.concatenate([cols_product(part, matrix_out).astype(BF) for part in middle_low])
        result = middle + scatter_seq(lambda step: product(after(hidden[step], middle_low[-1]), matrix_down))
        outputs = (result * live).astype(BF).reshape(slots, block, model)
        outward_delta = scatter_rows(rows_product(attended, jnp.concatenate(middle_low)))
        heads_back = after(heads_back, downward_delta).reshape(seq, slots, block, -1)
        projected_back = attend_back(where, joint, heads_back, head_size, scaling).reshape(total, -1)
        inward_delta = scatter_columns(rows_product(normed, projected_back), 3, heads)
        one_back = scatter_seq(lambda step: cols_product(piece(projected_back, step), matrix_in))
        unit_one, root_one = norm_parts(residual.astype(F32))
        input_flow, stretch_term, offset_term = norm_back(one_back, unit_one, root_one, gain_one)
        terms = jnp.stack([stretch_term, offset_term, dilation_term, translation_term])
        terms = terms.reshape(4, seq, dp, -1).transpose(1, 2, 0, 3).reshape(seq, dp, -1)
        terms = jnp.pad(terms, ((0, 0), (0, 0), (0, -taken % 1024))).reshape(seq, dp, -1, 128)
        deltas = closing(seq, dp, terms).reshape(-1)[:taken].reshape(4, -1)
        input_delta = (middle_back + input_flow).reshape(slots, block, model)
        return (
            outputs,
            input_delta,
            deltas[0],
            deltas[1],
            inward_delta,
            outward_delta,
            deltas[2],
            deltas[3],
            upward_delta,
            downward_delta,
        )

    return layer


def solution(mesh):
    tokens, vector, matrix = P("dp", "seq", None), P(("seq", "dp")), P(("seq", "dp"), None)
    return jax.shard_map(
        make_layer(mesh.shape["seq"], mesh.shape["dp"]),
        mesh=mesh,
        in_specs=(tokens, P("dp"), tokens, vector, vector, matrix, matrix, vector, vector, matrix, matrix),
        out_specs=(tokens, tokens, vector, vector, matrix, matrix, vector, vector, matrix, matrix),
        check_vma=False,
    )
```

time: 1560 us -> 1050 us (0.67)
  waiting for transfers between devices: 955 us -> 457 us
  matrix products: 340 us -> 261 us
  Pallas kernels: 0 us -> 76.6 us
  blocking collectives: 41.3 us -> 0 us
  starting transfers between devices: 17.1 us -> 57.4 us
  other arithmetic: 85 us -> 63.4 us
    ppermute x0 -> x40, waiting for transfers between devices: none -> 373 us  [shift(): return lax.ppermute(values, 'seq', pairs)]
    all_gather x6 -> x2, waiting for transfers between devices: 315 us -> 0.01 us  [the longest x1 0.01 us: layer(): lax.all_gather(after(outward, matrix_in), 'dp', axis=0, tiled=True)]
    reduce_scatter x4 -> x0, waiting for transfers between devices: 299 us -> none  [scatter_seq(): got = lax.psum_scatter(shaped, 'seq', scatter_dimension=1, tiled=True)]
    unnamed x18 -> x8, waiting for transfers between devices: 131 us -> 0.13 us
    dot_general x5 -> x0, matrix products: 77.5 us -> none  [the longest x1 25.5 us: layer(): jnp.einsum('sqhd,skhd->shqk', heads_back, value, preferred_element_type=F32)]
    pallas_call x0 -> x4, Pallas kernels: none -> 76.6 us  [the longest x1 29.4 us: attend_back(): pl.pallas_call(functools.partial(attend_back_kernel, scaling), out_shape=...]
    all_gather x2, waiting for transfers between devices: 111 us -> 55.3 us  [gather_columns(): lax.all_gather(swapped, 'dp', axis=1, tiled=True)]
    ppermute x0 -> x40, starting transfers between devices: none -> 46.2 us  [shift(): return lax.ppermute(values, 'seq', pairs)]
  transfers between devices with their start and end apart: 29 -> 57, of which waited for: 20 -> 27; matrix products, arithmetic and copies ran while one was open for 28% -> 32% of each run, Pallas kernels for 0% -> 6%
where the time goes in v2:
time: 1050 us; the launch traced here: 1040 us
  waiting for transfers between devices  457 us (44%)
  matrix products  261 us (25%)
  local copies, waits for them, and re-layouts  104 us (10%)
  Pallas kernels  76.6 us (7%)
  other arithmetic  63.4 us (6%)
  starting transfers between devices  57.4 us (5%)
  between operations  16.9 us (2%)
    ppermute x40, waiting for transfers between devices, shift(): return lax.ppermute(values, 'seq', pairs)  373 us
    dot_general x16, matrix products, product(): return jnp.dot(left, right, preferred_element_type=F32)  106 us
    dot_general x16, matrix products, cols_product(): lax.dot_general(left, right, (((1,), (1,)), ((), ())), preferred_element_...  90 us
    dot_general x4, matrix products, rows_product(): lax.dot_general(left, right, (((0,), (0,)), ((), ())), preferred_element_...  65.5 us
    all_gather x2, waiting for transfers between devices, gather_columns(): lax.all_gather(swapped, 'dp', axis=1, tiled=True)  55.3 us
    ppermute x40, starting transfers between devices, shift(): return lax.ppermute(values, 'seq', pairs)  46.2 us
    pallas_call x1, Pallas kernels, attend_back(): pl.pallas_call(functools.partial(attend_back_kernel, scaling), out_shape=...  29.4 us
    ppermute x9, waiting for transfers between devices, swap_over_seq(): got = lax.ppermute(sent, 'seq', pairs)  28.6 us
  transfers between devices with their start and end apart: 57, of which 27 were waited for; matrix products, arithmetic and copies ran while one was open for 32% of the time, Pallas kernels for 6%

profile of v2, /device:TPU:0, one launch (start us, length us, event | category | flops | bytes accessed | tf_op | source)
XLA Modules:
  0.0 1036.3 jit_solution(15373387614359790178)
XLA Ops:
  14.2 16.9 %opening.1 = (bf16[4,64,1536]{2,1,0:T(8,128)(2,1)}, f32[8,4,8,128]{3,2,1,0:T(8,128)}) custom-call(bf16[4,64,1536]{2,1,0:T(8,128)(2,1)} %reshape.263.pieces, f32[8,128]{1,0:T(8,128)} %bitcast_convert_fusion.small), custom_call_target="tpu_custom_call" | custom-call | tf_op jit(solution)/shard_map/opening/pallas_call | solution.py:106
  33.3 45.2 %collective-permute-done = bf16[512,2048]{1,0:T(8,128)(2,1)S(1)} collective-permute-done((bf16[512,2048]{1,0:T(8,128)(2,1)S(1)}, bf16[512,2048]{1,0:T(8,128)(2,1)S(1)}, u32[]{:S(2)}, u32[]{:S(2)}) %collective-permute-start) | collective-permute-done | bytes 2097184 | tf_op jit(solution)/shard_map/ppermute | solution.py:294
  85.1 18.6 %collective-permute-done.2 = bf16[256,2048]{1,0:T(8,128)(2,1)} collective-permute-done((bf16[256,2048]{1,0:T(8,128)(2,1)}, bf16[256,2048]{1,0:T(8,128)(2,1)}, u32[]{:S(2)}, u32[]{:S(2)}) %collective-permute-start.2) | collective-permute-done | bytes 1048608 | tf_op jit(solution)/shard_map/ppermute | solution.py:294
  161.5 55.3 %all-gather.9.cloned.1.call-done = bf16[4,512,2048]{2,1,0:T(8,128)(2,1)} async-done(((bf16[4,64,2048]{2,1,0:T(8,128)(2,1)}), bf16[4,512,2048]{2,1,0:T(8,128)(2,1)}) %all-gather.9.cloned.1.call-update) | async-done | bytes 8388624 | tf_op jit(solution)/shard_map/all_gather | solution.py:326
  237.5 19.6 %attend.1 = bf16[4,2,256,512]{3,2,1,0:T(8,128)(2,1)S(1)} custom-call(s32[4]{0:T(128)S(1)} %iota_xor_fusion.where, bf16[4,2,256,1536]{3,2,1,0:T(8,128)(2,1)} %bitcast.158), custom_call_target="tpu_custom_call" | custom-call | tf_op jit(solution)/shard_map/attend/pallas_call | solution.py:207
  273.9 16.5 %collective-permute-done.5 = bf16[256,2048]{1,0:T(8,128)(2,1)} collective-permute-done((bf16[256,2048]{1,0:T(8,128)(2,1)}, bf16[256,2048]{1,0:T(8,128)(2,1)}, u32[]{:S(2)}, u32[]{:S(2)}) %collective-permute-start.5) | collective-permute-done | bytes 1048608 | tf_op jit(solution)/shard_map/ppermute | solution.py:294
  296.7 16.1 %collective-permute-done.4 = bf16[256,2048]{1,0:T(8,128)(2,1)S(1)} collective-permute-done((bf16[256,2048]{1,0:T(8,128)(2,1)S(1)}, bf16[256,2048]{1,0:T(8,128)(2,1)S(1)}, u32[]{:S(2)}, u32[]{:S(2)}) %collective-permute-start.4) | collective-permute-done | bytes 1048608 | tf_op jit(solution)/shard_map/ppermute | solution.py:294
  314.3 23.4 %collective-permute-done.6 = bf16[256,2048]{1,0:T(8,128)(2,1)S(1)} collective-permute-done((bf16[256,2048]{1,0:T(8,128)(2,1)S(1)}, bf16[256,2048]{1,0:T(8,128)(2,1)S(1)}, u32[]{:S(2)}, u32[]{:S(2)}) %collective-permute-start.6) | collective-permute-done | bytes 1048608 | tf_op jit(solution)/shard_map/ppermute | solution.py:294
  344.9 35.3 %collective-permute-done.13 = bf16[512,2048]{1,0:T(8,128)(2,1)S(1)} collective-permute-done((bf16[512,2048]{1,0:T(8,128)(2,1)S(1)}, bf16[512,2048]{1,0:T(8,128)(2,1)S(1)}, u32[]{:S(2)}, u32[]{:S(2)}) %collective-permute-start.13) | collective-permute-done | bytes 2097184 | tf_op jit(solution)/shard_map/ppermute | solution.py:294
  383.7 41.4 %collective-permute-done.14 = bf16[512,2048]{1,0:T(8,128)(2,1)S(1)} collective-permute-done((bf16[512,2048]{1,0:T(8,128)(2,1)S(1)}, bf16[512,2048]{1,0:T(8,128)(2,1)S(1)}, u32[]{:S(2)}, u32[]{:S(2)}) %collective-permute-start.14) | collective-permute-done | bytes 2097184 | tf_op jit(solution)/shard_map/ppermute | solution.py:294
  428.9 21.1 %collective-permute-done.18 = bf16[256,2048]{1,0:T(8,128)(2,1)S(1)} collective-permute-done((bf16[256,2048]{1,0:T(8,128)(2,1)S(1)}, bf16[256,2048]{1,0:T(8,128)(2,1)S(1)}, u32[]{:S(2)}, u32[]{:S(2)}) %collective-permute-start.18) | collective-permute-done | bytes 1048608 | tf_op jit(solution)/shard_map/ppermute | solution.py:294
  451.2 20.3 %collective-permute-done.20 = bf16[256,2048]{1,0:T(8,128)(2,1)S(1)} collective-permute-done((bf16[256,2048]{1,0:T(8,128)(2,1)S(1)}, bf16[256,2048]{1,0:T(8,128)(2,1)S(1)}, u32[]{:S(2)}, u32[]{:S(2)}) %collective-permute-start.20) | collective-permute-done | bytes 1048608 | tf_op jit(solution)/shard_map/ppermute | solution.py:294
  488.1 12.1 %multiply_convert_fusion.3 = (bf16[512,2048]{1,0:T(8,128)(2,1)S(1)}, bf16[512,2048]{1,0:T(8,128)(2,1)}) fusion(f32[512,2048]{1,0:T(8,128)S(1)} %fusion.123, bf16[512,2048]{1,0:T(8,128)(2,1)S(1)} %copy-done.35, bf16[2048,2048]{1,0:T(8,128)(2,1)} %bitcast.196), kind=kOutput, calls=%fused_computation.126 | convolution fusion | flops 4318035968 | bytes 18874368 | tf_op jit(solution)/shard_map/dot_general | solution.py:46
  512.7 13.1 %multiply_convert_fusion.2 = (bf16[512,2048]{1,0:T(8,128)(2,1)}, bf16[512,2048]{1,0:T(8,128)(2,1)}) fusion(f32[512,2048]{1,0:T(8,128)} %fusion.124, bf16[512,2048]{1,0:T(8,128)(2,1)S(1)} %copy-done.23, bf16[2048,2048]{1,0:T(8,128)(2,1)} %bitcast.197), kind=kOutput, calls=%fused_computation.123 | convolution fusion | flops 4318035968 | bytes 18874368 | tf_op jit(solution)/shard_map/dot_general | solution.py:46
  536.4 21.2 %fusion.30 = bf16[2048,2048]{1,0:T(8,128)(2,1)} fusion(bf16[2048,2048]{1,0:T(8,128)(2,1)S(1)} %bitcast.175, bf16[512,2048]{1,0:T(8,128)(2,1)} %get-tuple-element.32, bf16[512,2048]{1,0:T(8,128)(2,1)} %get-tuple-element.31, bf16[512,2048]{1,0:T(8,128)(2,1)} %get-tuple-element.30, bf16[512,2048]{1,0:T(8,128)(2,1)S(1)} %get-tuple-element.29), kind=kOutput, calls=%fused_computation.26 | convolution fusion | flops 17217617920 | bytes 25165824 | tf_op jit(solution)/shard_map/dot_general | solution.py:38
  574.3 19.8 %fusion.24 = bf16[2048,2048]{1,0:T(8,128)(2,1)} fusion(bf16[2048,2048]{1,0:T(8,128)(2,1)S(1)} %copy-done.53, bf16[512,2048]{1,0:T(8,128)(2,1)S(1)} %fusion.95, bf16[512,2048]{1,0:T(8,128)(2,1)S(1)} %copy-done.78, bf16[512,2048]{1,0:T(8,128)(2,1)S(1)} %copy-done.77, bf16[512,2048]{1,0:T(8,128)(2,1)S(1)} %copy-done.74), kind=kOutput, calls=%fused_computation.24 | convolution fusion | flops 17217617920 | bytes 25165824 | tf_op jit(solution)/shard_map/dot_general | solution.py:38
  633.1 18.6 %collective-permute-done.15 = bf16[256,2048]{1,0:T(8,128)(2,1)S(1)} collective-permute-done((bf16[256,2048]{1,0:T(8,128)(2,1)S(1)}, bf16[256,2048]{1,0:T(8,128)(2,1)S(1)}, u32[]{:S(2)}, u32[]{:S(2)}) %collective-permute-start.15) | collective-permute-done | bytes 1048608 | tf_op jit(solution)/shard_map/ppermute | solution.py:294
  656.2 17.8 %collective-permute-done.26 = bf16[256,2048]{1,0:T(8,128)(2,1)S(1)} collective-permute-done((bf16[256,2048]{1,0:T(8,128)(2,1)S(1)}, bf16[256,2048]{1,0:T(8,128)(2,1)S(1)}, u32[]{:S(2)}, u32[]{:S(2)}) %collective-permute-start.26) | collective-permute-done | bytes 1048608 | tf_op jit(solution)/shard_map/ppermute | solution.py:294
  693.2 40.3 %collective-permute-done.27 = bf16[512,2048]{1,0:T(8,128)(2,1)S(1)} collective-permute-done((bf16[512,2048]{1,0:T(8,128)(2,1)S(1)}, bf16[512,2048]{1,0:T(8,128)(2,1)S(1)}, u32[]{:S(2)}, u32[]{:S(2)}) %collective-permute-start.27) | collective-permute-done | bytes 2097184 | tf_op jit(solution)/shard_map/ppermute | solution.py:294
  742.6 13.4 %collective-permute-done.28 = bf16[256,2048]{1,0:T(8,128)(2,1)S(1)} collective-permute-done((bf16[256,2048]{1,0:T(8,128)(2,1)S(1)}, bf16[256,2048]{1,0:T(8,128)(2,1)S(1)}, u32[]{:S(2)}, u32[]{:S(2)}) %collective-permute-start.28) | collective-permute-done | bytes 1048608 | tf_op jit(solution)/shard_map/ppermute | solution.py:294
  801.4 29.4 %attend_back.1 = bf16[4,2,256,1536]{3,2,1,0:T(8,128)(2,1)} custom-call(s32[4]{0:T(128)S(1)} %copy-done.3, bf16[4,2,256,1536]{3,2,1,0:T(8,128)(2,1)} %bitcast.159, bf16[4,2,256,512]{3,2,1,0:T(8,128)(2,1)S(1)} %bitcast.152), custom_call_target="tpu_custom_call" | custom-call | tf_op jit(solution)/shard_map/attend_back/pallas_call | solution.py:255
  830.9 18.8 %fusion.27 = bf16[2048,1536]{1,0:T(8,128)(2,1)} fusion(bf16[2048,1536]{1,0:T(8,128)(2,1)} %bitcast.160, bf16[512,2048]{1,0:T(8,128)(2,1)} %get-tuple-element.95, bf16[512,2048]{1,0:T(8,128)(2,1)S(1)} %copy-done.40, bf16[512,2048]{1,0:T(8,128)(2,1)S(1)} %copy-done.38, bf16[512,2048]{1,0:T(8,128)(2,1)S(1)} %copy-done.37), kind=kOutput, calls=%fused_computation.25 | convolution fusion | flops 12921602048 | bytes 20971520 | tf_op jit(solution)/shard_map/dot_general | solution.py:38
  861.8 12.7 %collective-permute-done.35 = bf16[256,2048]{1,0:T(8,128)(2,1)} collective-permute-done((bf16[256,2048]{1,0:T(8,128)(2,1)}, bf16[256,2048]{1,0:T(8,128)(2,1)}, u32[]{:S(2)}, u32[]{:S(2)}) %collective-permute-start.35) | collective-permute-done | bytes 1048608 | tf_op jit(solution)/shard_map/ppermute | solution.py:294
  902.9 11.1 %collective-permute-done.38 = bf16[256,2048]{1,0:T(8,128)(2,1)S(1)} collective-permute-done((bf16[256,2048]{1,0:T(8,128)(2,1)S(1)}, bf16[256,2048]{1,0:T(8,128)(2,1)S(1)}, u32[]{:S(2)}, u32[]{:S(2)}) %collective-permute-start.38) | collective-permute-done | bytes 1048608 | tf_op jit(solution)/shard_map/ppermute | solution.py:294
  (496 shorter events, 461.3 us)
Async XLA Ops:
  7.2 132.2 %all-gather.5.cloned.1.call-start = ((), (), s32[]{:S(2)}) async-start(), calls=%async_computation.4 | async-start | bytes 7077888 | tf_op jit(solution)/shard_map/all_gather | solution.py:326
  31.1 185.7 %all-gather.9.cloned.1.call-start = ((), (), s32[]{:S(2)}) async-start(), calls=%async_computation.6 | async-start | bytes 9437184 | tf_op jit(solution)/shard_map/all_gather | solution.py:326
  136.2 123.5 %all-gather.7.cloned.1.call-start = ((), (), s32[]{:S(2)}) async-start(), calls=%async_computation.5 | async-start | bytes 2359296 | tf_op jit(solution)/shard_map/all_gather | solution.py:360
  139.5 341.5 %all-gather.11.cloned.1.call-start = ((), (), s32[]{:S(2)}) async-start(), calls=%async_computation.7 | async-start | bytes 9437184 | tf_op jit(solution)/shard_map/all_gather | solution.py:363
  216.9 581.7 %reduce-scatter.5.cloned.1.call-start = ((), (), s32[]{:S(2)}) async-start(), calls=%async_computation.8 | async-start | bytes 9437184 | tf_op jit(solution)/shard_map/reduce_scatter | solution.py:339
  273.4 64.7 %collective-permute-start.9 = (bf16[256,2048]{1,0:T(8,128)(2,1)S(1)}, bf16[256,2048]{1,0:T(8,128)(2,1)S(1)}, u32[]{:S(2)}, u32[]{:S(2)}) collective-permute-start(bf16[256,2048]{1,0:T(8,128)(2,1)S(1)} %slice.251), channel_id=1, source_target_pairs={{0,16},{8,24},{16,0},{24,8},{1,17},{9,25},{17,1},{25,9},{2,18},{10... | collective-permute-start | bytes 3145736 | tf_op jit(solution)/shard_map/ppermute | solution.py:294
  296.0 84.2 %collective-permute-start.13 = (bf16[512,2048]{1,0:T(8,128)(2,1)S(1)}, bf16[512,2048]{1,0:T(8,128)(2,1)S(1)}, u32[]{:S(2)}, u32[]{:S(2)}) collective-permute-start(bf16[512,2048]{1,0:T(8,128)(2,1)S(1)} %fusion.99), channel_id=1, source_target_pairs={{0,8},{8,0},{16,24},{24,16},{1,9},{9,1},{17,25},{25,17},{2,10},{10... | collective-permute-start | bytes 6291464 | tf_op jit(solution)/shard_map/ppermute | solution.py:294
  312.8 69.9 %collective-permute-start.16 = (bf16[512,2048]{1,0:T(8,128)(2,1)S(1)}, bf16[512,2048]{1,0:T(8,128)(2,1)S(1)}, u32[]{:S(2)}, u32[]{:S(2)}) collective-permute-start(bf16[512,2048]{1,0:T(8,128)(2,1)S(1)} %fusion.99), channel_id=1, source_target_pairs={{0,16},{8,24},{16,0},{24,8},{1,17},{9,25},{17,1},{25,9},{2,18},{10... | collective-permute-start | bytes 6291464 | tf_op jit(solution)/shard_map/ppermute | solution.py:294
  342.8 82.4 %collective-permute-start.14 = (bf16[512,2048]{1,0:T(8,128)(2,1)S(1)}, bf16[512,2048]{1,0:T(8,128)(2,1)S(1)}, u32[]{:S(2)}, u32[]{:S(2)}) collective-permute-start(bf16[512,2048]{1,0:T(8,128)(2,1)S(1)} %get-tuple-element.47), channel_id=1, source_target_pairs={{0,8},{8,0},{16,24},{24,16},{1,9},{9,1},{17,25},{25,17},{2,10},{10... | collective-permute-start | bytes 6291464 | tf_op jit(solution)/shard_map/ppermute | solution.py:294
  343.4 84.2 %collective-permute-start.17 = (bf16[512,2048]{1,0:T(8,128)(2,1)S(1)}, bf16[512,2048]{1,0:T(8,128)(2,1)S(1)}, u32[]{:S(2)}, u32[]{:S(2)}) collective-permute-start(bf16[512,2048]{1,0:T(8,128)(2,1)S(1)} %get-tuple-element.47), channel_id=1, source_target_pairs={{0,16},{8,24},{16,0},{24,8},{1,17},{9,25},{17,1},{25,9},{2,18},{10... | collective-permute-start | bytes 6291464 | tf_op jit(solution)/shard_map/ppermute | solution.py:294
  380.3 69.8 %collective-permute-start.18 = (bf16[256,2048]{1,0:T(8,128)(2,1)S(1)}, bf16[256,2048]{1,0:T(8,128)(2,1)S(1)}, u32[]{:S(2)}, u32[]{:S(2)}) collective-permute-start(bf16[256,2048]{1,0:T(8,128)(2,1)S(1)} %slice.256), channel_id=1, source_target_pairs={{0,16},{8,24},{16,0},{24,8},{1,17},{9,25},{17,1},{25,9},{2,18},{10... | collective-permute-start | bytes 3145736 | tf_op jit(solution)/shard_map/ppermute | solution.py:294
  382.7 67.4 %collective-permute-start.19 = (bf16[256,2048]{1,0:T(8,128)(2,1)S(1)}, bf16[256,2048]{1,0:T(8,128)(2,1)S(1)}, u32[]{:S(2)}, u32[]{:S(2)}) collective-permute-start(bf16[256,2048]{1,0:T(8,128)(2,1)S(1)} %slice.257), channel_id=1, source_target_pairs={{0,8},{8,0},{16,24},{24,16},{1,9},{9,1},{17,25},{25,17},{2,10},{10... | collective-permute-start | bytes 3145736 | tf_op jit(solution)/shard_map/ppermute | solution.py:294
  557.6 320.2 %reduce-scatter.11.cloned.1.call-start = ((), (), s32[]{:S(2)}) async-start(), calls=%async_computation.11 | async-start | bytes 9437184 | tf_op jit(solution)/shard_map/reduce_scatter | solution.py:331
  594.2 338.9 %reduce-scatter.9.cloned.1.call-start = ((), (), s32[]{:S(2)}) async-start(), calls=%async_computation.10 | async-start | bytes 2359296 | tf_op jit(solution)/shard_map/reduce_scatter | solution.py:339
  771.6 237.0 %reduce-scatter.7.cloned.1.call-start = ((), (), s32[]{:S(2)}) async-start(), calls=%async_computation.9 | async-start | bytes 7077888 | tf_op jit(solution)/shard_map/reduce_scatter | solution.py:331
  790.1 64.5 %collective-permute-start.31 = (bf16[256,2048]{1,0:T(8,128)(2,1)}, bf16[256,2048]{1,0:T(8,128)(2,1)}, u32[]{:S(2)}, u32[]{:S(2)}) collective-permute-start(bf16[256,2048]{1,0:T(8,128)(2,1)} %slice.266), channel_id=1, source_target_pairs={{0,8},{8,0},{16,24},{24,16},{1,9},{9,1},{17,25},{25,17},{2,10},{10... | collective-permute-start | bytes 3145736 | tf_op jit(solution)/shard_map/ppermute | solution.py:294
  791.0 58.7 %collective-permute-start.34 = (bf16[256,2048]{1,0:T(8,128)(2,1)}, bf16[256,2048]{1,0:T(8,128)(2,1)}, u32[]{:S(2)}, u32[]{:S(2)}) collective-permute-start(bf16[256,2048]{1,0:T(8,128)(2,1)} %get-tuple-element.67), channel_id=1, source_target_pairs={{0,16},{8,24},{16,0},{24,8},{1,17},{9,25},{17,1},{25,9},{2,18},{10... | collective-permute-start | bytes 3145736 | tf_op jit(solution)/shard_map/ppermute | solution.py:294
  793.4 68.5 %collective-permute-start.36 = (bf16[256,2048]{1,0:T(8,128)(2,1)}, bf16[256,2048]{1,0:T(8,128)(2,1)}, u32[]{:S(2)}, u32[]{:S(2)}) collective-permute-start(bf16[256,2048]{1,0:T(8,128)(2,1)} %slice.271), channel_id=1, source_target_pairs={{0,16},{8,24},{16,0},{24,8},{1,17},{9,25},{17,1},{25,9},{2,18},{10... | collective-permute-start | bytes 3145736 | tf_op jit(solution)/shard_map/ppermute | solution.py:294
  797.2 61.4 %collective-permute-start.33 = (bf16[256,2048]{1,0:T(8,128)(2,1)S(1)}, bf16[256,2048]{1,0:T(8,128)(2,1)}, u32[]{:S(2)}, u32[]{:S(2)}) collective-permute-start(bf16[256,2048]{1,0:T(8,128)(2,1)S(1)} %add_convert_fusion.4), channel_id=1, source_target_pairs={{0,16},{8,24},{16,0},{24,8},{1,17},{9,25},{17,1},{25,9},{2,18},{10... | collective-permute-start | bytes 3145736 | tf_op jit(solution)/shard_map/ppermute | solution.py:294
  880.6 68.1 %collective-permute-start.48 = (bf16[1,64,2048]{2,1,0:T(8,128)(2,1)S(1)}, bf16[1,64,2048]{2,1,0:T(8,128)(2,1)}, u32[]{:S(2)}, u32[]{:S(2)}) collective-permute-start(bf16[1,64,2048]{2,1,0:T(8,128)(2,1)S(1)} %get-tuple-element.76), channel_id=1, source_target_pairs={{0,24},{8,16},{16,8},{24,0},{1,25},{9,17},{17,9},{25,1},{2,26},{10... | collective-permute-start | bytes 786440 | tf_op jit(solution)/shard_map/ppermute | solution.py:284
  914.0 63.5 %collective-permute-start.37 = (bf16[256,2048]{1,0:T(8,128)(2,1)}, bf16[256,2048]{1,0:T(8,128)(2,1)}, u32[]{:S(2)}, u32[]{:S(2)}) collective-permute-start(bf16[256,2048]{1,0:T(8,128)(2,1)} %slice.274), channel_id=1, source_target_pairs={{0,8},{8,0},{16,24},{24,16},{1,9},{9,1},{17,25},{25,17},{2,10},{10... | collective-permute-start | bytes 3145736 | tf_op jit(solution)/shard_map/ppermute | solution.py:294
  918.9 60.6 %collective-permute-start.42 = (bf16[256,2048]{1,0:T(8,128)(2,1)}, bf16[256,2048]{1,0:T(8,128)(2,1)}, u32[]{:S(2)}, u32[]{:S(2)}) collective-permute-start(bf16[256,2048]{1,0:T(8,128)(2,1)} %slice.281), channel_id=1, source_target_pairs={{0,16},{8,24},{16,0},{24,8},{1,17},{9,25},{17,1},{25,9},{2,18},{10... | collective-permute-start | bytes 3145736 | tf_op jit(solution)/shard_map/ppermute | solution.py:294
  920.9 56.7 %collective-permute-start.39 = (bf16[256,2048]{1,0:T(8,128)(2,1)}, bf16[256,2048]{1,0:T(8,128)(2,1)}, u32[]{:S(2)}, u32[]{:S(2)}) collective-permute-start(bf16[256,2048]{1,0:T(8,128)(2,1)} %add_convert_fusion.2), channel_id=1, source_target_pairs={{0,16},{8,24},{16,0},{24,8},{1,17},{9,25},{17,1},{25,9},{2,18},{10... | collective-permute-start | bytes 3145736 | tf_op jit(solution)/shard_map/ppermute | solution.py:294
  922.3 57.2 %collective-permute-start.41 = (bf16[256,2048]{1,0:T(8,128)(2,1)}, bf16[256,2048]{1,0:T(8,128)(2,1)}, u32[]{:S(2)}, u32[]{:S(2)}) collective-permute-start(bf16[256,2048]{1,0:T(8,128)(2,1)} %add_convert_fusion.1), channel_id=1, source_target_pairs={{0,8},{8,0},{16,24},{24,16},{1,9},{9,1},{17,25},{25,17},{2,10},{10... | collective-permute-start | bytes 3145736 | tf_op jit(solution)/shard_map/ppermute | solution.py:294
  (134 other events, 2588.2 us)
Sparse Core Ops, SparseCore 0:
  31.3 63.1 all-gather.4
  136.3 80.5 all-gather.8
  218.5 27.6 all-gather.6
  247.6 81.5 all-gather.10
  557.7 87.1 reduce-scatter.4
  647.1 87.9 reduce-scatter.10
  771.8 34.1 reduce-scatter.8
  849.8 67.8 reduce-scatter.6

commit v3 on v2

--- a/solution.py
+++ b/solution.py
@@ -28,10 +28,6 @@
     first = jnp.mean(scaled, axis=-1, keepdims=True)
     second = jnp.mean(scaled * unit, axis=-1, keepdims=True)
     return root * (scaled - first - unit * second), jnp.sum(flow * unit, axis=0), jnp.sum(flow, axis=0)
-
-
-def smooth_gate(values):
-    return jax.nn.gelu(values, approximate=True)
 
 
 def rows_product(left, right):
@@ -59,16 +55,28 @@
     pl.semaphore_wait(barrier, seq + dp - 2)
 
 
-def opening_kernel(seq, dp, pieces, small, swapped, params, own, send, recv, send_small, recv_small, send_row, recv_row):
+def start_trade(seq, me_seq, me_dp, pieces, swapped, own, send, recv):
+    copies = [pltpu.make_async_copy(pieces.at[me_seq], swapped.at[me_seq], own)]
+    copies[0].start()
+    for step in range(1, seq):
+        target = lax.rem(me_seq + step, seq)
+        copies.append(
+            pltpu.make_async_remote_copy(
+                pieces.at[target], swapped.at[me_seq], send.at[step], recv.at[step], (target, me_dp), MESH
+            )
+        )
+        copies[-1].start()
+    return copies
+
+
+def opening_kernel(
+    seq, dp, pieces, pieces_two, small, swapped, swapped_two, params, own, send, recv, send_two, recv_two, send_small, recv_small, send_row, recv_row
+):
     me_seq, me_dp = lax.axis_index("seq"), lax.axis_index("dp")
     greet(seq, dp, me_seq, me_dp)
-    keep = [
-        pltpu.make_async_copy(small, params.at[me_dp, me_seq], own.at[0]),
-        pltpu.make_async_copy(pieces.at[me_seq], swapped.at[me_seq], own.at[1]),
-    ]
-    for copy in keep:
-        copy.start()
-    tiny, large, rows = [], [], []
+    keep = pltpu.make_async_copy(small, params.at[me_dp, me_seq], own.at[0])
+    keep.start()
+    tiny, rows = [], []
     for step in range(1, seq):
         target = lax.rem(me_seq + step, seq)
         tiny.append(
@@ -77,16 +85,9 @@
             )
         )
         tiny[-1].start()
-    for step in range(1, seq):
-        target = lax.rem(me_seq + step, seq)
-        large.append(
-            pltpu.make_async_remote_copy(
-                pieces.at[target], swapped.at[me_seq], send.at[step], recv.at[step], (target, me_dp), MESH
-            )
-        )
-        large[-1].start()
-    keep[0].wait()
-    for copy in tiny:
+    large = start_trade(seq, me_seq, me_dp, pieces, swapped, own.at[1], send, recv)
+    large += start_trade(seq, me_seq, me_dp, pieces_two, swapped_two, own.at[2], send_two, recv_two)
+    for copy in [keep] + tiny:
         copy.wait()
     for step in range(1, dp):
         target = lax.rem(me_dp + step, dp)
@@ -96,30 +97,33 @@
             )
         )
         rows[-1].start()
-    keep[1].wait()
     for copy in rows + large:
         copy.wait()
 
 
-def opening(seq, dp, pieces, small):
+def opening(seq, dp, pieces, pieces_two, small):
     anywhere = pl.BlockSpec(memory_space=pl.ANY)
     return pl.pallas_call(
         functools.partial(opening_kernel, seq, dp),
         out_shape=(
             jax.ShapeDtypeStruct(pieces.shape, pieces.dtype),
+            jax.ShapeDtypeStruct(pieces_two.shape, pieces_two.dtype),
             jax.ShapeDtypeStruct((dp, seq) + small.shape, small.dtype),
         ),
-        in_specs=[anywhere, anywhere],
-        out_specs=(anywhere, anywhere),
-        scratch_shapes=[pltpu.SemaphoreType.DMA((2,))]
-        + [pltpu.SemaphoreType.DMA((seq,))] * 4
+        in_specs=[anywhere] * 3,
+        out_specs=(anywhere,) * 3,
+        scratch_shapes=[pltpu.SemaphoreType.DMA((3,))]
+        + [pltpu.SemaphoreType.DMA((seq,))] * 6
         + [pltpu.SemaphoreType.DMA((dp,))] * 2,
         compiler_params=pltpu.CompilerParams(collective_id=1, has_side_effects=True),
         name="opening",
-    )(pieces, small)
-
-
-def closing_kernel(seq, dp, terms, total, over_seq, partial, over_dp, send, recv, send_row, recv_row):
+    )(pieces, pieces_two, small)
+
+
+def closing_kernel(
+    seq, dp, terms, pieces, pieces_two, total, swapped, swapped_two, over_seq, partial, over_dp,
+    own, send, recv, send_two, recv_two, send_seq, recv_seq, send_row, recv_row,
+):
     me_seq, me_dp = lax.axis_index("seq"), lax.axis_index("dp")
     greet(seq, dp, me_seq, me_dp)
     copies = []
@@ -127,10 +131,12 @@
         target = lax.rem(me_seq + step, seq)
         copies.append(
             pltpu.make_async_remote_copy(
-                terms.at[target], over_seq.at[step], send.at[step], recv.at[step], (target, me_dp), MESH
+                terms.at[target], over_seq.at[step], send_seq.at[step], recv_seq.at[step], (target, me_dp), MESH
             )
         )
         copies[-1].start()
+    large = start_trade(seq, me_seq, me_dp, pieces, swapped, own.at[0], send, recv)
+    large += start_trade(seq, me_seq, me_dp, pieces_two, swapped_two, own.at[1], send_two, recv_two)
     value = terms[me_seq]
     for step, copy in enumerate(copies):
         copy.wait()
@@ -150,26 +156,33 @@
         copy.wait()
         value = value + over_dp[step + 1]
     total[...] = value
-
-
-def closing(seq, dp, terms):
+    for copy in large:
+        copy.wait()
+
+
+def closing(seq, dp, terms, pieces, pieces_two):
     tile = terms.shape[2:]
-    inside = pl.BlockSpec(memory_space=pltpu.VMEM)
+    inside, anywhere = pl.BlockSpec(memory_space=pltpu.VMEM), pl.BlockSpec(memory_space=pl.ANY)
     return pl.pallas_call(
         functools.partial(closing_kernel, seq, dp),
-        out_shape=jax.ShapeDtypeStruct(tile, F32),
-        in_specs=[inside],
-        out_specs=inside,
+        out_shape=(
+            jax.ShapeDtypeStruct(tile, F32),
+            jax.ShapeDtypeStruct(pieces.shape, pieces.dtype),
+            jax.ShapeDtypeStruct(pieces_two.shape, pieces_two.dtype),
+        ),
+        in_specs=[inside, anywhere, anywhere],
+        out_specs=(inside, anywhere, anywhere),
         scratch_shapes=[
             pltpu.VMEM(terms.shape, F32),
             pltpu.VMEM(terms.shape[1:], F32),
             pltpu.VMEM(terms.shape[1:], F32),
+            pltpu.SemaphoreType.DMA((2,)),
         ]
-        + [pltpu.SemaphoreType.DMA((seq,))] * 2
+        + [pltpu.SemaphoreType.DMA((seq,))] * 6
         + [pltpu.SemaphoreType.DMA((dp,))] * 2,
         compiler_params=pltpu.CompilerParams(collective_id=2, has_side_effects=True),
         name="closing",
-    )(terms)
+    )(terms, pieces, pieces_two)
 
 
 def head_parts(ref, where, part, size):
@@ -214,6 +227,7 @@
         ],
         out_specs=pl.BlockSpec((seq, 1, block, size), lambda slot, head: (0, slot, 0, head)),
         compiler_params=pltpu.CompilerParams(vmem_limit_bytes=48 << 20),
+        cost_estimate=pl.CostEstimate(flops=0, bytes_accessed=slots * (30 << 20), transcendentals=0),
         name="attend",
     )(where, joint)
 
@@ -264,26 +278,136 @@
         out_specs=wide,
         scratch_shapes=[pltpu.VMEM((seq * block, size), F32)] * 2,
         compiler_params=pltpu.CompilerParams(vmem_limit_bytes=48 << 20),
+        cost_estimate=pl.CostEstimate(flops=0, bytes_accessed=slots * (45 << 20), transcendentals=0),
         name="attend_back",
     )(where, joint, flow)
 
 
-def swap_over_seq(pieces, count):
-    me = lax.axis_index("seq")
-    result = jnp.zeros_like(pieces)
-    own = lax.dynamic_index_in_dim(pieces, me, 0, keepdims=True)
-    result = lax.dynamic_update_index_in_dim(result, own, me, 0)
-    for step in range(1, count):
-        if count & (count - 1) == 0:
-            target, source = me ^ step, me ^ step
-            pairs = [(i, i ^ step) for i in range(count)]
-        else:
-            target, source = (me + step) % count, (me - step) % count
-            pairs = [(i, (i + step) % count) for i in range(count)]
-        sent = lax.dynamic_index_in_dim(pieces, target, 0, keepdims=True)
-        got = lax.ppermute(sent, "seq", pairs)
-        result = lax.dynamic_update_index_in_dim(result, got, source, 0)
-    return result
+def partner(me, step, count):
+    if count & (count - 1):
+        return lax.rem(me + step, count), lax.rem(me + count - step, count)
+    bit = 1
+    while bit < count:
+        if step & bit:
+            me = me + bit * (1 - 2 * lax.rem(me // bit, 2))
+        bit *= 2
+    return me, me
+
+
+def forward_back_kernel(
+    seq, chunk, mine, upstream, up, down, normed_all, hidden, expanded_back, result, flow_all,
+    normed, flow, load, store, send, recv, send_flow, recv_flow, keep,
+):
+    model, width = up.shape
+    pull = math.sqrt(2.0 / math.pi)
+    me_seq, me_dp = lax.axis_index("seq"), lax.axis_index("dp")
+    here = pl.program_id(0)
+    out, back = {}, {}
+    for step in range(1, seq):
+        target, origin = partner(me_seq, step, seq)
+        out[step] = pltpu.make_async_remote_copy(
+            normed.at[0], normed.at[step], send.at[step], recv.at[step], (target, me_dp), MESH
+        )
+        back[step] = pltpu.make_async_remote_copy(
+            flow.at[step], flow_all.at[step], send_flow.at[step], recv_flow.at[step], (origin, me_dp), MESH
+        )
+    stores = [pltpu.make_async_copy(normed.at[step], normed_all.at[step], store.at[step]) for step in range(seq)]
+    own = pltpu.make_async_copy(flow.at[0], flow_all.at[0], keep)
+    early = [step for step in range(1, seq) if step & (step - 1) == 0]
+    late = [step for step in range(1, seq) if step & (step - 1)]
+
+    @pl.when(here == 0)
+    def _():
+        fetch = pltpu.make_async_copy(mine, normed.at[0], load)
+        fetch.start()
+        barrier = pltpu.get_barrier_semaphore()
+        for step in range(1, seq):
+            pl.semaphore_signal(barrier, inc=1, device_id=(lax.rem(me_seq + step, seq), me_dp), device_id_type=MESH)
+        fetch.wait()
+        pl.semaphore_wait(barrier, seq - 1)
+        for step in early:
+            out[step].start()
+
+    for step in range(1, seq):
+
+        @pl.when(here == step)
+        def _(step=step):
+            out[step].wait()
+            if step == 1:
+                for other in late:
+                    out[other].start()
+
+    def inner(step, carry):
+        columns = pl.ds(pl.multiple_of(step * chunk, chunk), chunk)
+        expanded = product(normed[here], up[:, columns])
+        pulled = cols_product(upstream[0], down[columns, :])
+        square = expanded * expanded
+        bend = jnp.tanh(pull * (expanded + 0.044715 * (square * expanded)))
+        half = 0.5 * (1.0 + bend)
+        hidden[0, :, columns] = (expanded * half).astype(BF)
+        slope = half + (0.5 * pull) * expanded * (1.0 - bend * bend) * (1.0 + 0.134145 * square)
+        expanded_back[0, :, columns] = (pulled * slope).astype(BF)
+        return carry
+
+    lax.fori_loop(0, width // chunk, inner, 0)
+
+    def outer(step, carry):
+        columns = pl.ds(pl.multiple_of(step * chunk, chunk), chunk)
+        flow[here, :, columns] = cols_product(expanded_back[0], up[columns, :]).astype(BF)
+        return carry
+
+    lax.fori_loop(0, model // chunk, outer, 0)
+    for step in range(seq):
+
+        @pl.when(here == step)
+        def _(step=step):
+            stores[step].start()
+            if step == 0:
+                own.start()
+            else:
+                back[step].start()
+
+    def last(step, carry):
+        columns = pl.ds(pl.multiple_of(step * chunk, chunk), chunk)
+        result[0, :, columns] = product(hidden[0], down[:, columns]).astype(BF)
+        return carry
+
+    lax.fori_loop(0, model // chunk, last, 0)
+
+    @pl.when(here == seq - 1)
+    def _():
+        for copy in stores + [own] + list(back.values()):
+            copy.wait()
+
+
+def forward_back(mine, upstream, up, down):
+    seq, rows, model = upstream.shape
+    width = up.shape[1]
+    anywhere = pl.BlockSpec(memory_space=pl.ANY)
+    by_step = lambda columns: pl.BlockSpec((1, rows, columns), lambda step: (step, 0, 0))
+    whole = lambda shape: pl.BlockSpec(shape, lambda step: (0, 0), pipeline_mode=pl.Buffered(1))
+    shape = lambda columns: jax.ShapeDtypeStruct((seq, rows, columns), BF)
+    return pl.pallas_call(
+        functools.partial(forward_back_kernel, seq, math.gcd(512, math.gcd(width, model))),
+        out_shape=[shape(model), shape(width), shape(width), shape(model), shape(model)],
+        grid=(seq,),
+        in_specs=[anywhere, by_step(model), whole(up.shape), whole(down.shape)],
+        out_specs=[anywhere, by_step(width), by_step(width), by_step(model), anywhere],
+        scratch_shapes=[
+            pltpu.VMEM((seq, rows, model), BF),
+            pltpu.VMEM((seq, rows, model), BF),
+            pltpu.SemaphoreType.DMA,
+        ]
+        + [pltpu.SemaphoreType.DMA((seq,))] * 5
+        + [pltpu.SemaphoreType.DMA],
+        compiler_params=pltpu.CompilerParams(
+            collective_id=3, has_side_effects=True, vmem_limit_bytes=58 << 20
+        ),
+        cost_estimate=pl.CostEstimate(
+            flops=8 * seq * rows * model * width, bytes_accessed=400 << 20, transcendentals=seq * rows * width
+        ),
+        name="forward_back",
+    )(mine, upstream, up, down)
 
 
 def make_layer(seq, dp):
@@ -293,15 +417,17 @@
         pairs = [(i, i ^ step if xor else (i + step) % seq) for i in range(seq)]
         return lax.ppermute(values, "seq", pairs)
 
-    def gather_seq(block):
+    def gather_seq(block, event=None):
         if seq != 4:
             return [block] + [shift(block, step) for step in range(1, seq)]
         half = block.shape[0] // 2
         near, far = shift(block, 1), shift(block, 2)
-        corner = [shift(near[:half], 2), shift(far[half:], 1)]
-        return [block, near, far, jnp.concatenate(corner)]
-
-    def scatter_seq(make):
+        halves = near[:half], far[half:]
+        if event is not None:
+            halves = after(halves, event)
+        return [block, near, far, jnp.concatenate([shift(halves[0], 2), shift(halves[1], 1)])]
+
+    def scatter_seq(make, event=None, begun=None):
         if seq != 4:
             sent = [shift(make(step).astype(BF), step if xor else seq - step).astype(F32) for step in range(1, seq)]
             return make(0) + sum(sent)
@@ -311,6 +437,10 @@
         near = lax.optimization_barrier(make(1).astype(BF))
         far = lax.optimization_barrier(make(2).astype(BF))
         near_first, far_last = shift(near[:half], 1), shift(far[half:], 2)
+        if event is not None:
+            by_near, by_far = after((by_near, by_far), event)
+        if begun is not None:
+            begun.extend([by_near, by_far])
         near_last = shift((near[half:].astype(F32) + by_far.astype(F32)).astype(BF), 1)
         far_first = shift((far[:half].astype(F32) + by_near.astype(F32)).astype(BF), 2)
         first = near_first.astype(F32) + far_first.astype(F32)
@@ -325,13 +455,16 @@
     def gather_columns(swapped):
         return lax.all_gather(swapped, "dp", axis=1, tiled=True).reshape(-1, swapped.shape[2])
 
-    def scatter_columns(term, thirds, groups):
+    def scatter_columns(term):
         total, width = term.shape
         rows = total // (seq * dp)
         summed = lax.psum_scatter(
             term.astype(BF).reshape(seq, dp * rows, width), "dp", scatter_dimension=1, tiled=True
         )
-        swapped = swap_over_seq(summed, seq)
+        return summed
+
+    def column_rows(swapped, thirds, groups):
+        _, rows, width = swapped.shape
         shaped = swapped.reshape(seq, rows, groups, thirds, -1).transpose(1, 3, 0, 2, 4)
         return shaped.reshape(rows, seq * width).astype(F32)
 
@@ -342,9 +475,9 @@
         inputs, counts, cotangent, stretch, offset, inward, outward, dilation, translation, upward, downward
     ):
         slots, block, model = inputs.shape
-        head_size = model // HEADS
+        size = model // HEADS
         heads = HEADS // seq
-        scaling = 1.0 / math.sqrt(head_size)
+        scaling = 1.0 / math.sqrt(size)
         local_rows = slots * block
         total = seq * local_rows
         live = jnp.repeat((jnp.arange(slots) < counts[0]).astype(F32), block)[:, None]
@@ -352,18 +485,15 @@
         small = jnp.stack([stretch, offset, dilation, translation]).astype(F32).reshape(-1)
         taken = small.shape[0]
         small = jnp.pad(small, (0, -taken % 1024)).reshape(-1, 128)
-        swapped_in, small = opening(seq, dp, column_pieces(inward, 3, heads), small)
+        swapped_in, swapped_up, small = opening(
+            seq, dp, column_pieces(inward, 3, heads), column_pieces(upward, 1, 1), small
+        )
         small = small.reshape(dp, seq, -1)[:, :, :taken].reshape(dp, seq, 4, -1).transpose(2, 1, 0, 3).reshape(4, model)
         gain_one, shift_one, gain_two, shift_two = small[0], small[1], small[2], small[3]
         matrix_in = gather_columns(swapped_in)
         blocks = gather_seq(after(residual, swapped_in))
-        matrix_out = lax.all_gather(after(outward, matrix_in), "dp", axis=0, tiled=True)
-        swapped_up = swap_over_seq(after(column_pieces(upward, 1, 1), blocks[-1]), seq)
-        matrix_up = gather_columns(swapped_up)
-        matrix_down = lax.all_gather(after(downward, matrix_up), "dp", axis=0, tiled=True)
+        matrix_out = lax.all_gather(after(outward, (matrix_in, blocks[-1])), "dp", axis=0, tiled=True)
         upstream = (cotangent.astype(F32).reshape(local_rows, model) * live).astype(BF)
-        upstream_all = jnp.concatenate(gather_seq(after(upstream, swapped_up)))
-
         def piece(values, step):
             return values[step * local_rows : (step + 1) * local_rows]
 
@@ -373,43 +503,56 @@
         normed = [norm_one(part) for part in blocks]
         projected = jnp.concatenate([product(part, matrix_in).astype(BF) for part in normed])
         normed = jnp.concatenate(normed)
-
+        upstream_all = gather_seq(after(upstream, blocks[-1]), projected)
+        matrix_up = gather_columns(after(swapped_up, (matrix_out, projected, upstream_all[1], upstream_all[2])))
         me = lax.axis_index("seq")
         where = me ^ jnp.arange(seq) if xor else (me + seq - jnp.arange(seq)) % seq
         joint = projected.reshape(seq, slots, block, -1)
-        attended = attend(where, joint, head_size, scaling).reshape(total, heads * head_size)
-        middle = residual.astype(F32) + scatter_seq(lambda step: product(piece(attended, step), matrix_out))
+        attended = attend(where, joint, size, scaling).reshape(total, heads * size)
+        attended = after(attended, upstream_all)
+        begun = []
+        middle = residual.astype(F32) + scatter_seq(
+            lambda step: product(piece(attended, step), matrix_out), None, begun
+        )
+        matrix_down = lax.all_gather(after(downward, (matrix_up, begun)), "dp", axis=0, tiled=True)
         unit_two, root_two = norm_parts(middle)
-        normed_two = gather_seq((unit_two * gain_two + shift_two).astype(BF))
-        expanded = [product(part, matrix_up) for part in normed_two]
-        normed_two = jnp.concatenate(normed_two)
-        hidden = [smooth_gate(part).astype(BF) for part in expanded]
-        def gate_back(step):
-            flow = cols_product(piece(upstream_all, step), matrix_down)
-            return jax.vjp(smooth_gate, expanded[step])[1](flow)[0].astype(BF)
-
-        expanded_back = [gate_back(step) for step in range(seq)]
-        two_back = scatter_seq(lambda step: cols_product(expanded_back[step], matrix_up))
-        expanded_back = jnp.concatenate(expanded_back)
-        downward_delta = scatter_rows(rows_product(jnp.concatenate(hidden), upstream_all))
-        upward_delta = scatter_columns(rows_product(normed_two, expanded_back), 1, 1)
+        mine = (unit_two * gain_two + shift_two).astype(BF)
+        upstream_all = jnp.stack(upstream_all)
+        normed_two, hidden, expanded_back, down_terms, two_terms = forward_back(mine, upstream_all, matrix_up, matrix_down)
+
+        def flat(values):
+            return values.reshape(-1, values.shape[-1])
+
+        down_sum = rows_product(flat(hidden), flat(upstream_all))
+        two_back = jnp.sum(two_terms.astype(F32), axis=0)
+        downward_delta = scatter_rows(down_sum)
         middle_flow, dilation_term, translation_term = norm_back(two_back, unit_two, root_two, gain_two)
         middle_back = upstream.astype(F32) + middle_flow
-        middle_low = gather_seq(middle_back.astype(BF))
+        near_flow = middle_back.astype(BF)
+        middle_low = gather_seq(near_flow)
+        up_sum = rows_product(after(flat(normed_two), (down_sum, middle_low[1:3])), flat(expanded_back))
+        summed_up = scatter_columns(up_sum)
         heads_back = jnp.concatenate([cols_product(part, matrix_out).astype(BF) for part in middle_low])
-        result = middle + scatter_seq(lambda step: product(after(hidden[step], middle_low[-1]), matrix_down))
+        outward_delta = scatter_rows(rows_product(attended, jnp.concatenate(middle_low)))
+        heads_back = after(heads_back, (downward_delta, up_sum)).reshape(seq, slots, block, -1)
+        projected_back = attend_back(where, joint, heads_back, size, scaling).reshape(total, -1)
+        corner = cols_product(piece(projected_back, seq - 1), matrix_in).astype(BF)
+        in_sum = rows_product(after(normed, (summed_up, corner)), projected_back)
+        summed_in = scatter_columns(in_sum)
+        one_terms = [cols_product(piece(projected_back, step), matrix_in) for step in range(seq - 1)]
+        one_terms = [one_terms[0]] + lax.optimization_barrier([part.astype(BF) for part in one_terms[1:]]) + [corner]
+        late_terms = after(down_terms, middle_low[-1])
+        result = middle + scatter_seq(lambda step: late_terms[step].astype(F32), one_terms[1:])
         outputs = (result * live).astype(BF).reshape(slots, block, model)
-        outward_delta = scatter_rows(rows_product(attended, jnp.concatenate(middle_low)))
-        heads_back = after(heads_back, downward_delta).reshape(seq, slots, block, -1)
-        projected_back = attend_back(where, joint, heads_back, head_size, scaling).reshape(total, -1)
-        inward_delta = scatter_columns(rows_product(normed, projected_back), 3, heads)
-        one_back = scatter_seq(lambda step: cols_product(piece(projected_back, step), matrix_in))
+        one_back = scatter_seq(lambda step: one_terms[step], in_sum)
         unit_one, root_one = norm_parts(residual.astype(F32))
         input_flow, stretch_term, offset_term = norm_back(one_back, unit_one, root_one, gain_one)
         terms = jnp.stack([stretch_term, offset_term, dilation_term, translation_term])
         terms = terms.reshape(4, seq, dp, -1).transpose(1, 2, 0, 3).reshape(seq, dp, -1)
         terms = jnp.pad(terms, ((0, 0), (0, 0), (0, -taken % 1024))).reshape(seq, dp, -1, 128)
-        deltas = closing(seq, dp, terms).reshape(-1)[:taken].reshape(4, -1)
+        deltas, swapped_in, swapped_up = closing(seq, dp, terms, summed_in, summed_up)
+        inward_delta, upward_delta = column_rows(swapped_in, 3, heads), column_rows(swapped_up, 1, 1)
+        deltas = deltas.reshape(-1)[:taken].reshape(4, -1)
         input_delta = (middle_back + input_flow).reshape(slots, block, model)
         return (
             outputs,

time: 1050 us -> 961 us (0.915)
  Pallas kernels: 76.6 us -> 301 us
  waiting for transfers between devices: 457 us -> 309 us
  matrix products: 261 us -> 135 us
  local copies, waits for them, and re-layouts: 104 us -> 64.4 us
  other arithmetic: 63.4 us -> 82.5 us
  starting transfers between devices: 57.4 us -> 43.2 us
    pallas_call x1 -> x2, Pallas kernels: 10.7 us -> 224 us  [the longest x1 196 us: forward_back(): pl.pallas_call(functools.partial(forward_back_kernel, seq, math.gcd(512,...]
    ppermute x40 -> x30, waiting for transfers between devices: 373 us -> 269 us  [shift(): return lax.ppermute(values, 'seq', pairs)]
    dot_general x16 -> x8, matrix products: 106 us -> 24.2 us  [product(): return jnp.dot(left, right, preferred_element_type=F32)]
    dot_general x16 -> x8, matrix products: 90 us -> 41.2 us  [cols_product(): lax.dot_general(left, right, (((1,), (1,)), ((), ())), preferred_element_...]
    dynamic_update_slice x11 -> x0, local copies, waits for them, and re-layouts: 32.4 us -> none  [the longest x9 24.4 us: swap_over_seq(): result = lax.dynamic_update_index_in_dim(result, got, source, 0)]
    all_gather x2, waiting for transfers between devices: 55.3 us -> 26.1 us  [gather_columns(): lax.all_gather(swapped, 'dp', axis=1, tiled=True)]
    ppermute x9 -> x0, waiting for transfers between devices: 28.6 us -> none  [swap_over_seq(): got = lax.ppermute(sent, 'seq', pairs)]
    ppermute x40 -> x30, starting transfers between devices: 46.2 us -> 31.7 us  [shift(): return lax.ppermute(values, 'seq', pairs)]
  transfers between devices with their start and end apart: 57 -> 38, of which waited for: 27 -> 24; matrix products, arithmetic and copies ran while one was open for 32% -> 24% of each run, Pallas kernels for 6% -> 5%
where the time goes in v3:
time: 961 us; the launch traced here: 952 us
  waiting for transfers between devices  309 us (32%)
  Pallas kernels  301 us (31%)
  matrix products  135 us (14%)
  other arithmetic  82.5 us (9%)
  local copies, waits for them, and re-layouts  64.4 us (7%)
  starting transfers between devices  43.2 us (4%)
  between operations  16.4 us (2%)
    ppermute x30, waiting for transfers between devices, shift(): return lax.ppermute(values, 'seq', pairs)  269 us
    pallas_call x1, Pallas kernels, forward_back(): pl.pallas_call(functools.partial(forward_back_kernel, seq, math.gcd(512,...  196 us
    dot_general x4, matrix products, rows_product(): lax.dot_general(left, right, (((0,), (0,)), ((), ())), preferred_element_...  70 us
    dot_general x8, matrix products, cols_product(): lax.dot_general(left, right, (((1,), (1,)), ((), ())), preferred_element_...  41.2 us
    ppermute x30, starting transfers between devices, shift(): return lax.ppermute(values, 'seq', pairs)  31.7 us
    pallas_call x1, Pallas kernels, attend_back(): pl.pallas_call(functools.partial(attend_back_kernel, scaling), out_shape=...  29.1 us
    pallas_call x1, Pallas kernels, closing(): pl.pallas_call(functools.partial(closing_kernel, seq, dp), out_shape=(jax...  28.4 us
    pallas_call x1, Pallas kernels, opening(): pl.pallas_call(functools.partial(opening_kernel, seq, dp), out_shape=(jax...  28.2 us
  transfers between devices with their start and end apart: 38, of which 24 were waited for; matrix products, arithmetic and copies ran while one was open for 24% of the time, Pallas kernels for 5%

profile of v3, /device:TPU:0, one launch (start us, length us, event | category | flops | bytes accessed | tf_op | source)
XLA Modules:
  0.0 952.1 jit_solution(14252868834297231957)
XLA Ops:
  15.7 28.2 %opening.1 = (bf16[4,64,1536]{2,1,0:T(8,128)(2,1)}, bf16[4,64,2048]{2,1,0:T(8,128)(2,1)}, f32[8,4,8,128]{3,2,1,0:T(8,128)}) custom-call(bf16[4,64,1536]{2,1,0:T(8,128)(2,1)} %reshape.255.pieces, bf16[4,64,2048]{2,1,0:T(8,128)(2,1)} %bitcast.153, f32[8,128]{1,0:T(8,128)} %bitcast_convert_fusion.small), custom_call_target="tpu_custom_call" | custom-call | tf_op jit(solution)/shard_map/opening/pallas_call | solution.py:106
  51.3 40.1 %collective-permute-done = bf16[512,2048]{1,0:T(8,128)(2,1)} collective-permute-done((bf16[512,2048]{1,0:T(8,128)(2,1)S(1)}, bf16[512,2048]{1,0:T(8,128)(2,1)}, u32[]{:S(2)}, u32[]{:S(2)}) %collective-permute-start) | collective-permute-done | bytes 2097184 | tf_op jit(solution)/shard_map/ppermute | solution.py:418
  104.6 12.0 %collective-permute-done.2 = bf16[256,2048]{1,0:T(8,128)(2,1)S(1)} collective-permute-done((bf16[256,2048]{1,0:T(8,128)(2,1)S(1)}, bf16[256,2048]{1,0:T(8,128)(2,1)S(1)}, u32[]{:S(2)}, u32[]{:S(2)}) %collective-permute-start.2) | collective-permute-done | bytes 1048608 | tf_op jit(solution)/shard_map/ppermute | solution.py:418
  150.1 14.6 %collective-permute-done.4 = bf16[512,2048]{1,0:T(8,128)(2,1)} collective-permute-done((bf16[512,2048]{1,0:T(8,128)(2,1)}, bf16[512,2048]{1,0:T(8,128)(2,1)}, u32[]{:S(2)}, u32[]{:S(2)}) %collective-permute-start.4) | collective-permute-done | bytes 2097184 | tf_op jit(solution)/shard_map/ppermute | solution.py:418
  170.8 19.7 %attend.1 = bf16[4,2,256,512]{3,2,1,0:T(8,128)(2,1)S(1)} custom-call(s32[4]{0:T(128)S(1)} %iota_xor_fusion.where, bf16[4,2,256,1536]{3,2,1,0:T(8,128)(2,1)} %bitcast.145), custom_call_target="tpu_custom_call" | custom-call | bytes 62914560 | tf_op jit(solution)/shard_map/attend/pallas_call | solution.py:220
  199.7 18.8 %collective-permute-done.11 = bf16[256,2048]{1,0:T(8,128)(2,1)S(1)} collective-permute-done((bf16[256,2048]{1,0:T(8,128)(2,1)S(1)}, bf16[256,2048]{1,0:T(8,128)(2,1)S(1)}, u32[]{:S(2)}, u32[]{:S(2)}) %collective-permute-start.11) | collective-permute-done | bytes 1048608 | tf_op jit(solution)/shard_map/ppermute | solution.py:418
  219.7 26.1 %all-gather.9.cloned.1.call-done = bf16[4,512,2048]{2,1,0:T(8,128)(2,1)} async-done(((bf16[4,64,2048]{2,1,0:T(8,128)(2,1)}), bf16[4,512,2048]{2,1,0:T(8,128)(2,1)}) %all-gather.9.cloned.1.call-update) | async-done | bytes 8388624 | tf_op jit(solution)/shard_map/all_gather | solution.py:456
  245.9 10.4 %reduce-scatter.5.cloned.1.call-start = ((), (), s32[]{:S(2)}) async-start(), calls=%async_computation.8 | async-start | bytes 9437184 | tf_op jit(solution)/shard_map/reduce_scatter | solution.py:472
  274.4 12.5 %collective-permute-done.8 = bf16[256,2048]{1,0:T(8,128)(2,1)S(1)} collective-permute-done((bf16[256,2048]{1,0:T(8,128)(2,1)S(1)}, bf16[256,2048]{1,0:T(8,128)(2,1)S(1)}, u32[]{:S(2)}, u32[]{:S(2)}) %collective-permute-start.8) | collective-permute-done | bytes 1048608 | tf_op jit(solution)/shard_map/ppermute | solution.py:418
  286.8 23.1 %collective-permute-done.10 = bf16[256,2048]{1,0:T(8,128)(2,1)S(1)} collective-permute-done((bf16[256,2048]{1,0:T(8,128)(2,1)S(1)}, bf16[256,2048]{1,0:T(8,128)(2,1)S(1)}, u32[]{:S(2)}, u32[]{:S(2)}) %collective-permute-start.10) | collective-permute-done | bytes 1048608 | tf_op jit(solution)/shard_map/ppermute | solution.py:418
  316.2 11.7 %all-gather.11.cloned.1.call-done.down = bf16[2048,2048]{1,0:T(8,128)(2,1)} async-done(((bf16[256,2048]{1,0:T(8,128)(2,1)}), bf16[2048,2048]{1,0:T(8,128)(2,1)}) %all-gather.11.cloned.1.call-update) | async-done | bytes 8388624 | tf_op jit(solution)/shard_map/all_gather | solution.py:517
  327.9 195.6 %forward_back.1 = (bf16[4,512,2048]{2,1,0:T(8,128)(2,1)}, bf16[4,512,2048]{2,1,0:T(8,128)(2,1)}, bf16[4,512,2048]{2,1,0:T(8,128)(2,1)}, bf16[4,512,2048]{2,1,0:T(8,128)(2,1)}, bf16[4,512,2048]{2,1,0:T(8,128)(2,1)}) custom-call(bf16[512,2048]{1,0:T(8,128)(2,1)} %add_convert_fusion.mine, bf16[4,512,2048]{2,1,0:T(8,128)(2,1)} %pad_maximum_fusion.upstream, ...), custom_call_target="tpu_custom_call" | custom-call | flops 68719476736 | bytes 419430400 | tf_op jit(solution)/shard_map/forward_back/pallas_call | solution.py:390
  523.5 24.2 %convolution_bitcast_fusion = bf16[2048,2048]{1,0:T(8,128)(2,1)} fusion(bf16[4,512,2048]{2,1,0:T(8,128)(2,1)} %get-tuple-element.53, bf16[1,512,2048]{2,1,0:T(8,128)(2,1)} %bitcast.18, bf16[1,512,2048]{2,1,0:T(8,128)(2,1)} %bitcast.17, bf16[1,512,2048]{2,1,0:T(8,128)(2,1)} %bitcast.16, bf16[1,512,2048]{2,1,0:T(8,128)(2,1)} %bitcast.15), kind=kOutput, calls=%fused_computation.2 | convolution fusion | flops 17192452096 | bytes 25165824 | tf_op jit(solution)/shard_map/dot_general | solution.py:34
  564.9 44.9 %collective-permute-done.14 = bf16[512,2048]{1,0:T(8,128)(2,1)} collective-permute-done((bf16[512,2048]{1,0:T(8,128)(2,1)S(1)}, bf16[512,2048]{1,0:T(8,128)(2,1)}, u32[]{:S(2)}, u32[]{:S(2)}) %collective-permute-start.14) | collective-permute-done | bytes 2097184 | tf_op jit(solution)/shard_map/ppermute | solution.py:418
  611.1 20.7 %fusion.48 = bf16[2048,2048]{1,0:T(8,128)(2,1)} fusion(bf16[2048,2048]{1,0:T(8,128)(2,1)S(1)} %bitcast.185, bf16[2048,2048]{1,0:T(8,128)(2,1)S(1)} %bitcast.188), kind=kOutput, calls=%fused_computation.156 | convolution fusion | flops 17179869184 | bytes 25165824 | tf_op jit(solution)/shard_map/dot_general | solution.py:34
  682.1 29.1 %attend_back.1 = bf16[4,2,256,1536]{3,2,1,0:T(8,128)(2,1)} custom-call(s32[4]{0:T(128)S(1)} %copy-done.3, bf16[4,2,256,1536]{3,2,1,0:T(8,128)(2,1)} %bitcast.146, bf16[4,2,256,512]{3,2,1,0:T(8,128)(2,1)S(1)} %bitcast.133), custom_call_target="tpu_custom_call" | custom-call | bytes 94371840 | tf_op jit(solution)/shard_map/attend_back/pallas_call | solution.py:269
  725.2 19.4 %fusion.49 = bf16[2048,1536]{1,0:T(8,128)(2,1)} fusion(bf16[2048,2048]{1,0:T(8,128)(2,1)} %pad_maximum_fusion.1, bf16[2048,1536]{1,0:T(8,128)(2,1)} %bitcast.147), kind=kOutput, calls=%fused_computation.157 | convolution fusion | flops 12884901888 | bytes 20971520 | tf_op jit(solution)/shard_map/dot_general | solution.py:34
  784.5 15.1 %collective-permute-done.18 = bf16[256,2048]{1,0:T(8,128)(2,1)} collective-permute-done((bf16[256,2048]{1,0:T(8,128)(2,1)}, bf16[256,2048]{1,0:T(8,128)(2,1)}, u32[]{:S(2)}, u32[]{:S(2)}) %collective-permute-start.18) | collective-permute-done | bytes 1048608 | tf_op jit(solution)/shard_map/ppermute | solution.py:418
  801.0 22.4 %collective-permute-done.21 = bf16[256,2048]{1,0:T(8,128)(2,1)S(1)} collective-permute-done((bf16[256,2048]{1,0:T(8,128)(2,1)S(1)}, bf16[256,2048]{1,0:T(8,128)(2,1)S(1)}, u32[]{:S(2)}, u32[]{:S(2)}) %collective-permute-start.21) | collective-permute-done | bytes 1048608 | tf_op jit(solution)/shard_map/ppermute | solution.py:418
  828.7 15.7 %collective-permute-done.25 = bf16[256,2048]{1,0:T(8,128)(2,1)S(1)} collective-permute-done((bf16[256,2048]{1,0:T(8,128)(2,1)S(1)}, bf16[256,2048]{1,0:T(8,128)(2,1)S(1)}, u32[]{:S(2)}, u32[]{:S(2)}) %collective-permute-start.25) | collective-permute-done | bytes 1048608 | tf_op jit(solution)/shard_map/ppermute | solution.py:418
  853.2 13.7 %collective-permute-done.24 = bf16[256,2048]{1,0:T(8,128)(2,1)S(1)} collective-permute-done((bf16[256,2048]{1,0:T(8,128)(2,1)S(1)}, bf16[256,2048]{1,0:T(8,128)(2,1)S(1)}, u32[]{:S(2)}, u32[]{:S(2)}) %collective-permute-start.24) | collective-permute-done | bytes 1048608 | tf_op jit(solution)/shard_map/ppermute | solution.py:418
  866.8 20.3 %collective-permute-done.27 = bf16[256,2048]{1,0:T(8,128)(2,1)S(1)} collective-permute-done((bf16[256,2048]{1,0:T(8,128)(2,1)S(1)}, bf16[256,2048]{1,0:T(8,128)(2,1)S(1)}, u32[]{:S(2)}, u32[]{:S(2)}) %collective-permute-start.27) | collective-permute-done | bytes 1048608 | tf_op jit(solution)/shard_map/ppermute | solution.py:418
  887.9 9.0 fusion.32
  903.8 28.4 %closing.1 = (f32[8,128]{1,0:T(8,128)}, bf16[4,64,1536]{2,1,0:T(8,128)(2,1)}, bf16[4,64,2048]{2,1,0:T(8,128)(2,1)}) custom-call(f32[4,8,8,128]{3,2,1,0:T(8,128)} %copy.46, bf16[4,64,1536]{2,1,0:T(8,128)(2,1)} %reduce-scatter.9.cloned.1.call-done.pieces, bf16[4,64,2048]{2,1,0:T(8,128)(2,1)} %reduce-scatter.7.cloned.1.call-done.pieces_two), custom_call_target="tpu_custom_call" | custom-call | tf_op jit(solution)/shard_map/closing/pallas_call | solution.py:166
  (297 shorter events, 260.0 us)
Async XLA Ops:
  7.2 122.2 %all-gather.5.cloned.1.call-start = ((), (), s32[]{:S(2)}) async-start(), calls=%async_computation.4 | async-start | bytes 7077888 | tf_op jit(solution)/shard_map/all_gather | solution.py:456
  43.9 121.1 %all-gather.7.cloned.1.call-start = ((), (), s32[]{:S(2)}) async-start(), calls=%async_computation.5 | async-start | bytes 2359296 | tf_op jit(solution)/shard_map/all_gather | solution.py:495
  44.0 47.4 %collective-permute-start = (bf16[512,2048]{1,0:T(8,128)(2,1)S(1)}, bf16[512,2048]{1,0:T(8,128)(2,1)}, u32[]{:S(2)}, u32[]{:S(2)}) collective-permute-start(bf16[512,2048]{1,0:T(8,128)(2,1)S(1)} %bitcast.139), channel_id=1, source_target_pairs={{0,8},{8,0},{16,24},{24,16},{1,9},{9,1},{17,25},{25,17},{2,10},{10... | collective-permute-start | bytes 6291464 | tf_op jit(solution)/shard_map/ppermute | solution.py:418
  45.5 48.7 %collective-permute-start.1 = (bf16[512,2048]{1,0:T(8,128)(2,1)S(1)}, bf16[512,2048]{1,0:T(8,128)(2,1)}, u32[]{:S(2)}, u32[]{:S(2)}) collective-permute-start(bf16[512,2048]{1,0:T(8,128)(2,1)S(1)} %bitcast.140), channel_id=1, source_target_pairs={{0,16},{8,24},{16,0},{24,8},{1,17},{9,25},{17,1},{25,9},{2,18},{10... | collective-permute-start | bytes 6291464 | tf_op jit(solution)/shard_map/ppermute | solution.py:418
  119.3 45.5 %collective-permute-start.4 = (bf16[512,2048]{1,0:T(8,128)(2,1)}, bf16[512,2048]{1,0:T(8,128)(2,1)}, u32[]{:S(2)}, u32[]{:S(2)}) collective-permute-start(bf16[512,2048]{1,0:T(8,128)(2,1)} %fusion.38), channel_id=1, source_target_pairs={{0,8},{8,0},{16,24},{24,16},{1,9},{9,1},{17,25},{25,17},{2,10},{10... | collective-permute-start | bytes 6291464 | tf_op jit(solution)/shard_map/ppermute | solution.py:418
  119.9 45.2 %collective-permute-start.5 = (bf16[512,2048]{1,0:T(8,128)(2,1)}, bf16[512,2048]{1,0:T(8,128)(2,1)}, u32[]{:S(2)}, u32[]{:S(2)}) collective-permute-start(bf16[512,2048]{1,0:T(8,128)(2,1)} %fusion.38), channel_id=1, source_target_pairs={{0,16},{8,24},{16,0},{24,8},{1,17},{9,25},{17,1},{25,9},{2,18},{10... | collective-permute-start | bytes 6291464 | tf_op jit(solution)/shard_map/ppermute | solution.py:418
  129.4 116.4 %all-gather.9.cloned.1.call-start = ((), (), s32[]{:S(2)}) async-start(), calls=%async_computation.6 | async-start | bytes 9437184 | tf_op jit(solution)/shard_map/all_gather | solution.py:456
  165.1 162.8 %all-gather.11.cloned.1.call-start = ((), (), s32[]{:S(2)}) async-start(), calls=%async_computation.7 | async-start | bytes 9437184 | tf_op jit(solution)/shard_map/all_gather | solution.py:517
  245.9 433.4 %reduce-scatter.5.cloned.1.call-start = ((), (), s32[]{:S(2)}) async-start(), calls=%async_computation.8 | async-start | bytes 9437184 | tf_op jit(solution)/shard_map/reduce_scatter | solution.py:472
  262.4 47.9 %collective-permute-start.13 = (bf16[256,2048]{1,0:T(8,128)(2,1)S(1)}, bf16[256,2048]{1,0:T(8,128)(2,1)S(1)}, u32[]{:S(2)}, u32[]{:S(2)}) collective-permute-start(bf16[256,2048]{1,0:T(8,128)(2,1)S(1)} %slice.224), channel_id=1, source_target_pairs={{0,16},{8,24},{16,0},{24,8},{1,17},{9,25},{17,1},{25,9},{2,18},{10... | collective-permute-start | bytes 3145736 | tf_op jit(solution)/shard_map/ppermute | solution.py:418
  265.5 44.4 %collective-permute-start.10 = (bf16[256,2048]{1,0:T(8,128)(2,1)S(1)}, bf16[256,2048]{1,0:T(8,128)(2,1)S(1)}, u32[]{:S(2)}, u32[]{:S(2)}) collective-permute-start(bf16[256,2048]{1,0:T(8,128)(2,1)S(1)} %add_convert_fusion.6), channel_id=1, source_target_pairs={{0,16},{8,24},{16,0},{24,8},{1,17},{9,25},{17,1},{25,9},{2,18},{10... | collective-permute-start | bytes 3145736 | tf_op jit(solution)/shard_map/ppermute | solution.py:418
  266.6 43.8 %collective-permute-start.12 = (bf16[256,2048]{1,0:T(8,128)(2,1)S(1)}, bf16[256,2048]{1,0:T(8,128)(2,1)S(1)}, u32[]{:S(2)}, u32[]{:S(2)}) collective-permute-start(bf16[256,2048]{1,0:T(8,128)(2,1)S(1)} %add_convert_fusion.5), channel_id=1, source_target_pairs={{0,8},{8,0},{16,24},{24,16},{1,9},{9,1},{17,25},{25,17},{2,10},{10... | collective-permute-start | bytes 3145736 | tf_op jit(solution)/shard_map/ppermute | solution.py:418
  547.7 177.5 %reduce-scatter.7.cloned.1.call-start = ((), (), s32[]{:S(2)}) async-start(), calls=%async_computation.9 | async-start | bytes 9437184 | tf_op jit(solution)/shard_map/reduce_scatter | solution.py:461
  563.5 46.3 %collective-permute-start.14 = (bf16[512,2048]{1,0:T(8,128)(2,1)S(1)}, bf16[512,2048]{1,0:T(8,128)(2,1)}, u32[]{:S(2)}, u32[]{:S(2)}) collective-permute-start(bf16[512,2048]{1,0:T(8,128)(2,1)S(1)} %get-tuple-element.82), channel_id=1, source_target_pairs={{0,8},{8,0},{16,24},{24,16},{1,9},{9,1},{17,25},{25,17},{2,10},{10... | collective-permute-start | bytes 6291464 | tf_op jit(solution)/shard_map/ppermute | solution.py:418
  564.8 46.3 %collective-permute-start.16 = (bf16[512,2048]{1,0:T(8,128)(2,1)S(1)}, bf16[512,2048]{1,0:T(8,128)(2,1)}, u32[]{:S(2)}, u32[]{:S(2)}) collective-permute-start(bf16[512,2048]{1,0:T(8,128)(2,1)S(1)} %get-tuple-element.82), channel_id=1, source_target_pairs={{0,16},{8,24},{16,0},{24,8},{1,17},{9,25},{17,1},{25,9},{2,18},{10... | collective-permute-start | bytes 6291464 | tf_op jit(solution)/shard_map/ppermute | solution.py:418
  631.8 130.0 %reduce-scatter.11.cloned.1.call-start = ((), (), s32[]{:S(2)}) async-start(), calls=%async_computation.11 | async-start | bytes 2359296 | tf_op jit(solution)/shard_map/reduce_scatter | solution.py:472
  675.9 227.9 %reduce-scatter.9.cloned.1.call-start = ((), (), s32[]{:S(2)}) async-start(), calls=%async_computation.10 | async-start | bytes 7077888 | tf_op jit(solution)/shard_map/reduce_scatter | solution.py:461
  760.4 65.1 %collective-permute-start.23 = (bf16[256,2048]{1,0:T(8,128)(2,1)}, bf16[256,2048]{1,0:T(8,128)(2,1)}, u32[]{:S(2)}, u32[]{:S(2)}) collective-permute-start(bf16[256,2048]{1,0:T(8,128)(2,1)} %slice.235), channel_id=1, source_target_pairs={{0,16},{8,24},{16,0},{24,8},{1,17},{9,25},{17,1},{25,9},{2,18},{10... | collective-permute-start | bytes 3145736 | tf_op jit(solution)/shard_map/ppermute | solution.py:418
  780.0 43.3 %collective-permute-start.21 = (bf16[256,2048]{1,0:T(8,128)(2,1)S(1)}, bf16[256,2048]{1,0:T(8,128)(2,1)S(1)}, u32[]{:S(2)}, u32[]{:S(2)}) collective-permute-start(bf16[256,2048]{1,0:T(8,128)(2,1)S(1)} %add_convert_fusion.4), channel_id=1, source_target_pairs={{0,16},{8,24},{16,0},{24,8},{1,17},{9,25},{17,1},{25,9},{2,18},{10... | collective-permute-start | bytes 3145736 | tf_op jit(solution)/shard_map/ppermute | solution.py:418
  782.0 45.1 %collective-permute-start.22 = (bf16[256,2048]{1,0:T(8,128)(2,1)S(1)}, bf16[256,2048]{1,0:T(8,128)(2,1)S(1)}, u32[]{:S(2)}, u32[]{:S(2)}) collective-permute-start(bf16[256,2048]{1,0:T(8,128)(2,1)S(1)} %add_convert_fusion.3), channel_id=1, source_target_pairs={{0,8},{8,0},{16,24},{24,16},{1,9},{9,1},{17,25},{25,17},{2,10},{10... | collective-permute-start | bytes 3145736 | tf_op jit(solution)/shard_map/ppermute | solution.py:418
  783.0 61.4 %collective-permute-start.25 = (bf16[256,2048]{1,0:T(8,128)(2,1)S(1)}, bf16[256,2048]{1,0:T(8,128)(2,1)S(1)}, u32[]{:S(2)}, u32[]{:S(2)}) collective-permute-start(bf16[256,2048]{1,0:T(8,128)(2,1)S(1)} %get-tuple-element.94), channel_id=1, source_target_pairs={{0,8},{8,0},{16,24},{24,16},{1,9},{9,1},{17,25},{25,17},{2,10},{10... | collective-permute-start | bytes 3145736 | tf_op jit(solution)/shard_map/ppermute | solution.py:418
  799.5 46.3 %collective-permute-start.26 = (bf16[256,2048]{1,0:T(8,128)(2,1)S(1)}, bf16[256,2048]{1,0:T(8,128)(2,1)S(1)}, u32[]{:S(2)}, u32[]{:S(2)}) collective-permute-start(bf16[256,2048]{1,0:T(8,128)(2,1)S(1)} %get-tuple-element.93), channel_id=1, source_target_pairs={{0,16},{8,24},{16,0},{24,8},{1,17},{9,25},{17,1},{25,9},{2,18},{10... | collective-permute-start | bytes 3145736 | tf_op jit(solution)/shard_map/ppermute | solution.py:418
  823.4 43.5 %collective-permute-start.24 = (bf16[256,2048]{1,0:T(8,128)(2,1)S(1)}, bf16[256,2048]{1,0:T(8,128)(2,1)S(1)}, u32[]{:S(2)}, u32[]{:S(2)}) collective-permute-start(bf16[256,2048]{1,0:T(8,128)(2,1)S(1)} %slice.237), channel_id=1, source_target_pairs={{0,8},{8,0},{16,24},{24,16},{1,9},{9,1},{17,25},{25,17},{2,10},{10... | collective-permute-start | bytes 3145736 | tf_op jit(solution)/shard_map/ppermute | solution.py:418
  825.5 62.0 %collective-permute-start.29 = (bf16[256,2048]{1,0:T(8,128)(2,1)S(1)}, bf16[256,2048]{1,0:T(8,128)(2,1)S(1)}, u32[]{:S(2)}, u32[]{:S(2)}) collective-permute-start(bf16[256,2048]{1,0:T(8,128)(2,1)S(1)} %slice.242), channel_id=1, source_target_pairs={{0,16},{8,24},{16,0},{24,8},{1,17},{9,25},{17,1},{25,9},{2,18},{10... | collective-permute-start | bytes 3145736 | tf_op jit(solution)/shard_map/ppermute | solution.py:418
  (60 other events, 1169.9 us)
Sparse Core Ops, SparseCore 0:
  44.1 63.1 all-gather.4
  129.5 27.2 all-gather.6
  165.2 80.6 all-gather.8
  247.3 80.5 all-gather.10
  547.9 87.1 reduce-scatter.4
  637.2 87.9 reduce-scatter.6
  727.5 34.1 reduce-scatter.10
  764.1 68.2 reduce-scatter.8

commit v4 on v3

--- a/solution.py
+++ b/solution.py
@@ -70,7 +70,8 @@
 
 
 def opening_kernel(
-    seq, dp, pieces, pieces_two, small, swapped, swapped_two, params, own, send, recv, send_two, recv_two, send_small, recv_small, send_row, recv_row
+    seq, dp, pieces, pieces_two, small, shard, swapped, swapped_two, params, shards,
+    own, send, recv, send_two, recv_two, send_small, recv_small, send_row, recv_row, send_shard, recv_shard, send_next, recv_next,
 ):
     me_seq, me_dp = lax.axis_index("seq"), lax.axis_index("dp")
     greet(seq, dp, me_seq, me_dp)
@@ -86,6 +87,18 @@
         )
         tiny[-1].start()
     large = start_trade(seq, me_seq, me_dp, pieces, swapped, own.at[1], send, recv)
+    span = 1 if dp % 2 else 2
+    keep_shard = pltpu.make_async_copy(shard, shards.at[me_dp], own.at[3])
+    keep_shard.start()
+    firsts = []
+    for step in range(1, dp // span):
+        target = lax.rem(me_dp + span * step, dp)
+        firsts.append(
+            pltpu.make_async_remote_copy(
+                shard, shards.at[me_dp], send_shard.at[step], recv_shard.at[step], (me_seq, target), MESH
+            )
+        )
+        firsts[-1].start()
     large += start_trade(seq, me_seq, me_dp, pieces_two, swapped_two, own.at[2], send_two, recv_two)
     for copy in [keep] + tiny:
         copy.wait()
@@ -97,11 +110,24 @@
             )
         )
         rows[-1].start()
+    keep_shard.wait()
+    for step in range(dp // span):
+        if step:
+            firsts[step - 1].wait()
+        if span == 2:
+            origin = lax.rem(me_dp + dp - span * step, dp)
+            sibling = me_dp + 1 - 2 * lax.rem(me_dp, 2)
+            rows.append(
+                pltpu.make_async_remote_copy(
+                    shards.at[origin], shards.at[origin], send_next.at[step], recv_next.at[step], (me_seq, sibling), MESH
+                )
+            )
+            rows[-1].start()
     for copy in rows + large:
         copy.wait()
 
 
-def opening(seq, dp, pieces, pieces_two, small):
+def opening(seq, dp, pieces, pieces_two, small, shard):
     anywhere = pl.BlockSpec(memory_space=pl.ANY)
     return pl.pallas_call(
         functools.partial(opening_kernel, seq, dp),
@@ -109,20 +135,21 @@
             jax.ShapeDtypeStruct(pieces.shape, pieces.dtype),
             jax.ShapeDtypeStruct(pieces_two.shape, pieces_two.dtype),
             jax.ShapeDtypeStruct((dp, seq) + small.shape, small.dtype),
+            jax.ShapeDtypeStruct((dp,) + shard.shape, shard.dtype),
         ),
-        in_specs=[anywhere] * 3,
-        out_specs=(anywhere,) * 3,
-        scratch_shapes=[pltpu.SemaphoreType.DMA((3,))]
+        in_specs=[anywhere] * 4,
+        out_specs=(anywhere,) * 4,
+        scratch_shapes=[pltpu.SemaphoreType.DMA((4,))]
         + [pltpu.SemaphoreType.DMA((seq,))] * 6
-        + [pltpu.SemaphoreType.DMA((dp,))] * 2,
+        + [pltpu.SemaphoreType.DMA((dp,))] * 6,
         compiler_params=pltpu.CompilerParams(collective_id=1, has_side_effects=True),
         name="opening",
-    )(pieces, pieces_two, small)
+    )(pieces, pieces_two, small, shard)
 
 
 def closing_kernel(
-    seq, dp, terms, pieces, pieces_two, total, swapped, swapped_two, over_seq, partial, over_dp,
-    own, send, recv, send_two, recv_two, send_seq, recv_seq, send_row, recv_row,
+    seq, dp, terms, pieces, total, swapped, over_seq, partial, over_dp,
+    own, send, recv, send_seq, recv_seq, send_row, recv_row,
 ):
     me_seq, me_dp = lax.axis_index("seq"), lax.axis_index("dp")
     greet(seq, dp, me_seq, me_dp)
@@ -135,8 +162,7 @@
             )
         )
         copies[-1].start()
-    large = start_trade(seq, me_seq, me_dp, pieces, swapped, own.at[0], send, recv)
-    large += start_trade(seq, me_seq, me_dp, pieces_two, swapped_two, own.at[1], send_two, recv_two)
+    large = start_trade(seq, me_seq, me_dp, pieces, swapped, own, send, recv)
     value = terms[me_seq]
     for step, copy in enumerate(copies):
         copy.wait()
@@ -160,7 +186,7 @@
         copy.wait()
 
 
-def closing(seq, dp, terms, pieces, pieces_two):
+def closing(seq, dp, terms, pieces):
     tile = terms.shape[2:]
     inside, anywhere = pl.BlockSpec(memory_space=pltpu.VMEM), pl.BlockSpec(memory_space=pl.ANY)
     return pl.pallas_call(
@@ -168,21 +194,20 @@
         out_shape=(
             jax.ShapeDtypeStruct(tile, F32),
             jax.ShapeDtypeStruct(pieces.shape, pieces.dtype),
-            jax.ShapeDtypeStruct(pieces_two.shape, pieces_two.dtype),
         ),
-        in_specs=[inside, anywhere, anywhere],
-        out_specs=(inside, anywhere, anywhere),
+        in_specs=[inside, anywhere],
+        out_specs=(inside, anywhere),
         scratch_shapes=[
             pltpu.VMEM(terms.shape, F32),
             pltpu.VMEM(terms.shape[1:], F32),
             pltpu.VMEM(terms.shape[1:], F32),
-            pltpu.SemaphoreType.DMA((2,)),
+            pltpu.SemaphoreType.DMA,
         ]
-        + [pltpu.SemaphoreType.DMA((seq,))] * 6
+        + [pltpu.SemaphoreType.DMA((seq,))] * 4
         + [pltpu.SemaphoreType.DMA((dp,))] * 2,
         compiler_params=pltpu.CompilerParams(collective_id=2, has_side_effects=True),
         name="closing",
-    )(terms, pieces, pieces_two)
+    )(terms, pieces)
 
 
 def head_parts(ref, where, part, size):
@@ -232,8 +257,37 @@
     )(where, joint)
 
 
-def attend_back_kernel(scaling, where, joint, flow, joint_back, key_sum, value_sum):
+def partner(me, step, count):
+    if count & (count - 1):
+        return lax.rem(me + step, count), lax.rem(me + count - step, count)
+    bit = 1
+    while bit < count:
+        if step & bit:
+            me = me + bit * (1 - 2 * lax.rem(me // bit, 2))
+        bit *= 2
+    return me, me
+
+
+def attend_back_kernel(scaling, plan, joint, flow, terms, joint_back, terms_all, key_sum, value_sum, send, recv):
     seq, _, block, size = flow.shape
+    me_seq, me_dp = lax.axis_index("seq"), lax.axis_index("dp")
+    here = pl.program_id(0) * pl.num_programs(1) + pl.program_id(1)
+    final = pl.num_programs(0) * pl.num_programs(1) - 1
+    copies = [
+        pltpu.make_async_remote_copy(
+            terms.at[spot], terms_all.at[spot], send.at[spot], recv.at[spot], (partner(me_seq, step, seq)[1], me_dp), MESH
+        )
+        for spot, (step, half) in enumerate(plan)
+        if step
+    ]
+
+    @pl.when(here == 0)
+    def _():
+        greet(seq, 1, me_seq, me_dp)
+        for copy in copies:
+            copy.start()
+
+    where = [partner(me_seq, place, seq)[1] for place in range(seq)]
     keys = jnp.concatenate(head_parts(joint, where, 1, size))
     values = jnp.concatenate(head_parts(joint, where, 2, size))
     for place in reversed(range(seq)):
@@ -261,81 +315,103 @@
         joint_back[where[place], 0, :, size : 2 * size] = key_sum[rows].astype(BF)
         joint_back[where[place], 0, :, 2 * size :] = value_sum[rows].astype(BF)
 
-
-def attend_back(where, joint, flow, size, scaling):
+    @pl.when(here == final)
+    def _():
+        for copy in copies:
+            copy.wait()
+
+
+def attend_back(plan, joint, flow, terms, size, scaling):
     seq, slots, block, width = joint.shape
     heads = width // (3 * size)
+    anywhere = pl.BlockSpec(memory_space=pl.ANY)
     wide = pl.BlockSpec((seq, 1, block, 3 * size), lambda slot, head: (0, slot, 0, head))
     return pl.pallas_call(
-        functools.partial(attend_back_kernel, scaling),
-        out_shape=jax.ShapeDtypeStruct(joint.shape, BF),
+        functools.partial(attend_back_kernel, scaling, plan),
+        out_shape=[jax.ShapeDtypeStruct(joint.shape, BF), jax.ShapeDtypeStruct(terms.shape, BF)],
         grid=(slots, heads),
-        in_specs=[
-            pl.BlockSpec(memory_space=pltpu.SMEM),
-            wide,
-            pl.BlockSpec((seq, 1, block, size), lambda slot, head: (0, slot, 0, head)),
-        ],
-        out_specs=wide,
-        scratch_shapes=[pltpu.VMEM((seq * block, size), F32)] * 2,
-        compiler_params=pltpu.CompilerParams(vmem_limit_bytes=48 << 20),
-        cost_estimate=pl.CostEstimate(flops=0, bytes_accessed=slots * (45 << 20), transcendentals=0),
+        in_specs=[wide, pl.BlockSpec((seq, 1, block, size), lambda slot, head: (0, slot, 0, head)), anywhere],
+        out_specs=[wide, anywhere],
+        scratch_shapes=[pltpu.VMEM((seq * block, size), F32)] * 2
+        + [pltpu.SemaphoreType.DMA((terms.shape[0],))] * 2,
+        compiler_params=pltpu.CompilerParams(
+            collective_id=4, has_side_effects=True, vmem_limit_bytes=48 << 20
+        ),
+        cost_estimate=pl.CostEstimate(flops=0, bytes_accessed=300 << 20, transcendentals=0),
         name="attend_back",
-    )(where, joint, flow)
-
-
-def partner(me, step, count):
-    if count & (count - 1):
-        return lax.rem(me + step, count), lax.rem(me + count - step, count)
-    bit = 1
-    while bit < count:
-        if step & bit:
-            me = me + bit * (1 - 2 * lax.rem(me // bit, 2))
-        bit *= 2
-    return me, me
+    )(joint, flow, terms)
+
+
+def forward_back_plan(seq):
+    if seq == 4:
+        order = [(0, 0), (0, 1), (1, 0), (2, 0), (1, 1), (2, 1), (3, 0), (3, 1)]
+    else:
+        order = [(step, half) for step in range(seq) for half in range(2)]
+    at = {pair: spot for spot, pair in enumerate(order)}
+    moves = []
+    for step, half in order[2:]:
+        if seq == 4 and step == 3:
+            source = (1, 0) if half == 0 else (2, 1)
+            moves.append((at[source], at[step, half], step - source[0], at[source]))
+        else:
+            moves.append((at[0, half], at[step, half], step, half))
+    return order, moves
 
 
 def forward_back_kernel(
     seq, chunk, mine, upstream, up, down, normed_all, hidden, expanded_back, result, flow_all,
-    normed, flow, load, store, send, recv, send_flow, recv_flow, keep,
+    normed, flow, load, store, send, recv, send_flow, recv_flow,
 ):
     model, width = up.shape
+    rows = normed.shape[1]
     pull = math.sqrt(2.0 / math.pi)
     me_seq, me_dp = lax.axis_index("seq"), lax.axis_index("dp")
     here = pl.program_id(0)
-    out, back = {}, {}
-    for step in range(1, seq):
-        target, origin = partner(me_seq, step, seq)
-        out[step] = pltpu.make_async_remote_copy(
-            normed.at[0], normed.at[step], send.at[step], recv.at[step], (target, me_dp), MESH
-        )
-        back[step] = pltpu.make_async_remote_copy(
-            flow.at[step], flow_all.at[step], send_flow.at[step], recv_flow.at[step], (origin, me_dp), MESH
-        )
-    stores = [pltpu.make_async_copy(normed.at[step], normed_all.at[step], store.at[step]) for step in range(seq)]
-    own = pltpu.make_async_copy(flow.at[0], flow_all.at[0], keep)
-    early = [step for step in range(1, seq) if step & (step - 1) == 0]
-    late = [step for step in range(1, seq) if step & (step - 1)]
+    order, moves = forward_back_plan(seq)
+    steps = len(order)
+    copies = {}
+    for source, target, step, begin in moves:
+        copies[target] = pltpu.make_async_remote_copy(
+            normed.at[source], normed.at[target], send.at[target], recv.at[target],
+            (partner(me_seq, step, seq)[0], me_dp), MESH,
+        )
+    backs = []
+    for spot, (step, half) in enumerate(order):
+        if step:
+            backs.append(
+                pltpu.make_async_remote_copy(
+                    flow.at[spot], flow_all.at[spot], send_flow.at[spot], recv_flow.at[spot],
+                    (partner(me_seq, step, seq)[1], me_dp), MESH,
+                )
+            )
+        else:
+            backs.append(pltpu.make_async_copy(flow.at[spot], flow_all.at[spot], recv_flow.at[spot]))
+    stores = [pltpu.make_async_copy(normed.at[spot], normed_all.at[spot], store.at[spot]) for spot in range(steps)]
 
     @pl.when(here == 0)
     def _():
-        fetch = pltpu.make_async_copy(mine, normed.at[0], load)
-        fetch.start()
+        fetches = [
+            pltpu.make_async_copy(mine.at[pl.ds(half * rows, rows)], normed.at[half], load.at[half]) for half in range(2)
+        ]
+        for fetch in fetches:
+            fetch.start()
         barrier = pltpu.get_barrier_semaphore()
         for step in range(1, seq):
             pl.semaphore_signal(barrier, inc=1, device_id=(lax.rem(me_seq + step, seq), me_dp), device_id_type=MESH)
-        fetch.wait()
+        for fetch in fetches:
+            fetch.wait()
         pl.semaphore_wait(barrier, seq - 1)
-        for step in early:
-            out[step].start()
-
-    for step in range(1, seq):
-
-        @pl.when(here == step)
-        def _(step=step):
-            out[step].wait()
-            if step == 1:
-                for other in late:
-                    out[other].start()
+
+    for spot in range(steps):
+
+        @pl.when(here == spot)
+        def _(spot=spot):
+            if spot > 1:
+                copies[spot].wait_recv()
+            for source, target, step, begin in moves:
+                if begin == spot:
+                    copies[target].start()
+            stores[spot].start()
 
     def inner(step, carry):
         columns = pl.ds(pl.multiple_of(step * chunk, chunk), chunk)
@@ -357,15 +433,11 @@
         return carry
 
     lax.fori_loop(0, model // chunk, outer, 0)
-    for step in range(seq):
-
-        @pl.when(here == step)
-        def _(step=step):
-            stores[step].start()
-            if step == 0:
-                own.start()
-            else:
-                back[step].start()
+    for spot in range(steps):
+
+        @pl.when(here == spot)
+        def _(spot=spot):
+            backs[spot].start()
 
     def last(step, carry):
         columns = pl.ds(pl.multiple_of(step * chunk, chunk), chunk)
@@ -374,37 +446,39 @@
 
     lax.fori_loop(0, model // chunk, last, 0)
 
-    @pl.when(here == seq - 1)
+    @pl.when(here == steps - 1)
     def _():
-        for copy in stores + [own] + list(back.values()):
+        for copy in copies.values():
+            copy.wait_send()
+        for copy in stores + backs:
             copy.wait()
 
 
 def forward_back(mine, upstream, up, down):
-    seq, rows, model = upstream.shape
+    steps, rows, model = upstream.shape
+    seq = steps // 2
     width = up.shape[1]
     anywhere = pl.BlockSpec(memory_space=pl.ANY)
     by_step = lambda columns: pl.BlockSpec((1, rows, columns), lambda step: (step, 0, 0))
     whole = lambda shape: pl.BlockSpec(shape, lambda step: (0, 0), pipeline_mode=pl.Buffered(1))
-    shape = lambda columns: jax.ShapeDtypeStruct((seq, rows, columns), BF)
+    shape = lambda columns: jax.ShapeDtypeStruct((steps, rows, columns), BF)
     return pl.pallas_call(
         functools.partial(forward_back_kernel, seq, math.gcd(512, math.gcd(width, model))),
         out_shape=[shape(model), shape(width), shape(width), shape(model), shape(model)],
-        grid=(seq,),
+        grid=(steps,),
         in_specs=[anywhere, by_step(model), whole(up.shape), whole(down.shape)],
         out_specs=[anywhere, by_step(width), by_step(width), by_step(model), anywhere],
         scratch_shapes=[
-            pltpu.VMEM((seq, rows, model), BF),
-            pltpu.VMEM((seq, rows, model), BF),
-            pltpu.SemaphoreType.DMA,
+            pltpu.VMEM((steps, rows, model), BF),
+            pltpu.VMEM((steps, rows, model), BF),
+            pltpu.SemaphoreType.DMA((2,)),
         ]
-        + [pltpu.SemaphoreType.DMA((seq,))] * 5
-        + [pltpu.SemaphoreType.DMA],
+        + [pltpu.SemaphoreType.DMA((steps,))] * 5,
         compiler_params=pltpu.CompilerParams(
-            collective_id=3, has_side_effects=True, vmem_limit_bytes=58 << 20
+            collective_id=3, has_side_effects=True, vmem_limit_bytes=56 << 20
         ),
         cost_estimate=pl.CostEstimate(
-            flops=8 * seq * rows * model * width, bytes_accessed=400 << 20, transcendentals=seq * rows * width
+            flops=8 * steps * rows * model * width, bytes_accessed=400 << 20, transcendentals=steps * rows * width
         ),
         name="forward_back",
     )(mine, upstream, up, down)
@@ -485,14 +559,14 @@
         small = jnp.stack([stretch, offset, dilation, translation]).astype(F32).reshape(-1)
         taken = small.shape[0]
         small = jnp.pad(small, (0, -taken % 1024)).reshape(-1, 128)
-        swapped_in, swapped_up, small = opening(
-            seq, dp, column_pieces(inward, 3, heads), column_pieces(upward, 1, 1), small
-        )
+        swapped_in, swapped_up, small, matrix_out = opening(
+            seq, dp, column_pieces(inward, 3, heads), column_pieces(upward, 1, 1), small, outward
+        )
+        matrix_out = matrix_out.reshape(-1, model)
         small = small.reshape(dp, seq, -1)[:, :, :taken].reshape(dp, seq, 4, -1).transpose(2, 1, 0, 3).reshape(4, model)
         gain_one, shift_one, gain_two, shift_two = small[0], small[1], small[2], small[3]
         matrix_in = gather_columns(swapped_in)
         blocks = gather_seq(after(residual, swapped_in))
-        matrix_out = lax.all_gather(after(outward, (matrix_in, blocks[-1])), "dp", axis=0, tiled=True)
         upstream = (cotangent.astype(F32).reshape(local_rows, model) * live).astype(BF)
         def piece(values, step):
             return values[step * local_rows : (step + 1) * local_rows]
@@ -504,54 +578,63 @@
         projected = jnp.concatenate([product(part, matrix_in).astype(BF) for part in normed])
         normed = jnp.concatenate(normed)
         upstream_all = gather_seq(after(upstream, blocks[-1]), projected)
-        matrix_up = gather_columns(after(swapped_up, (matrix_out, projected, upstream_all[1], upstream_all[2])))
+        matrix_up = gather_columns(after(swapped_up, (matrix_in, blocks[-1])))
         me = lax.axis_index("seq")
         where = me ^ jnp.arange(seq) if xor else (me + seq - jnp.arange(seq)) % seq
         joint = projected.reshape(seq, slots, block, -1)
         attended = attend(where, joint, size, scaling).reshape(total, heads * size)
-        attended = after(attended, upstream_all)
-        begun = []
-        middle = residual.astype(F32) + scatter_seq(
-            lambda step: product(piece(attended, step), matrix_out), None, begun
-        )
-        matrix_down = lax.all_gather(after(downward, (matrix_up, begun)), "dp", axis=0, tiled=True)
+        middle = residual.astype(F32) + scatter_seq(lambda step: product(piece(attended, step), matrix_out))
+        matrix_down = lax.all_gather(after(downward, (matrix_up, attended, upstream_all)), "dp", axis=0, tiled=True)
         unit_two, root_two = norm_parts(middle)
         mine = (unit_two * gain_two + shift_two).astype(BF)
-        upstream_all = jnp.stack(upstream_all)
+        half = local_rows // 2
+        plan = forward_back_plan(seq)[0]
+        upstream_all = jnp.stack([upstream_all[step][part * half : (part + 1) * half] for step, part in plan])
         normed_two, hidden, expanded_back, down_terms, two_terms = forward_back(mine, upstream_all, matrix_up, matrix_down)
 
         def flat(values):
             return values.reshape(-1, values.shape[-1])
 
         down_sum = rows_product(flat(hidden), flat(upstream_all))
-        two_back = jnp.sum(two_terms.astype(F32), axis=0)
+        spots = [[spot for spot, (_, part) in enumerate(plan) if part == which] for which in range(2)]
+
+        def over_plan(values):
+            return jnp.concatenate([sum(values[spot].astype(F32) for spot in places) for places in spots])
+
+        two_back = over_plan(two_terms)
         downward_delta = scatter_rows(down_sum)
         middle_flow, dilation_term, translation_term = norm_back(two_back, unit_two, root_two, gain_two)
         middle_back = upstream.astype(F32) + middle_flow
-        near_flow = middle_back.astype(BF)
-        middle_low = gather_seq(near_flow)
-        up_sum = rows_product(after(flat(normed_two), (down_sum, middle_low[1:3])), flat(expanded_back))
-        summed_up = scatter_columns(up_sum)
+        up_sum = rows_product(after(flat(normed_two), down_sum), flat(expanded_back))
+        middle_low = gather_seq(after(middle_back.astype(BF), up_sum))
         heads_back = jnp.concatenate([cols_product(part, matrix_out).astype(BF) for part in middle_low])
-        outward_delta = scatter_rows(rows_product(attended, jnp.concatenate(middle_low)))
+        out_sum = rows_product(attended, jnp.concatenate(middle_low))
         heads_back = after(heads_back, (downward_delta, up_sum)).reshape(seq, slots, block, -1)
-        projected_back = attend_back(where, joint, heads_back, size, scaling).reshape(total, -1)
-        corner = cols_product(piece(projected_back, seq - 1), matrix_in).astype(BF)
-        in_sum = rows_product(after(normed, (summed_up, corner)), projected_back)
+        summed_up = scatter_columns(after(up_sum, heads_back))
+        projected_back, result_terms = attend_back(plan, joint, heads_back, down_terms, size, scaling)
+        projected_back = projected_back.reshape(total, -1)
+        result = middle + over_plan([down_terms[0], down_terms[1]] + [result_terms[spot] for spot in range(2, len(plan))])
+        outputs = (result * live).astype(BF).reshape(slots, block, model)
+        one_terms = [cols_product(piece(projected_back, step), matrix_in) for step in range(seq)]
+        one_terms = [one_terms[0]] + lax.optimization_barrier([part.astype(BF) for part in one_terms[1:]])
+        near_up = [lax.dynamic_index_in_dim(summed_up, where[step], 0, keepdims=False) for step in range(seq)]
+        near_up = jnp.stack([near_up[0]] + [shift(near_up[step], step if xor else seq - step) for step in range(1, seq)])
+        if not xor:
+            near_up = near_up[(-jnp.arange(seq)) % seq]
+        upward_delta = jnp.concatenate(
+            [lax.dynamic_index_in_dim(near_up, where[step], 0, keepdims=False) for step in range(seq)], axis=1
+        ).astype(F32)
+        in_sum = rows_product(after(normed, (summed_up, one_terms[1:])), projected_back)
         summed_in = scatter_columns(in_sum)
-        one_terms = [cols_product(piece(projected_back, step), matrix_in) for step in range(seq - 1)]
-        one_terms = [one_terms[0]] + lax.optimization_barrier([part.astype(BF) for part in one_terms[1:]]) + [corner]
-        late_terms = after(down_terms, middle_low[-1])
-        result = middle + scatter_seq(lambda step: late_terms[step].astype(F32), one_terms[1:])
-        outputs = (result * live).astype(BF).reshape(slots, block, model)
-        one_back = scatter_seq(lambda step: one_terms[step], in_sum)
+        outward_delta = scatter_rows(after(out_sum, summed_in))
+        one_back = scatter_seq(lambda step: one_terms[step])
         unit_one, root_one = norm_parts(residual.astype(F32))
         input_flow, stretch_term, offset_term = norm_back(one_back, unit_one, root_one, gain_one)
         terms = jnp.stack([stretch_term, offset_term, dilation_term, translation_term])
         terms = terms.reshape(4, seq, dp, -1).transpose(1, 2, 0, 3).reshape(seq, dp, -1)
         terms = jnp.pad(terms, ((0, 0), (0, 0), (0, -taken % 1024))).reshape(seq, dp, -1, 128)
-        deltas, swapped_in, swapped_up = closing(seq, dp, terms, summed_in, summed_up)
-        inward_delta, upward_delta = column_rows(swapped_in, 3, heads), column_rows(swapped_up, 1, 1)
+        deltas, swapped_in = closing(seq, dp, terms, summed_in)
+        inward_delta = column_rows(swapped_in, 3, heads)
         deltas = deltas.reshape(-1)[:taken].reshape(4, -1)
         input_delta = (middle_back + input_flow).reshape(slots, block, model)
         return (

time: 961 us -> 920 us (0.957)
  Pallas kernels: 301 us -> 329 us
  matrix products: 135 us -> 116 us
  other arithmetic: 82.5 us -> 64 us
  waiting for transfers between devices: 309 us -> 295 us
  local copies, waits for them, and re-layouts: 64.4 us -> 52.3 us
  starting transfers between devices: 43.2 us -> 31.4 us
    pallas_call x1, Pallas kernels: 29.1 us -> 93.1 us  [attend_back(): pl.pallas_call(functools.partial(attend_back_kernel, scaling, plan), out_...]
    pallas_call x1, Pallas kernels: 196 us -> 169 us  [forward_back(): pl.pallas_call(functools.partial(forward_back_kernel, seq, math.gcd(512,...]
    pallas_call x1, Pallas kernels: 28.4 us -> 15 us  [closing(): pl.pallas_call(functools.partial(closing_kernel, seq, dp), out_shape=(jax...]
    dot_general x8, matrix products: 41.2 us -> 28 us  [cols_product(): lax.dot_general(left, right, (((1,), (1,)), ((), ())), preferred_element_...]
    all_gather x2 -> x1, waiting for transfers between devices: 11.7 us -> 0.01 us  [layer(): lax.all_gather(after(downward, (matrix_up, attended, upstream_all)), 'dp'...]
    reduce_scatter x2, starting transfers between devices: 10.5 us -> 0.49 us  [scatter_rows(): lax.psum_scatter(term.astype(BF), 'dp', scatter_dimension=0, tiled=True)]
    ppermute x30 -> x27, waiting for transfers between devices: 269 us -> 266 us  [shift(): return lax.ppermute(values, 'seq', pairs)]
    ppermute x30 -> x27, starting transfers between devices: 31.7 us -> 30.7 us  [shift(): return lax.ppermute(values, 'seq', pairs)]
  transfers between devices with their start and end apart: 38 -> 34, of which waited for: 24 -> 17; matrix products, arithmetic and copies ran while one was open for 24% -> 19% of each run, Pallas kernels for 5% -> 14%
where the time goes in v4:
time: 920 us; the launch traced here: 912 us
  Pallas kernels  329 us (36%)
  waiting for transfers between devices  295 us (32%)
  matrix products  116 us (13%)
  other arithmetic  64 us (7%)
  local copies, waits for them, and re-layouts  52.3 us (6%)
  starting transfers between devices  31.4 us (3%)
  between operations  24 us (3%)
    ppermute x27, waiting for transfers between devices, shift(): return lax.ppermute(values, 'seq', pairs)  266 us
    pallas_call x1, Pallas kernels, forward_back(): pl.pallas_call(functools.partial(forward_back_kernel, seq, math.gcd(512,...  169 us
    pallas_call x1, Pallas kernels, attend_back(): pl.pallas_call(functools.partial(attend_back_kernel, scaling, plan), out_...  93.1 us
    dot_general x4, matrix products, rows_product(): lax.dot_general(left, right, (((0,), (0,)), ((), ())), preferred_element_...  69.5 us
    pallas_call x1, Pallas kernels, opening(): pl.pallas_call(functools.partial(opening_kernel, seq, dp), out_shape=(jax...  32.8 us
    ppermute x27, starting transfers between devices, shift(): return lax.ppermute(values, 'seq', pairs)  30.7 us
    all_gather x2, waiting for transfers between devices, gather_columns(): lax.all_gather(swapped, 'dp', axis=1, tiled=True)  29.1 us
    dot_general x8, matrix products, cols_product(): lax.dot_general(left, right, (((1,), (1,)), ((), ())), preferred_element_...  28 us
  transfers between devices with their start and end apart: 34, of which 17 were waited for; matrix products, arithmetic and copies ran while one was open for 19% of the time, Pallas kernels for 14%

profile of v4, /device:TPU:0, one launch (start us, length us, event | category | flops | bytes accessed | tf_op | source)
XLA Modules:
  0.0 912.3 jit_solution(8028340926666258850)
XLA Ops:
  15.7 32.8 %opening.1 = (bf16[4,64,1536]{2,1,0:T(8,128)(2,1)}, bf16[4,64,2048]{2,1,0:T(8,128)(2,1)}, f32[8,4,8,128]{3,2,1,0:T(8,128)}, bf16[8,64,2048]{2,1,0:T(8,128)(2,1)}) custom-call(bf16[4,64,1536]{2,1,0:T(8,128)(2,1)} %reshape.299.pieces, bf16[4,64,2048]{2,1,0:T(8,128)(2,1)} %bitcast.185, f32[8,128]{1,0:T(8,128)} %bitcast_convert_fusion.small, bf16[64,2048]{1,0:T(8,128)(2,1)} %shard.1), custom_call_target="tpu_custom_call" | custom-call | tf_op jit(solution)/shard_map/opening/pallas_call | solution.py:132
  50.8 45.5 %collective-permute-done = bf16[512,2048]{1,0:T(8,128)(2,1)S(1)} collective-permute-done((bf16[512,2048]{1,0:T(8,128)(2,1)S(1)}, bf16[512,2048]{1,0:T(8,128)(2,1)S(1)}, u32[]{:S(2)}, u32[]{:S(2)}) %collective-permute-start) | collective-permute-done | bytes 2097184 | tf_op jit(solution)/shard_map/ppermute | solution.py:492
  100.1 20.9 %collective-permute-done.2 = bf16[256,2048]{1,0:T(8,128)(2,1)S(1)} collective-permute-done((bf16[256,2048]{1,0:T(8,128)(2,1)S(1)}, bf16[256,2048]{1,0:T(8,128)(2,1)S(1)}, u32[]{:S(2)}, u32[]{:S(2)}) %collective-permute-start.2) | collective-permute-done | bytes 1048608 | tf_op jit(solution)/shard_map/ppermute | solution.py:492
  159.6 19.6 %attend.1 = bf16[4,2,256,512]{3,2,1,0:T(8,128)(2,1)S(1)} custom-call(s32[4]{0:T(128)S(1)} %iota_xor_fusion.where, bf16[4,2,256,1536]{3,2,1,0:T(8,128)(2,1)} %bitcast.178), custom_call_target="tpu_custom_call" | custom-call | bytes 62914560 | tf_op jit(solution)/shard_map/attend/pallas_call | solution.py:245
  179.2 29.1 %all-gather.6.cloned.1.call-done = bf16[4,512,2048]{2,1,0:T(8,128)(2,1)} async-done(((bf16[4,64,2048]{2,1,0:T(8,128)(2,1)}), bf16[4,512,2048]{2,1,0:T(8,128)(2,1)}) %all-gather.6.cloned.1.call-update) | async-done | bytes 8388624 | tf_op jit(solution)/shard_map/all_gather | solution.py:530
  229.9 16.5 %collective-permute-done.5 = bf16[256,2048]{1,0:T(8,128)(2,1)S(1)} collective-permute-done((bf16[256,2048]{1,0:T(8,128)(2,1)S(1)}, bf16[256,2048]{1,0:T(8,128)(2,1)S(1)}, u32[]{:S(2)}, u32[]{:S(2)}) %collective-permute-start.5) | collective-permute-done | bytes 1048608 | tf_op jit(solution)/shard_map/ppermute | solution.py:492
  248.1 23.5 %collective-permute-done.7 = bf16[256,2048]{1,0:T(8,128)(2,1)S(1)} collective-permute-done((bf16[256,2048]{1,0:T(8,128)(2,1)S(1)}, bf16[256,2048]{1,0:T(8,128)(2,1)S(1)}, u32[]{:S(2)}, u32[]{:S(2)}) %collective-permute-start.7) | collective-permute-done | bytes 1048608 | tf_op jit(solution)/shard_map/ppermute | solution.py:492
  274.2 17.1 %collective-permute-done.4 = bf16[256,2048]{1,0:T(8,128)(2,1)S(1)} collective-permute-done((bf16[256,2048]{1,0:T(8,128)(2,1)S(1)}, bf16[256,2048]{1,0:T(8,128)(2,1)S(1)}, u32[]{:S(2)}, u32[]{:S(2)}) %collective-permute-start.4) | collective-permute-done | bytes 1048608 | tf_op jit(solution)/shard_map/ppermute | solution.py:492
  291.4 24.1 %collective-permute-done.6 = bf16[256,2048]{1,0:T(8,128)(2,1)S(1)} collective-permute-done((bf16[256,2048]{1,0:T(8,128)(2,1)S(1)}, bf16[256,2048]{1,0:T(8,128)(2,1)S(1)}, u32[]{:S(2)}, u32[]{:S(2)}) %collective-permute-start.6) | collective-permute-done | bytes 1048608 | tf_op jit(solution)/shard_map/ppermute | solution.py:492
  321.8 168.9 %forward_back.1 = (bf16[8,256,2048]{2,1,0:T(8,128)(2,1)}, bf16[8,256,2048]{2,1,0:T(8,128)(2,1)}, bf16[8,256,2048]{2,1,0:T(8,128)(2,1)}, bf16[8,256,2048]{2,1,0:T(8,128)(2,1)}, bf16[8,256,2048]{2,1,0:T(8,128)(2,1)}) custom-call(bf16[512,2048]{1,0:T(8,128)(2,1)} %add_convert_fusion.mine, bf16[8,256,2048]{2,1,0:T(8,128)(2,1)} %copy-done.35, ...), custom_call_target="tpu_custom_call" | custom-call | flops 68719476736 | bytes 419430400 | tf_op jit(solution)/shard_map/forward_back/pallas_call | solution.py:465
  490.7 23.7 %convolution_bitcast_fusion = bf16[2048,2048]{1,0:T(8,128)(2,1)} fusion(bf16[8,256,2048]{2,1,0:T(8,128)(2,1)} %get-tuple-element.51, bf16[8,256,2048]{2,1,0:T(8,128)(2,1)} %copy-done.35), kind=kOutput, calls=%fused_computation | convolution fusion | flops 17179869184 | bytes 25165824 | tf_op jit(solution)/shard_map/dot_general | solution.py:34
  526.9 20.7 %fusion.60 = bf16[2048,2048]{1,0:T(8,128)(2,1)} fusion(bf16[2048,2048]{1,0:T(8,128)(2,1)S(1)} %bitcast.232, bf16[2048,2048]{1,0:T(8,128)(2,1)S(1)} %bitcast.235), kind=kOutput, calls=%fused_computation.172 | convolution fusion | flops 17179869184 | bytes 25165824 | tf_op jit(solution)/shard_map/dot_general | solution.py:34
  549.9 44.0 %collective-permute-done.14 = bf16[512,2048]{1,0:T(8,128)(2,1)S(1)} collective-permute-done((bf16[512,2048]{1,0:T(8,128)(2,1)S(1)}, bf16[512,2048]{1,0:T(8,128)(2,1)S(1)}, u32[]{:S(2)}, u32[]{:S(2)}) %collective-permute-start.14) | collective-permute-done | bytes 2097184 | tf_op jit(solution)/shard_map/ppermute | solution.py:492
  600.7 16.8 %collective-permute-done.16 = bf16[256,2048]{1,0:T(8,128)(2,1)S(1)} collective-permute-done((bf16[256,2048]{1,0:T(8,128)(2,1)S(1)}, bf16[256,2048]{1,0:T(8,128)(2,1)S(1)}, u32[]{:S(2)}, u32[]{:S(2)}) %collective-permute-start.16) | collective-permute-done | bytes 1048608 | tf_op jit(solution)/shard_map/ppermute | solution.py:492
  623.6 8.1 pad_maximum_fusion
  631.8 93.1 %attend_back.1 = (bf16[4,2,256,1536]{3,2,1,0:T(8,128)(2,1)}, bf16[8,256,2048]{2,1,0:T(8,128)(2,1)}) custom-call(bf16[4,2,256,1536]{3,2,1,0:T(8,128)(2,1)} %bitcast.179, bf16[4,2,256,512]{3,2,1,0:T(8,128)(2,1)S(1)} %bitcast.172, bf16[8,256,2048]{2,1,0:T(8,128)(2,1)} %get-tuple-element.48.terms), custom_call_target="tpu_custom_call" | custom-call | bytes 314572800 | tf_op jit(solution)/shard_map/attend_back/pallas_call | solution.py:329
  743.3 19.2 %convolution_convert_fusion = bf16[2048,1536]{1,0:T(8,128)(2,1)} fusion(bf16[2048,2048]{1,0:T(8,128)(2,1)} %pad_maximum_fusion, bf16[2048,1536]{1,0:T(8,128)(2,1)} %bitcast.183), kind=kOutput, calls=%fused_computation.2 | convolution fusion | flops 12888047616 | bytes 20971520 | tf_op jit(solution)/shard_map/dot_general | solution.py:34
  780.6 6.0 fusion.61
  797.4 8.0 collective-permute-done.19
  806.8 8.1 collective-permute-done.21
  818.5 9.4 %collective-permute-done.18 = bf16[256,2048]{1,0:T(8,128)(2,1)S(1)} collective-permute-done((bf16[256,2048]{1,0:T(8,128)(2,1)S(1)}, bf16[256,2048]{1,0:T(8,128)(2,1)S(1)}, u32[]{:S(2)}, u32[]{:S(2)}) %collective-permute-start.18) | collective-permute-done | bytes 1048608 | tf_op jit(solution)/shard_map/ppermute | solution.py:492
  827.9 26.1 %collective-permute-done.20 = bf16[256,2048]{1,0:T(8,128)(2,1)S(1)} collective-permute-done((bf16[256,2048]{1,0:T(8,128)(2,1)S(1)}, bf16[256,2048]{1,0:T(8,128)(2,1)S(1)}, u32[]{:S(2)}, u32[]{:S(2)}) %collective-permute-start.20) | collective-permute-done | bytes 1048608 | tf_op jit(solution)/shard_map/ppermute | solution.py:492
  857.5 8.8 fusion.32
  880.0 15.0 %closing.1 = (f32[8,128]{1,0:T(8,128)}, bf16[4,64,1536]{2,1,0:T(8,128)(2,1)}) custom-call(f32[4,8,8,128]{3,2,1,0:T(8,128)} %copy.43, bf16[4,64,1536]{2,1,0:T(8,128)(2,1)} %reduce-scatter.9.cloned.1.call-done.pieces), custom_call_target="tpu_custom_call" | custom-call | tf_op jit(solution)/shard_map/closing/pallas_call | solution.py:192
  (306 shorter events, 183.2 us)
Async XLA Ops:
  7.2 117.3 %all-gather.4.cloned.1.call-start = ((), (), s32[]{:S(2)}) async-start(), calls=%async_computation.4 | async-start | bytes 7077888 | tf_op jit(solution)/shard_map/all_gather | solution.py:530
  48.6 159.8 %all-gather.6.cloned.1.call-start = ((), (), s32[]{:S(2)}) async-start(), calls=%async_computation.5 | async-start | bytes 9437184 | tf_op jit(solution)/shard_map/all_gather | solution.py:530
  48.6 47.7 %collective-permute-start = (bf16[512,2048]{1,0:T(8,128)(2,1)S(1)}, bf16[512,2048]{1,0:T(8,128)(2,1)S(1)}, u32[]{:S(2)}, u32[]{:S(2)}) collective-permute-start(bf16[512,2048]{1,0:T(8,128)(2,1)S(1)} %bitcast.173), channel_id=1, source_target_pairs={{0,8},{8,0},{16,24},{24,16},{1,9},{9,1},{17,25},{25,17},{2,10},{10... | collective-permute-start | bytes 6291464 | tf_op jit(solution)/shard_map/ppermute | solution.py:492
  49.7 47.9 %collective-permute-start.1 = (bf16[512,2048]{1,0:T(8,128)(2,1)S(1)}, bf16[512,2048]{1,0:T(8,128)(2,1)S(1)}, u32[]{:S(2)}, u32[]{:S(2)}) collective-permute-start(bf16[512,2048]{1,0:T(8,128)(2,1)S(1)} %bitcast.174), channel_id=1, source_target_pairs={{0,16},{8,24},{16,0},{24,8},{1,17},{9,25},{17,1},{25,9},{2,18},{10... | collective-permute-start | bytes 6291464 | tf_op jit(solution)/shard_map/ppermute | solution.py:492
  124.5 197.3 %all-gather.8.cloned.1.call-start = ((), (), s32[]{:S(2)}) async-start(), calls=%async_computation.6 | async-start | bytes 9437184 | tf_op jit(solution)/shard_map/all_gather | solution.py:587
  130.1 49.1 %collective-permute-start.10 = (bf16[512,2048]{1,0:T(8,128)(2,1)S(1)}, bf16[512,2048]{1,0:T(8,128)(2,1)}, u32[]{:S(2)}, u32[]{:S(2)}) collective-permute-start(bf16[512,2048]{1,0:T(8,128)(2,1)S(1)} %fusion.37), channel_id=1, source_target_pairs={{0,8},{8,0},{16,24},{24,16},{1,9},{9,1},{17,25},{25,17},{2,10},{10... | collective-permute-start | bytes 6291464 | tf_op jit(solution)/shard_map/ppermute | solution.py:492
  131.3 47.9 %collective-permute-start.11 = (bf16[512,2048]{1,0:T(8,128)(2,1)S(1)}, bf16[512,2048]{1,0:T(8,128)(2,1)}, u32[]{:S(2)}, u32[]{:S(2)}) collective-permute-start(bf16[512,2048]{1,0:T(8,128)(2,1)S(1)} %fusion.37), channel_id=1, source_target_pairs={{0,16},{8,24},{16,0},{24,8},{1,17},{9,25},{17,1},{25,9},{2,18},{10... | collective-permute-start | bytes 6291464 | tf_op jit(solution)/shard_map/ppermute | solution.py:492
  208.4 412.4 %reduce-scatter.5.cloned.1.call-start = ((), (), s32[]{:S(2)}) async-start(), calls=%async_computation.7 | async-start | bytes 9437184 | tf_op jit(solution)/shard_map/reduce_scatter | solution.py:546
  223.0 50.4 %collective-permute-start.12 = (bf16[256,2048]{1,0:T(8,128)(2,1)S(1)}, bf16[256,2048]{1,0:T(8,128)(2,1)S(1)}, u32[]{:S(2)}, u32[]{:S(2)}) collective-permute-start(bf16[256,2048]{1,0:T(8,128)(2,1)S(1)} %slice.300), channel_id=1, source_target_pairs={{0,16},{8,24},{16,0},{24,8},{1,17},{9,25},{17,1},{25,9},{2,18},{10... | collective-permute-start | bytes 3145736 | tf_op jit(solution)/shard_map/ppermute | solution.py:492
  224.5 49.6 %collective-permute-start.13 = (bf16[256,2048]{1,0:T(8,128)(2,1)S(1)}, bf16[256,2048]{1,0:T(8,128)(2,1)S(1)}, u32[]{:S(2)}, u32[]{:S(2)}) collective-permute-start(bf16[256,2048]{1,0:T(8,128)(2,1)S(1)} %slice.303), channel_id=1, source_target_pairs={{0,8},{8,0},{16,24},{24,16},{1,9},{9,1},{17,25},{25,17},{2,10},{10... | collective-permute-start | bytes 3145736 | tf_op jit(solution)/shard_map/ppermute | solution.py:492
  225.1 46.5 %collective-permute-start.7 = (bf16[256,2048]{1,0:T(8,128)(2,1)S(1)}, bf16[256,2048]{1,0:T(8,128)(2,1)S(1)}, u32[]{:S(2)}, u32[]{:S(2)}) collective-permute-start(bf16[256,2048]{1,0:T(8,128)(2,1)S(1)} %get-tuple-element.95), channel_id=1, source_target_pairs={{0,16},{8,24},{16,0},{24,8},{1,17},{9,25},{17,1},{25,9},{2,18},{10... | collective-permute-start | bytes 3145736 | tf_op jit(solution)/shard_map/ppermute | solution.py:492
  228.5 62.9 %collective-permute-start.4 = (bf16[256,2048]{1,0:T(8,128)(2,1)S(1)}, bf16[256,2048]{1,0:T(8,128)(2,1)S(1)}, u32[]{:S(2)}, u32[]{:S(2)}) collective-permute-start(bf16[256,2048]{1,0:T(8,128)(2,1)S(1)} %slice.290), channel_id=1, source_target_pairs={{0,8},{8,0},{16,24},{24,16},{1,9},{9,1},{17,25},{25,17},{2,10},{10... | collective-permute-start | bytes 3145736 | tf_op jit(solution)/shard_map/ppermute | solution.py:492
  246.4 69.4 %collective-permute-start.9 = (bf16[256,2048]{1,0:T(8,128)(2,1)S(1)}, bf16[256,2048]{1,0:T(8,128)(2,1)S(1)}, u32[]{:S(2)}, u32[]{:S(2)}) collective-permute-start(bf16[256,2048]{1,0:T(8,128)(2,1)S(1)} %slice.297), channel_id=1, source_target_pairs={{0,16},{8,24},{16,0},{24,8},{1,17},{9,25},{17,1},{25,9},{2,18},{10... | collective-permute-start | bytes 3145736 | tf_op jit(solution)/shard_map/ppermute | solution.py:492
  271.6 44.0 %collective-permute-start.6 = (bf16[256,2048]{1,0:T(8,128)(2,1)S(1)}, bf16[256,2048]{1,0:T(8,128)(2,1)S(1)}, u32[]{:S(2)}, u32[]{:S(2)}) collective-permute-start(bf16[256,2048]{1,0:T(8,128)(2,1)S(1)} %add_convert_fusion.4), channel_id=1, source_target_pairs={{0,16},{8,24},{16,0},{24,8},{1,17},{9,25},{17,1},{25,9},{2,18},{10... | collective-permute-start | bytes 3145736 | tf_op jit(solution)/shard_map/ppermute | solution.py:492
  273.4 42.5 %collective-permute-start.8 = (bf16[256,2048]{1,0:T(8,128)(2,1)S(1)}, bf16[256,2048]{1,0:T(8,128)(2,1)S(1)}, u32[]{:S(2)}, u32[]{:S(2)}) collective-permute-start(bf16[256,2048]{1,0:T(8,128)(2,1)S(1)} %add_convert_fusion.3), channel_id=1, source_target_pairs={{0,8},{8,0},{16,24},{24,16},{1,9},{9,1},{17,25},{25,17},{2,10},{10... | collective-permute-start | bytes 3145736 | tf_op jit(solution)/shard_map/ppermute | solution.py:492
  514.4 228.9 %reduce-scatter.7.cloned.1.call-start = ((), (), s32[]{:S(2)}) async-start(), calls=%async_computation.8 | async-start | bytes 9437184 | tf_op jit(solution)/shard_map/reduce_scatter | solution.py:535
  547.6 46.2 %collective-permute-start.14 = (bf16[512,2048]{1,0:T(8,128)(2,1)S(1)}, bf16[512,2048]{1,0:T(8,128)(2,1)S(1)}, u32[]{:S(2)}, u32[]{:S(2)}) collective-permute-start(bf16[512,2048]{1,0:T(8,128)(2,1)S(1)} %get-tuple-element.54), channel_id=1, source_target_pairs={{0,8},{8,0},{16,24},{24,16},{1,9},{9,1},{17,25},{25,17},{2,10},{10... | collective-permute-start | bytes 6291464 | tf_op jit(solution)/shard_map/ppermute | solution.py:492
  549.2 46.3 %collective-permute-start.15 = (bf16[512,2048]{1,0:T(8,128)(2,1)S(1)}, bf16[512,2048]{1,0:T(8,128)(2,1)S(1)}, u32[]{:S(2)}, u32[]{:S(2)}) collective-permute-start(bf16[512,2048]{1,0:T(8,128)(2,1)S(1)} %get-tuple-element.54), channel_id=1, source_target_pairs={{0,16},{8,24},{16,0},{24,8},{1,17},{9,25},{17,1},{25,9},{2,18},{10... | collective-permute-start | bytes 6291464 | tf_op jit(solution)/shard_map/ppermute | solution.py:492
  623.6 233.8 %reduce-scatter.9.cloned.1.call-start = ((), (), s32[]{:S(2)}) async-start(), calls=%async_computation.9 | async-start | bytes 7077888 | tf_op jit(solution)/shard_map/reduce_scatter | solution.py:535
  762.5 141.0 %reduce-scatter.11.cloned.1.call-start = ((), (), s32[]{:S(2)}) async-start(), calls=%async_computation.10 | async-start | bytes 2359296 | tf_op jit(solution)/shard_map/reduce_scatter | solution.py:546
  787.9 40.0 %collective-permute-start.18 = (bf16[256,2048]{1,0:T(8,128)(2,1)S(1)}, bf16[256,2048]{1,0:T(8,128)(2,1)S(1)}, u32[]{:S(2)}, u32[]{:S(2)}) collective-permute-start(bf16[256,2048]{1,0:T(8,128)(2,1)S(1)} %slice.306), channel_id=1, source_target_pairs={{0,8},{8,0},{16,24},{24,16},{1,9},{9,1},{17,25},{25,17},{2,10},{10... | collective-permute-start | bytes 3145736 | tf_op jit(solution)/shard_map/ppermute | solution.py:492
  790.8 64.9 %collective-permute-start.23 = (bf16[256,2048]{1,0:T(8,128)(2,1)S(1)}, bf16[256,2048]{1,0:T(8,128)(2,1)S(1)}, u32[]{:S(2)}, u32[]{:S(2)}) collective-permute-start(bf16[256,2048]{1,0:T(8,128)(2,1)S(1)} %slice.309), channel_id=1, source_target_pairs={{0,16},{8,24},{16,0},{24,8},{1,17},{9,25},{17,1},{25,9},{2,18},{10... | collective-permute-start | bytes 3145736 | tf_op jit(solution)/shard_map/ppermute | solution.py:492
  805.8 48.2 %collective-permute-start.20 = (bf16[256,2048]{1,0:T(8,128)(2,1)S(1)}, bf16[256,2048]{1,0:T(8,128)(2,1)S(1)}, u32[]{:S(2)}, u32[]{:S(2)}) collective-permute-start(bf16[256,2048]{1,0:T(8,128)(2,1)S(1)} %add_convert_fusion.2), channel_id=1, source_target_pairs={{0,16},{8,24},{16,0},{24,8},{1,17},{9,25},{17,1},{25,9},{2,18},{10... | collective-permute-start | bytes 3145736 | tf_op jit(solution)/shard_map/ppermute | solution.py:492
  815.3 40.5 %collective-permute-start.22 = (bf16[256,2048]{1,0:T(8,128)(2,1)S(1)}, bf16[256,2048]{1,0:T(8,128)(2,1)S(1)}, u32[]{:S(2)}, u32[]{:S(2)}) collective-permute-start(bf16[256,2048]{1,0:T(8,128)(2,1)S(1)} %add_convert_fusion.1), channel_id=1, source_target_pairs={{0,8},{8,0},{16,24},{24,16},{1,9},{9,1},{17,25},{25,17},{2,10},{10... | collective-permute-start | bytes 3145736 | tf_op jit(solution)/shard_map/ppermute | solution.py:492
  (63 other events, 986.3 us)
Sparse Core Ops, SparseCore 0:
  48.7 65.8 all-gather.3
  124.6 83.7 all-gather.5
  210.0 80.5 all-gather.7
  514.6 87.1 reduce-scatter.4
  623.7 87.9 reduce-scatter.6
  762.7 67.8 reduce-scatter.8
  857.6 34.2 reduce-scatter.10

commit v5 on v4

--- a/solution.py
+++ b/solution.py
@@ -268,23 +268,72 @@
     return me, me
 
 
-def attend_back_kernel(scaling, plan, joint, flow, terms, joint_back, terms_all, key_sum, value_sum, send, recv):
+def forward_back_plan(seq):
+    if seq == 4:
+        order = [(0, 0), (0, 1), (1, 0), (2, 0), (1, 1), (2, 1), (3, 0), (3, 1)]
+    else:
+        order = [(step, half) for step in range(seq) for half in range(2)]
+    at = {pair: spot for spot, pair in enumerate(order)}
+    moves = []
+    for step, half in order[2:]:
+        if seq == 4 and step == 3:
+            source = (1, 0) if half == 0 else (2, 1)
+            moves.append((at[source], at[step, half], step - source[0], at[source]))
+        else:
+            moves.append((at[0, half], at[step, half], step, half))
+    return order, moves
+
+
+def returns(seq, plan, me_seq, me_dp, parts, extra, landing, send, recv):
+    def copy(source, target, step, spot):
+        device = (partner(me_seq, step, seq)[1], me_dp)
+        return pltpu.make_async_remote_copy(source, target, send.at[spot], recv.at[spot], device, MESH)
+
+    if seq != 4:
+        return {spot: copy(parts(spot), landing.at[spot], step, spot) for spot, (step, _) in enumerate(plan) if step}, []
+    at = {pair: spot for spot, pair in enumerate(plan)}
+    now = {spot: copy(parts(spot), landing.at[spot], plan[spot][0], spot) for spot in (at[1, 0], at[2, 1])}
+    now[at[3, 0]] = copy(parts(at[3, 0]), extra.at[0], 1, at[3, 0])
+    now[at[3, 1]] = copy(parts(at[3, 1]), extra.at[1], 2, at[3, 1])
+    later = []
+    for half, spot in enumerate((at[2, 0], at[1, 1])):
+        later.append((spot, at[3, half], copy(parts(spot), landing.at[spot], plan[spot][0], spot)))
+    return now, later
+
+
+def landings(seq):
+    return 6 if seq == 4 else 2 * seq
+
+
+def add_into(ref, spot, other, half, chunk):
+    def body(step, carry):
+        columns = pl.ds(pl.multiple_of(step * chunk, chunk), chunk)
+        ref[spot, :, columns] = (ref[spot, :, columns].astype(F32) + other[half, :, columns].astype(F32)).astype(BF)
+        return carry
+
+    lax.fori_loop(0, ref.shape[2] // chunk, body, 0)
+
+
+def attend_back_kernel(
+    scaling, plan, joint, flow, terms, joint_back, terms_all, key_sum, value_sum, extra, held, load, send, recv
+):
     seq, _, block, size = flow.shape
     me_seq, me_dp = lax.axis_index("seq"), lax.axis_index("dp")
     here = pl.program_id(0) * pl.num_programs(1) + pl.program_id(1)
     final = pl.num_programs(0) * pl.num_programs(1) - 1
-    copies = [
-        pltpu.make_async_remote_copy(
-            terms.at[spot], terms_all.at[spot], send.at[spot], recv.at[spot], (partner(me_seq, step, seq)[1], me_dp), MESH
-        )
-        for spot, (step, half) in enumerate(plan)
-        if step
-    ]
+    delayed = {spot: half for half, spot in enumerate([plan.index((2, 0)), plan.index((1, 1))])} if seq == 4 else {}
+    now, later = returns(
+        seq, plan, me_seq, me_dp, lambda spot: held.at[delayed[spot]] if spot in delayed else terms.at[spot],
+        extra, terms_all, send, recv,
+    )
+    loads = [pltpu.make_async_copy(terms.at[spot], held.at[half], load.at[half]) for spot, half in delayed.items()]
 
     @pl.when(here == 0)
     def _():
+        for copy in loads:
+            copy.start()
         greet(seq, 1, me_seq, me_dp)
-        for copy in copies:
+        for copy in now.values():
             copy.start()
 
     where = [partner(me_seq, place, seq)[1] for place in range(seq)]
@@ -317,7 +366,17 @@
 
     @pl.when(here == final)
     def _():
-        for copy in copies:
+        for copy in loads:
+            copy.wait()
+        for half, (spot, corner, copy) in enumerate(later):
+            now[corner].wait_recv()
+            add_into(held, half, extra, half, 256)
+            copy.start()
+        for spot, copy in now.items():
+            copy.wait_send()
+            if spot not in [corner for _, corner, _ in later]:
+                copy.wait_recv()
+        for _, _, copy in later:
             copy.wait()
 
 
@@ -328,39 +387,28 @@
     wide = pl.BlockSpec((seq, 1, block, 3 * size), lambda slot, head: (0, slot, 0, head))
     return pl.pallas_call(
         functools.partial(attend_back_kernel, scaling, plan),
-        out_shape=[jax.ShapeDtypeStruct(joint.shape, BF), jax.ShapeDtypeStruct(terms.shape, BF)],
+        out_shape=[
+            jax.ShapeDtypeStruct(joint.shape, BF),
+            jax.ShapeDtypeStruct((landings(seq),) + terms.shape[1:], BF),
+        ],
         grid=(slots, heads),
         in_specs=[wide, pl.BlockSpec((seq, 1, block, size), lambda slot, head: (0, slot, 0, head)), anywhere],
         out_specs=[wide, anywhere],
         scratch_shapes=[pltpu.VMEM((seq * block, size), F32)] * 2
+        + [pltpu.VMEM((2,) + terms.shape[1:], BF)] * 2
+        + [pltpu.SemaphoreType.DMA((2,))]
         + [pltpu.SemaphoreType.DMA((terms.shape[0],))] * 2,
         compiler_params=pltpu.CompilerParams(
             collective_id=4, has_side_effects=True, vmem_limit_bytes=48 << 20
         ),
-        cost_estimate=pl.CostEstimate(flops=0, bytes_accessed=300 << 20, transcendentals=0),
+        cost_estimate=pl.CostEstimate(flops=0, bytes_accessed=240 << 20, transcendentals=0),
         name="attend_back",
     )(joint, flow, terms)
 
 
-def forward_back_plan(seq):
-    if seq == 4:
-        order = [(0, 0), (0, 1), (1, 0), (2, 0), (1, 1), (2, 1), (3, 0), (3, 1)]
-    else:
-        order = [(step, half) for step in range(seq) for half in range(2)]
-    at = {pair: spot for spot, pair in enumerate(order)}
-    moves = []
-    for step, half in order[2:]:
-        if seq == 4 and step == 3:
-            source = (1, 0) if half == 0 else (2, 1)
-            moves.append((at[source], at[step, half], step - source[0], at[source]))
-        else:
-            moves.append((at[0, half], at[step, half], step, half))
-    return order, moves
-
-
 def forward_back_kernel(
     seq, chunk, mine, upstream, up, down, normed_all, hidden, expanded_back, result, flow_all,
-    normed, flow, load, store, send, recv, send_flow, recv_flow,
+    normed, flow, extra, load, store, send, recv, send_flow, recv_flow,
 ):
     model, width = up.shape
     rows = normed.shape[1]
@@ -375,17 +423,8 @@
             normed.at[source], normed.at[target], send.at[target], recv.at[target],
             (partner(me_seq, step, seq)[0], me_dp), MESH,
         )
-    backs = []
-    for spot, (step, half) in enumerate(order):
-        if step:
-            backs.append(
-                pltpu.make_async_remote_copy(
-                    flow.at[spot], flow_all.at[spot], send_flow.at[spot], recv_flow.at[spot],
-                    (partner(me_seq, step, seq)[1], me_dp), MESH,
-                )
-            )
-        else:
-            backs.append(pltpu.make_async_copy(flow.at[spot], flow_all.at[spot], recv_flow.at[spot]))
+    backs, later = returns(seq, order, me_seq, me_dp, lambda spot: flow.at[spot], extra, flow_all, send_flow, recv_flow)
+    owns = [pltpu.make_async_copy(flow.at[spot], flow_all.at[spot], recv_flow.at[spot]) for spot in range(2)]
     stores = [pltpu.make_async_copy(normed.at[spot], normed_all.at[spot], store.at[spot]) for spot in range(steps)]
 
     @pl.when(here == 0)
@@ -437,7 +476,10 @@
 
         @pl.when(here == spot)
         def _(spot=spot):
-            backs[spot].start()
+            if spot in backs:
+                backs[spot].start()
+            elif spot < 2:
+                owns[spot].start()
 
     def last(step, carry):
         columns = pl.ds(pl.multiple_of(step * chunk, chunk), chunk)
@@ -448,9 +490,19 @@
 
     @pl.when(here == steps - 1)
     def _():
+        for half, (spot, corner, copy) in enumerate(later):
+            backs[corner].wait_recv()
+            add_into(flow, spot, extra, half, chunk)
+            copy.start()
         for copy in copies.values():
             copy.wait_send()
-        for copy in stores + backs:
+        for spot, copy in backs.items():
+            copy.wait_send()
+            if spot not in [corner for _, corner, _ in later]:
+                copy.wait_recv()
+        for _, _, copy in later:
+            copy.wait()
+        for copy in stores + owns:
             copy.wait()
 
 
@@ -464,13 +516,15 @@
     shape = lambda columns: jax.ShapeDtypeStruct((steps, rows, columns), BF)
     return pl.pallas_call(
         functools.partial(forward_back_kernel, seq, math.gcd(512, math.gcd(width, model))),
-        out_shape=[shape(model), shape(width), shape(width), shape(model), shape(model)],
+        out_shape=[shape(model), shape(width), shape(width), shape(model)]
+        + [jax.ShapeDtypeStruct((landings(seq), rows, model), BF)],
         grid=(steps,),
         in_specs=[anywhere, by_step(model), whole(up.shape), whole(down.shape)],
         out_specs=[anywhere, by_step(width), by_step(width), by_step(model), anywhere],
         scratch_shapes=[
             pltpu.VMEM((steps, rows, model), BF),
             pltpu.VMEM((steps, rows, model), BF),
+            pltpu.VMEM((2, rows, model), BF),
             pltpu.SemaphoreType.DMA((2,)),
         ]
         + [pltpu.SemaphoreType.DMA((steps,))] * 5,
@@ -583,8 +637,9 @@
         where = me ^ jnp.arange(seq) if xor else (me + seq - jnp.arange(seq)) % seq
         joint = projected.reshape(seq, slots, block, -1)
         attended = attend(where, joint, size, scaling).reshape(total, heads * size)
-        middle = residual.astype(F32) + scatter_seq(lambda step: product(piece(attended, step), matrix_out))
-        matrix_down = lax.all_gather(after(downward, (matrix_up, attended, upstream_all)), "dp", axis=0, tiled=True)
+        begun = []
+        middle = residual.astype(F32) + scatter_seq(lambda step: product(piece(attended, step), matrix_out), None, begun)
+        matrix_down = lax.all_gather(after(downward, (matrix_up, begun, upstream_all[1:3])), "dp", axis=0, tiled=True)
         unit_two, root_two = norm_parts(middle)
         mine = (unit_two * gain_two + shift_two).astype(BF)
         half = local_rows // 2
@@ -596,7 +651,7 @@
             return values.reshape(-1, values.shape[-1])
 
         down_sum = rows_product(flat(hidden), flat(upstream_all))
-        spots = [[spot for spot, (_, part) in enumerate(plan) if part == which] for which in range(2)]
+        spots = [[spot for spot, (_, part) in enumerate(plan) if part == which and spot < landings(seq)] for which in range(2)]
 
         def over_plan(values):
             return jnp.concatenate([sum(values[spot].astype(F32) for spot in places) for places in spots])
@@ -613,7 +668,7 @@
         summed_up = scatter_columns(after(up_sum, heads_back))
         projected_back, result_terms = attend_back(plan, joint, heads_back, down_terms, size, scaling)
         projected_back = projected_back.reshape(total, -1)
-        result = middle + over_plan([down_terms[0], down_terms[1]] + [result_terms[spot] for spot in range(2, len(plan))])
+        result = middle + over_plan([down_terms[0], down_terms[1]] + [result_terms[spot] for spot in range(2, landings(seq))])
         outputs = (result * live).astype(BF).reshape(slots, block, model)
         one_terms = [cols_product(piece(projected_back, step), matrix_in) for step in range(seq)]
         one_terms = [one_terms[0]] + lax.optimization_barrier([part.astype(BF) for part in one_terms[1:]])

time: 920 us -> 858 us (0.933)
  Pallas kernels: 329 us -> 295 us
  waiting for transfers between devices: 295 us -> 264 us
    all_gather x2, waiting for transfers between devices: 29.1 us -> 1.14 us  [gather_columns(): lax.all_gather(swapped, 'dp', axis=1, tiled=True)]
    pallas_call x1, Pallas kernels: 93.1 us -> 71.6 us  [attend_back(): pl.pallas_call(functools.partial(attend_back_kernel, scaling, plan), out_...]
    pallas_call x1, Pallas kernels: 169 us -> 156 us  [forward_back(): pl.pallas_call(functools.partial(forward_back_kernel, seq, math.gcd(512,...]
    unnamed x125 -> x127, local copies, waits for them, and re-layouts: 20.9 us -> 21.7 us
  transfers between devices with their start and end apart: 34 -> 34, of which waited for: 17 -> 17; matrix products, arithmetic and copies ran while one was open for 19% -> 20% of each run, Pallas kernels for 14% -> 12%
where the time goes in v5:
time: 858 us; the launch traced here: 850 us
  Pallas kernels  295 us (34%)
  waiting for transfers between devices  264 us (31%)
  matrix products  117 us (14%)
  other arithmetic  65.1 us (8%)
  local copies, waits for them, and re-layouts  54.1 us (6%)
  starting transfers between devices  31.2 us (4%)
  between operations  24 us (3%)
    ppermute x27, waiting for transfers between devices, shift(): return lax.ppermute(values, 'seq', pairs)  263 us
    pallas_call x1, Pallas kernels, forward_back(): pl.pallas_call(functools.partial(forward_back_kernel, seq, math.gcd(512,...  156 us
    pallas_call x1, Pallas kernels, attend_back(): pl.pallas_call(functools.partial(attend_back_kernel, scaling, plan), out_...  71.6 us
    dot_general x4, matrix products, rows_product(): lax.dot_general(left, right, (((0,), (0,)), ((), ())), preferred_element_...  69.6 us
    pallas_call x1, Pallas kernels, opening(): pl.pallas_call(functools.partial(opening_kernel, seq, dp), out_shape=(jax...  32.8 us
    ppermute x27, starting transfers between devices, shift(): return lax.ppermute(values, 'seq', pairs)  30.9 us
    dot_general x8, matrix products, cols_product(): lax.dot_general(left, right, (((1,), (1,)), ((), ())), preferred_element_...  28.2 us
    unnamed x127, local copies, waits for them, and re-layouts  21.7 us
  transfers between devices with their start and end apart: 34, of which 17 were waited for; matrix products, arithmetic and copies ran while one was open for 20% of the time, Pallas kernels for 12%

profile of v5, /device:TPU:0, one launch (start us, length us, event | category | flops | bytes accessed | tf_op | source)
XLA Modules:
  0.0 849.8 jit_solution(1908112632440752518)
XLA Ops:
  15.7 32.8 %opening.1 = (bf16[4,64,1536]{2,1,0:T(8,128)(2,1)}, bf16[4,64,2048]{2,1,0:T(8,128)(2,1)}, f32[8,4,8,128]{3,2,1,0:T(8,128)}, bf16[8,64,2048]{2,1,0:T(8,128)(2,1)}) custom-call(bf16[4,64,1536]{2,1,0:T(8,128)(2,1)} %reshape.291.pieces, bf16[4,64,2048]{2,1,0:T(8,128)(2,1)} %bitcast.185, f32[8,128]{1,0:T(8,128)} %bitcast_convert_fusion.small, bf16[64,2048]{1,0:T(8,128)(2,1)} %shard.1), custom_call_target="tpu_custom_call" | custom-call | tf_op jit(solution)/shard_map/opening/pallas_call | solution.py:132
  50.8 45.5 %collective-permute-done = bf16[512,2048]{1,0:T(8,128)(2,1)S(1)} collective-permute-done((bf16[512,2048]{1,0:T(8,128)(2,1)S(1)}, bf16[512,2048]{1,0:T(8,128)(2,1)S(1)}, u32[]{:S(2)}, u32[]{:S(2)}) %collective-permute-start) | collective-permute-done | bytes 2097184 | tf_op jit(solution)/shard_map/ppermute | solution.py:546
  100.1 20.9 %collective-permute-done.2 = bf16[256,2048]{1,0:T(8,128)(2,1)S(1)} collective-permute-done((bf16[256,2048]{1,0:T(8,128)(2,1)S(1)}, bf16[256,2048]{1,0:T(8,128)(2,1)S(1)}, u32[]{:S(2)}, u32[]{:S(2)}) %collective-permute-start.2) | collective-permute-done | bytes 1048608 | tf_op jit(solution)/shard_map/ppermute | solution.py:546
  137.4 5.2 fusion.23
  159.6 20.0 %attend.1 = bf16[4,2,256,512]{3,2,1,0:T(8,128)(2,1)S(1)} custom-call(s32[4]{0:T(128)S(1)} %iota_xor_fusion.where, bf16[4,2,256,1536]{3,2,1,0:T(8,128)(2,1)} %bitcast.178), custom_call_target="tpu_custom_call" | custom-call | bytes 62914560 | tf_op jit(solution)/shard_map/attend/pallas_call | solution.py:245
  185.5 21.3 %collective-permute-done.5 = bf16[256,2048]{1,0:T(8,128)(2,1)} collective-permute-done((bf16[256,2048]{1,0:T(8,128)(2,1)S(1)}, bf16[256,2048]{1,0:T(8,128)(2,1)}, u32[]{:S(2)}, u32[]{:S(2)}) %collective-permute-start.5) | collective-permute-done | bytes 1048608 | tf_op jit(solution)/shard_map/ppermute | solution.py:546
  231.6 14.0 %collective-permute-done.12 = bf16[256,2048]{1,0:T(8,128)(2,1)S(1)} collective-permute-done((bf16[256,2048]{1,0:T(8,128)(2,1)S(1)}, bf16[256,2048]{1,0:T(8,128)(2,1)S(1)}, u32[]{:S(2)}, u32[]{:S(2)}) %collective-permute-start.12) | collective-permute-done | bytes 1048608 | tf_op jit(solution)/shard_map/ppermute | solution.py:546
  247.6 22.3 %collective-permute-done.4 = bf16[256,2048]{1,0:T(8,128)(2,1)S(1)} collective-permute-done((bf16[256,2048]{1,0:T(8,128)(2,1)S(1)}, bf16[256,2048]{1,0:T(8,128)(2,1)S(1)}, u32[]{:S(2)}, u32[]{:S(2)}) %collective-permute-start.4) | collective-permute-done | bytes 1048608 | tf_op jit(solution)/shard_map/ppermute | solution.py:546
  269.9 20.0 %collective-permute-done.6 = bf16[256,2048]{1,0:T(8,128)(2,1)S(1)} collective-permute-done((bf16[256,2048]{1,0:T(8,128)(2,1)S(1)}, bf16[256,2048]{1,0:T(8,128)(2,1)S(1)}, u32[]{:S(2)}, u32[]{:S(2)}) %collective-permute-start.6) | collective-permute-done | bytes 1048608 | tf_op jit(solution)/shard_map/ppermute | solution.py:546
  297.3 155.6 %forward_back.1 = (bf16[8,256,2048]{2,1,0:T(8,128)(2,1)}, bf16[8,256,2048]{2,1,0:T(8,128)(2,1)}, bf16[8,256,2048]{2,1,0:T(8,128)(2,1)}, bf16[8,256,2048]{2,1,0:T(8,128)(2,1)}, bf16[6,256,2048]{2,1,0:T(8,128)(2,1)}) custom-call(bf16[512,2048]{1,0:T(8,128)(2,1)} %add_convert_fusion.mine, bf16[8,256,2048]{2,1,0:T(8,128)(2,1)} %copy-done.36, ...), custom_call_target="tpu_custom_call" | custom-call | flops 68719476736 | bytes 419430400 | tf_op jit(solution)/shard_map/forward_back/pallas_call | solution.py:517
  452.9 23.8 %convolution_bitcast_fusion = bf16[2048,2048]{1,0:T(8,128)(2,1)} fusion(bf16[8,256,2048]{2,1,0:T(8,128)(2,1)} %get-tuple-element.51, bf16[8,256,2048]{2,1,0:T(8,128)(2,1)} %copy-done.36), kind=kOutput, calls=%fused_computation | convolution fusion | flops 17179869184 | bytes 25165824 | tf_op jit(solution)/shard_map/dot_general | solution.py:34
  488.3 20.6 %fusion.60 = bf16[2048,2048]{1,0:T(8,128)(2,1)} fusion(bf16[2048,2048]{1,0:T(8,128)(2,1)S(1)} %bitcast.232, bf16[2048,2048]{1,0:T(8,128)(2,1)S(1)} %bitcast.235), kind=kOutput, calls=%fused_computation.172 | convolution fusion | flops 17179869184 | bytes 25165824 | tf_op jit(solution)/shard_map/dot_general | solution.py:34
  510.7 43.5 %collective-permute-done.14 = bf16[512,2048]{1,0:T(8,128)(2,1)S(1)} collective-permute-done((bf16[512,2048]{1,0:T(8,128)(2,1)S(1)}, bf16[512,2048]{1,0:T(8,128)(2,1)S(1)}, u32[]{:S(2)}, u32[]{:S(2)}) %collective-permute-start.14) | collective-permute-done | bytes 2097184 | tf_op jit(solution)/shard_map/ppermute | solution.py:546
  562.2 14.4 %collective-permute-done.16 = bf16[256,2048]{1,0:T(8,128)(2,1)S(1)} collective-permute-done((bf16[256,2048]{1,0:T(8,128)(2,1)S(1)}, bf16[256,2048]{1,0:T(8,128)(2,1)S(1)}, u32[]{:S(2)}, u32[]{:S(2)}) %collective-permute-start.16) | collective-permute-done | bytes 1048608 | tf_op jit(solution)/shard_map/ppermute | solution.py:546
  581.9 8.1 pad_maximum_fusion
  590.0 71.6 %attend_back.1 = (bf16[4,2,256,1536]{3,2,1,0:T(8,128)(2,1)}, bf16[6,256,2048]{2,1,0:T(8,128)(2,1)}) custom-call(bf16[4,2,256,1536]{3,2,1,0:T(8,128)(2,1)} %bitcast.179, bf16[4,2,256,512]{3,2,1,0:T(8,128)(2,1)S(1)} %bitcast.172, bf16[8,256,2048]{2,1,0:T(8,128)(2,1)} %get-tuple-element.48.terms), custom_call_target="tpu_custom_call" | custom-call | bytes 251658240 | tf_op jit(solution)/shard_map/attend_back/pallas_call | solution.py:388
  680.2 19.2 %convolution_convert_fusion = bf16[2048,1536]{1,0:T(8,128)(2,1)} fusion(bf16[2048,2048]{1,0:T(8,128)(2,1)} %pad_maximum_fusion, bf16[2048,1536]{1,0:T(8,128)(2,1)} %bitcast.183), kind=kOutput, calls=%fused_computation.2 | convolution fusion | flops 12888047616 | bytes 20971520 | tf_op jit(solution)/shard_map/dot_general | solution.py:34
  716.5 5.9 fusion.61
  733.0 9.3 %collective-permute-done.19 = bf16[256,2048]{1,0:T(8,128)(2,1)S(1)} collective-permute-done((bf16[256,2048]{1,0:T(8,128)(2,1)}, bf16[256,2048]{1,0:T(8,128)(2,1)S(1)}, u32[]{:S(2)}, u32[]{:S(2)}) %collective-permute-start.19) | collective-permute-done | bytes 1048608 | tf_op jit(solution)/shard_map/ppermute | solution.py:546
  743.3 8.3 collective-permute-done.21
  754.4 10.3 %collective-permute-done.18 = bf16[256,2048]{1,0:T(8,128)(2,1)S(1)} collective-permute-done((bf16[256,2048]{1,0:T(8,128)(2,1)S(1)}, bf16[256,2048]{1,0:T(8,128)(2,1)S(1)}, u32[]{:S(2)}, u32[]{:S(2)}) %collective-permute-start.18) | collective-permute-done | bytes 1048608 | tf_op jit(solution)/shard_map/ppermute | solution.py:546
  764.7 27.8 %collective-permute-done.20 = bf16[256,2048]{1,0:T(8,128)(2,1)S(1)} collective-permute-done((bf16[256,2048]{1,0:T(8,128)(2,1)S(1)}, bf16[256,2048]{1,0:T(8,128)(2,1)S(1)}, u32[]{:S(2)}, u32[]{:S(2)}) %collective-permute-start.20) | collective-permute-done | bytes 1048608 | tf_op jit(solution)/shard_map/ppermute | solution.py:546
  795.9 9.0 %fusion.32 = (f32[2048]{0:T(1024)S(1)}, f32[512]{0:T(512)S(1)}, f32[512]{0:T(512)S(1)}, f32[2048]{0:T(1024)S(1)}, f32[512,2048]{1,0:T(8,128)S(1)}) fusion(f32[512]{0:T(512)S(1)} %bitcast.211, f32[512]{0:T(512)S(1)} %bitcast.209, bf16[2,256,2048]{2,1,0:T(8,128)(2,1)S(1)} %copy-done.8, f32[2048]{0:T(1024)S(1)} %copy-done.39, ...), kind=kOutput, calls=%fused_computation.48 | convolution fusion | flops 3233803264 | bytes 18382848 | tf_op jit(solution)/shard_map/dot_general | solution.py:38
  818.0 14.4 %closing.1 = (f32[8,128]{1,0:T(8,128)}, bf16[4,64,1536]{2,1,0:T(8,128)(2,1)}) custom-call(f32[4,8,8,128]{3,2,1,0:T(8,128)} %copy.43, bf16[4,64,1536]{2,1,0:T(8,128)(2,1)} %reduce-scatter.9.cloned.1.call-done.pieces), custom_call_target="tpu_custom_call" | custom-call | tf_op jit(solution)/shard_map/closing/pallas_call | solution.py:192
  (308 shorter events, 181.8 us)
Async XLA Ops:
  7.2 117.3 %all-gather.4.cloned.1.call-start = ((), (), s32[]{:S(2)}) async-start(), calls=%async_computation.4 | async-start | bytes 7077888 | tf_op jit(solution)/shard_map/all_gather | solution.py:584
  48.6 159.8 %all-gather.6.cloned.1.call-start = ((), (), s32[]{:S(2)}) async-start(), calls=%async_computation.5 | async-start | bytes 9437184 | tf_op jit(solution)/shard_map/all_gather | solution.py:584
  48.6 47.7 %collective-permute-start = (bf16[512,2048]{1,0:T(8,128)(2,1)S(1)}, bf16[512,2048]{1,0:T(8,128)(2,1)S(1)}, u32[]{:S(2)}, u32[]{:S(2)}) collective-permute-start(bf16[512,2048]{1,0:T(8,128)(2,1)S(1)} %bitcast.173), channel_id=1, source_target_pairs={{0,8},{8,0},{16,24},{24,16},{1,9},{9,1},{17,25},{25,17},{2,10},{10... | collective-permute-start | bytes 6291464 | tf_op jit(solution)/shard_map/ppermute | solution.py:546
  49.7 47.9 %collective-permute-start.1 = (bf16[512,2048]{1,0:T(8,128)(2,1)S(1)}, bf16[512,2048]{1,0:T(8,128)(2,1)S(1)}, u32[]{:S(2)}, u32[]{:S(2)}) collective-permute-start(bf16[512,2048]{1,0:T(8,128)(2,1)S(1)} %bitcast.174), channel_id=1, source_target_pairs={{0,16},{8,24},{16,0},{24,8},{1,17},{9,25},{17,1},{25,9},{2,18},{10... | collective-permute-start | bytes 6291464 | tf_op jit(solution)/shard_map/ppermute | solution.py:546
  124.5 172.8 %all-gather.8.cloned.1.call-start = ((), (), s32[]{:S(2)}) async-start(), calls=%async_computation.6 | async-start | bytes 9437184 | tf_op jit(solution)/shard_map/all_gather | solution.py:642
  130.1 55.4 %collective-permute-start.10 = (bf16[512,2048]{1,0:T(8,128)(2,1)S(1)}, bf16[512,2048]{1,0:T(8,128)(2,1)}, u32[]{:S(2)}, u32[]{:S(2)}) collective-permute-start(bf16[512,2048]{1,0:T(8,128)(2,1)S(1)} %fusion.37), channel_id=1, source_target_pairs={{0,8},{8,0},{16,24},{24,16},{1,9},{9,1},{17,25},{25,17},{2,10},{10... | collective-permute-start | bytes 6291464 | tf_op jit(solution)/shard_map/ppermute | solution.py:546
  131.3 54.2 %collective-permute-start.11 = (bf16[512,2048]{1,0:T(8,128)(2,1)S(1)}, bf16[512,2048]{1,0:T(8,128)(2,1)}, u32[]{:S(2)}, u32[]{:S(2)}) collective-permute-start(bf16[512,2048]{1,0:T(8,128)(2,1)S(1)} %fusion.37), channel_id=1, source_target_pairs={{0,16},{8,24},{16,0},{24,8},{1,17},{9,25},{17,1},{25,9},{2,18},{10... | collective-permute-start | bytes 6291464 | tf_op jit(solution)/shard_map/ppermute | solution.py:546
  208.4 370.6 %reduce-scatter.5.cloned.1.call-start = ((), (), s32[]{:S(2)}) async-start(), calls=%async_computation.7 | async-start | bytes 9437184 | tf_op jit(solution)/shard_map/reduce_scatter | solution.py:600
  221.4 26.1 %collective-permute-start.13 = (bf16[256,2048]{1,0:T(8,128)(2,1)S(1)}, bf16[256,2048]{1,0:T(8,128)(2,1)S(1)}, u32[]{:S(2)}, u32[]{:S(2)}) collective-permute-start(bf16[256,2048]{1,0:T(8,128)(2,1)S(1)} %slice.287), channel_id=1, source_target_pairs={{0,8},{8,0},{16,24},{24,16},{1,9},{9,1},{17,25},{25,17},{2,10},{10... | collective-permute-start | bytes 3145736 | tf_op jit(solution)/shard_map/ppermute | solution.py:546
  225.5 44.4 %collective-permute-start.4 = (bf16[256,2048]{1,0:T(8,128)(2,1)S(1)}, bf16[256,2048]{1,0:T(8,128)(2,1)S(1)}, u32[]{:S(2)}, u32[]{:S(2)}) collective-permute-start(bf16[256,2048]{1,0:T(8,128)(2,1)S(1)} %slice.274), channel_id=1, source_target_pairs={{0,8},{8,0},{16,24},{24,16},{1,9},{9,1},{17,25},{25,17},{2,10},{10... | collective-permute-start | bytes 3145736 | tf_op jit(solution)/shard_map/ppermute | solution.py:546
  226.2 64.1 %collective-permute-start.9 = (bf16[256,2048]{1,0:T(8,128)(2,1)S(1)}, bf16[256,2048]{1,0:T(8,128)(2,1)S(1)}, u32[]{:S(2)}, u32[]{:S(2)}) collective-permute-start(bf16[256,2048]{1,0:T(8,128)(2,1)S(1)} %slice.281), channel_id=1, source_target_pairs={{0,16},{8,24},{16,0},{24,8},{1,17},{9,25},{17,1},{25,9},{2,18},{10... | collective-permute-start | bytes 3145736 | tf_op jit(solution)/shard_map/ppermute | solution.py:546
  228.2 61.7 %collective-permute-start.6 = (bf16[256,2048]{1,0:T(8,128)(2,1)S(1)}, bf16[256,2048]{1,0:T(8,128)(2,1)S(1)}, u32[]{:S(2)}, u32[]{:S(2)}) collective-permute-start(bf16[256,2048]{1,0:T(8,128)(2,1)S(1)} %add_convert_fusion.4), channel_id=1, source_target_pairs={{0,16},{8,24},{16,0},{24,8},{1,17},{9,25},{17,1},{25,9},{2,18},{10... | collective-permute-start | bytes 3145736 | tf_op jit(solution)/shard_map/ppermute | solution.py:546
  245.6 45.7 %collective-permute-start.8 = (bf16[256,2048]{1,0:T(8,128)(2,1)S(1)}, bf16[256,2048]{1,0:T(8,128)(2,1)S(1)}, u32[]{:S(2)}, u32[]{:S(2)}) collective-permute-start(bf16[256,2048]{1,0:T(8,128)(2,1)S(1)} %add_convert_fusion.3), channel_id=1, source_target_pairs={{0,8},{8,0},{16,24},{24,16},{1,9},{9,1},{17,25},{25,17},{2,10},{10... | collective-permute-start | bytes 3145736 | tf_op jit(solution)/shard_map/ppermute | solution.py:546
  476.7 203.4 %reduce-scatter.7.cloned.1.call-start = ((), (), s32[]{:S(2)}) async-start(), calls=%async_computation.8 | async-start | bytes 9437184 | tf_op jit(solution)/shard_map/reduce_scatter | solution.py:589
  508.9 45.3 %collective-permute-start.14 = (bf16[512,2048]{1,0:T(8,128)(2,1)S(1)}, bf16[512,2048]{1,0:T(8,128)(2,1)S(1)}, u32[]{:S(2)}, u32[]{:S(2)}) collective-permute-start(bf16[512,2048]{1,0:T(8,128)(2,1)S(1)} %get-tuple-element.54), channel_id=1, source_target_pairs={{0,8},{8,0},{16,24},{24,16},{1,9},{9,1},{17,25},{25,17},{2,10},{10... | collective-permute-start | bytes 6291464 | tf_op jit(solution)/shard_map/ppermute | solution.py:546
  509.7 44.8 %collective-permute-start.15 = (bf16[512,2048]{1,0:T(8,128)(2,1)S(1)}, bf16[512,2048]{1,0:T(8,128)(2,1)S(1)}, u32[]{:S(2)}, u32[]{:S(2)}) collective-permute-start(bf16[512,2048]{1,0:T(8,128)(2,1)S(1)} %get-tuple-element.54), channel_id=1, source_target_pairs={{0,16},{8,24},{16,0},{24,8},{1,17},{9,25},{17,1},{25,9},{2,18},{10... | collective-permute-start | bytes 6291464 | tf_op jit(solution)/shard_map/ppermute | solution.py:546
  581.8 214.1 %reduce-scatter.9.cloned.1.call-start = ((), (), s32[]{:S(2)}) async-start(), calls=%async_computation.9 | async-start | bytes 7077888 | tf_op jit(solution)/shard_map/reduce_scatter | solution.py:589
  699.4 141.6 %reduce-scatter.11.cloned.1.call-start = ((), (), s32[]{:S(2)}) async-start(), calls=%async_computation.10 | async-start | bytes 2359296 | tf_op jit(solution)/shard_map/reduce_scatter | solution.py:600
  715.9 26.3 %collective-permute-start.19 = (bf16[256,2048]{1,0:T(8,128)(2,1)}, bf16[256,2048]{1,0:T(8,128)(2,1)S(1)}, u32[]{:S(2)}, u32[]{:S(2)}) collective-permute-start(bf16[256,2048]{1,0:T(8,128)(2,1)} %get-tuple-element.92), channel_id=1, source_target_pairs={{0,8},{8,0},{16,24},{24,16},{1,9},{9,1},{17,25},{25,17},{2,10},{10... | collective-permute-start | bytes 3145736 | tf_op jit(solution)/shard_map/ppermute | solution.py:546
  723.8 41.0 %collective-permute-start.18 = (bf16[256,2048]{1,0:T(8,128)(2,1)S(1)}, bf16[256,2048]{1,0:T(8,128)(2,1)S(1)}, u32[]{:S(2)}, u32[]{:S(2)}) collective-permute-start(bf16[256,2048]{1,0:T(8,128)(2,1)S(1)} %slice.290), channel_id=1, source_target_pairs={{0,8},{8,0},{16,24},{24,16},{1,9},{9,1},{17,25},{25,17},{2,10},{10... | collective-permute-start | bytes 3145736 | tf_op jit(solution)/shard_map/ppermute | solution.py:546
  725.3 26.3 %collective-permute-start.21 = (bf16[256,2048]{1,0:T(8,128)(2,1)}, bf16[256,2048]{1,0:T(8,128)(2,1)S(1)}, u32[]{:S(2)}, u32[]{:S(2)}) collective-permute-start(bf16[256,2048]{1,0:T(8,128)(2,1)} %get-tuple-element.93), channel_id=1, source_target_pairs={{0,16},{8,24},{16,0},{24,8},{1,17},{9,25},{17,1},{25,9},{2,18},{10... | collective-permute-start | bytes 3145736 | tf_op jit(solution)/shard_map/ppermute | solution.py:546
  727.2 67.0 %collective-permute-start.23 = (bf16[256,2048]{1,0:T(8,128)(2,1)S(1)}, bf16[256,2048]{1,0:T(8,128)(2,1)S(1)}, u32[]{:S(2)}, u32[]{:S(2)}) collective-permute-start(bf16[256,2048]{1,0:T(8,128)(2,1)S(1)} %slice.293), channel_id=1, source_target_pairs={{0,16},{8,24},{16,0},{24,8},{1,17},{9,25},{17,1},{25,9},{2,18},{10... | collective-permute-start | bytes 3145736 | tf_op jit(solution)/shard_map/ppermute | solution.py:546
  742.7 49.8 %collective-permute-start.20 = (bf16[256,2048]{1,0:T(8,128)(2,1)S(1)}, bf16[256,2048]{1,0:T(8,128)(2,1)S(1)}, u32[]{:S(2)}, u32[]{:S(2)}) collective-permute-start(bf16[256,2048]{1,0:T(8,128)(2,1)S(1)} %add_convert_fusion.2), channel_id=1, source_target_pairs={{0,16},{8,24},{16,0},{24,8},{1,17},{9,25},{17,1},{25,9},{2,18},{10... | collective-permute-start | bytes 3145736 | tf_op jit(solution)/shard_map/ppermute | solution.py:546
  752.1 42.1 %collective-permute-start.22 = (bf16[256,2048]{1,0:T(8,128)(2,1)S(1)}, bf16[256,2048]{1,0:T(8,128)(2,1)S(1)}, u32[]{:S(2)}, u32[]{:S(2)}) collective-permute-start(bf16[256,2048]{1,0:T(8,128)(2,1)S(1)} %add_convert_fusion.1), channel_id=1, source_target_pairs={{0,8},{8,0},{16,24},{24,16},{1,9},{9,1},{17,25},{25,17},{2,10},{10... | collective-permute-start | bytes 3145736 | tf_op jit(solution)/shard_map/ppermute | solution.py:546
  (64 other events, 877.1 us)
Sparse Core Ops, SparseCore 0:
  48.7 65.8 all-gather.3
  124.6 83.7 all-gather.5
  210.0 81.0 all-gather.7
  476.9 86.3 reduce-scatter.4
  581.9 87.4 reduce-scatter.6
  699.5 67.3 reduce-scatter.8
  796.0 32.5 reduce-scatter.10

commit v6 on v5

--- a/solution.py
+++ b/solution.py
@@ -148,7 +148,7 @@
 
 
 def closing_kernel(
-    seq, dp, terms, pieces, total, swapped, over_seq, partial, over_dp,
+    seq, dp, groups, terms, pieces, total, whole, swapped, over_seq, partial, over_dp,
     own, send, recv, send_seq, recv_seq, send_row, recv_row,
 ):
     me_seq, me_dp = lax.axis_index("seq"), lax.axis_index("dp")
@@ -184,20 +184,28 @@
     total[...] = value
     for copy in large:
         copy.wait()
-
-
-def closing(seq, dp, terms, pieces):
+    size = whole.shape[1] // (3 * seq * groups)
+    for source in range(seq):
+        for group in range(groups):
+            for third in range(3):
+                place = ((third * seq + source) * groups + group) * size
+                piece = swapped[source, :, (group * 3 + third) * size : (group * 3 + third + 1) * size]
+                whole[:, place : place + size] = piece.astype(F32)
+
+
+def closing(seq, dp, groups, terms, pieces):
     tile = terms.shape[2:]
     inside, anywhere = pl.BlockSpec(memory_space=pltpu.VMEM), pl.BlockSpec(memory_space=pl.ANY)
     return pl.pallas_call(
-        functools.partial(closing_kernel, seq, dp),
+        functools.partial(closing_kernel, seq, dp, groups),
         out_shape=(
             jax.ShapeDtypeStruct(tile, F32),
-            jax.ShapeDtypeStruct(pieces.shape, pieces.dtype),
+            jax.ShapeDtypeStruct((pieces.shape[1], seq * pieces.shape[2]), F32),
         ),
         in_specs=[inside, anywhere],
-        out_specs=(inside, anywhere),
+        out_specs=(inside, inside),
         scratch_shapes=[
+            pltpu.VMEM(pieces.shape, BF),
             pltpu.VMEM(terms.shape, F32),
             pltpu.VMEM(terms.shape[1:], F32),
             pltpu.VMEM(terms.shape[1:], F32),
@@ -538,6 +546,80 @@
     )(mine, upstream, up, down)
 
 
+def send_back_kernel(
+    seq, plan, chunk, left, right, pieces, landing, swapped, flow, extra, keep, send, recv, own, send_piece, recv_piece
+):
+    me_seq, me_dp = lax.axis_index("seq"), lax.axis_index("dp")
+    model = right.shape[0]
+    now, later = returns(seq, plan, me_seq, me_dp, lambda spot: flow.at[spot], extra, landing, send, recv)
+    owns = [pltpu.make_async_copy(flow.at[spot], landing.at[spot], keep.at[spot]) for spot in range(2)]
+    greet(seq, 1, me_seq, me_dp)
+
+    def work(spot):
+        def body(step, carry):
+            columns = pl.ds(pl.multiple_of(step * chunk, chunk), chunk)
+            flow[spot, :, columns] = cols_product(left[plan[spot][0] * 2 + plan[spot][1]], right[columns, :]).astype(BF)
+            return carry
+
+        lax.fori_loop(0, model // chunk, body, 0)
+
+    corners = [corner for _, corner, _ in later]
+    for spot in corners + [spot for spot in now if spot not in corners]:
+        work(spot)
+        now[spot].start()
+    for spot, _, _ in later:
+        work(spot)
+    for spot in range(2):
+        work(spot)
+        owns[spot].start()
+    for half, (spot, corner, copy) in enumerate(later):
+        now[corner].wait_recv()
+        add_into(flow, spot, extra, half, chunk)
+        copy.start()
+    for copy in start_trade(seq, me_seq, me_dp, pieces, swapped, own, send_piece, recv_piece):
+        copy.wait()
+    for spot, copy in now.items():
+        copy.wait_send()
+        if spot not in corners:
+            copy.wait_recv()
+    for _, _, copy in later:
+        copy.wait()
+    for copy in owns:
+        copy.wait()
+
+
+def send_back(seq, plan, left, right, pieces):
+    steps = len(plan)
+    model, depth = right.shape
+    left = left.reshape(steps, -1, depth)
+    rows = left.shape[1]
+    inside, anywhere = pl.BlockSpec(memory_space=pltpu.VMEM), pl.BlockSpec(memory_space=pl.ANY)
+    return pl.pallas_call(
+        functools.partial(send_back_kernel, seq, plan, math.gcd(512, model)),
+        out_shape=[
+            jax.ShapeDtypeStruct((landings(seq), rows, model), BF),
+            jax.ShapeDtypeStruct(pieces.shape, pieces.dtype),
+        ],
+        in_specs=[inside, inside, anywhere],
+        out_specs=[anywhere, anywhere],
+        scratch_shapes=[
+            pltpu.VMEM((steps, rows, model), BF),
+            pltpu.VMEM((2, rows, model), BF),
+            pltpu.SemaphoreType.DMA((2,)),
+        ]
+        + [pltpu.SemaphoreType.DMA((steps,))] * 2
+        + [pltpu.SemaphoreType.DMA]
+        + [pltpu.SemaphoreType.DMA((seq,))] * 2,
+        compiler_params=pltpu.CompilerParams(
+            collective_id=5, has_side_effects=True, vmem_limit_bytes=44 << 20
+        ),
+        cost_estimate=pl.CostEstimate(
+            flops=2 * steps * rows * model * depth, bytes_accessed=240 << 20, transcendentals=0
+        ),
+        name="send_back",
+    )(left, right, pieces)
+
+
 def make_layer(seq, dp):
     xor = seq & (seq - 1) == 0
 
@@ -591,11 +673,6 @@
         )
         return summed
 
-    def column_rows(swapped, thirds, groups):
-        _, rows, width = swapped.shape
-        shaped = swapped.reshape(seq, rows, groups, thirds, -1).transpose(1, 3, 0, 2, 4)
-        return shaped.reshape(rows, seq * width).astype(F32)
-
     def scatter_rows(term):
         return lax.psum_scatter(term.astype(BF), "dp", scatter_dimension=0, tiled=True).astype(F32)
 
@@ -670,26 +747,18 @@
         projected_back = projected_back.reshape(total, -1)
         result = middle + over_plan([down_terms[0], down_terms[1]] + [result_terms[spot] for spot in range(2, landings(seq))])
         outputs = (result * live).astype(BF).reshape(slots, block, model)
-        one_terms = [cols_product(piece(projected_back, step), matrix_in) for step in range(seq)]
-        one_terms = [one_terms[0]] + lax.optimization_barrier([part.astype(BF) for part in one_terms[1:]])
-        near_up = [lax.dynamic_index_in_dim(summed_up, where[step], 0, keepdims=False) for step in range(seq)]
-        near_up = jnp.stack([near_up[0]] + [shift(near_up[step], step if xor else seq - step) for step in range(1, seq)])
-        if not xor:
-            near_up = near_up[(-jnp.arange(seq)) % seq]
-        upward_delta = jnp.concatenate(
-            [lax.dynamic_index_in_dim(near_up, where[step], 0, keepdims=False) for step in range(seq)], axis=1
-        ).astype(F32)
-        in_sum = rows_product(after(normed, (summed_up, one_terms[1:])), projected_back)
+        in_sum = rows_product(after(normed, (summed_up, outputs)), projected_back)
         summed_in = scatter_columns(in_sum)
-        outward_delta = scatter_rows(after(out_sum, summed_in))
-        one_back = scatter_seq(lambda step: one_terms[step])
+        one_terms, swapped_up = send_back(seq, plan, after(projected_back, in_sum), matrix_in, summed_up)
+        upward_delta = jnp.concatenate([swapped_up[step] for step in range(seq)], axis=1).astype(F32)
+        one_back = over_plan(one_terms)
+        outward_delta = scatter_rows(after(out_sum, (summed_in, one_terms)))
         unit_one, root_one = norm_parts(residual.astype(F32))
         input_flow, stretch_term, offset_term = norm_back(one_back, unit_one, root_one, gain_one)
         terms = jnp.stack([stretch_term, offset_term, dilation_term, translation_term])
         terms = terms.reshape(4, seq, dp, -1).transpose(1, 2, 0, 3).reshape(seq, dp, -1)
         terms = jnp.pad(terms, ((0, 0), (0, 0), (0, -taken % 1024))).reshape(seq, dp, -1, 128)
-        deltas, swapped_in = closing(seq, dp, terms, summed_in)
-        inward_delta = column_rows(swapped_in, 3, heads)
+        deltas, inward_delta = closing(seq, dp, heads, terms, summed_in)
         deltas = deltas.reshape(-1)[:taken].reshape(4, -1)
         input_delta = (middle_back + input_flow).reshape(slots, block, model)
         return (

time: 858 us -> 855 us (level)
  Pallas kernels: 295 us -> 387 us
  waiting for transfers between devices: 264 us -> 209 us
  matrix products: 117 us -> 93.7 us
  starting transfers between devices: 31.2 us -> 21.4 us
    pallas_call x1 -> x2, Pallas kernels: 14.4 us -> 107 us  [the longest x1 89.2 us: send_back(): pl.pallas_call(functools.partial(send_back_kernel, seq, plan, math.gcd(51...]
    ppermute x27 -> x18, waiting for transfers between devices: 263 us -> 205 us  [shift(): return lax.ppermute(values, 'seq', pairs)]
    dot_general x8 -> x4, matrix products: 28.2 us -> 5.21 us  [cols_product(): lax.dot_general(left, right, (((1,), (1,)), ((), ())), preferred_element_...]
    ppermute x27 -> x18, starting transfers between devices: 30.9 us -> 21.2 us  [shift(): return lax.ppermute(values, 'seq', pairs)]
    unnamed x127 -> x121, local copies, waits for them, and re-layouts: 21.7 us -> 30 us
  transfers between devices with their start and end apart: 34 -> 25, of which waited for: 17 -> 13; matrix products, arithmetic and copies ran while one was open for 20% -> 17% of each run, Pallas kernels for 12% -> 23%
where the time goes in v6:
time: 855 us; the launch traced here: 847 us
  Pallas kernels  387 us (45%)
  waiting for transfers between devices  209 us (24%)
  matrix products  93.7 us (11%)
  other arithmetic  73.4 us (9%)
  local copies, waits for them, and re-layouts  45.7 us (5%)
  starting transfers between devices  21.4 us (3%)
  between operations  16.4 us (2%)
    ppermute x18, waiting for transfers between devices, shift(): return lax.ppermute(values, 'seq', pairs)  205 us
    pallas_call x1, Pallas kernels, forward_back(): pl.pallas_call(functools.partial(forward_back_kernel, seq, math.gcd(512,...  156 us
    pallas_call x1, Pallas kernels, send_back(): pl.pallas_call(functools.partial(send_back_kernel, seq, plan, math.gcd(51...  89.2 us
    pallas_call x1, Pallas kernels, attend_back(): pl.pallas_call(functools.partial(attend_back_kernel, scaling, plan), out_...  71.5 us
    dot_general x4, matrix products, rows_product(): lax.dot_general(left, right, (((0,), (0,)), ((), ())), preferred_element_...  69.6 us
    pallas_call x1, Pallas kernels, opening(): pl.pallas_call(functools.partial(opening_kernel, seq, dp), out_shape=(jax...  32.8 us
    unnamed x121, local copies, waits for them, and re-layouts  30 us
    ppermute x18, starting transfers between devices, shift(): return lax.ppermute(values, 'seq', pairs)  21.2 us
  transfers between devices with their start and end apart: 25, of which 13 were waited for; matrix products, arithmetic and copies ran while one was open for 17% of the time, Pallas kernels for 23%

profile of v6, /device:TPU:0, one launch (start us, length us, event | category | flops | bytes accessed | tf_op | source)
XLA Modules:
  0.0 846.9 jit_solution(10043163558385711457)
XLA Ops:
  15.7 32.8 %opening.1 = (bf16[4,64,1536]{2,1,0:T(8,128)(2,1)}, bf16[4,64,2048]{2,1,0:T(8,128)(2,1)}, f32[8,4,8,128]{3,2,1,0:T(8,128)}, bf16[8,64,2048]{2,1,0:T(8,128)(2,1)}) custom-call(bf16[4,64,1536]{2,1,0:T(8,128)(2,1)} %reshape.346.pieces, bf16[4,64,2048]{2,1,0:T(8,128)(2,1)} %bitcast.166, f32[8,128]{1,0:T(8,128)} %bitcast_convert_fusion.small, bf16[64,2048]{1,0:T(8,128)(2,1)} %shard.1), custom_call_target="tpu_custom_call" | custom-call | tf_op jit(solution)/shard_map/opening/pallas_call | solution.py:132
  50.8 45.5 %collective-permute-done = bf16[512,2048]{1,0:T(8,128)(2,1)S(1)} collective-permute-done((bf16[512,2048]{1,0:T(8,128)(2,1)S(1)}, bf16[512,2048]{1,0:T(8,128)(2,1)S(1)}, u32[]{:S(2)}, u32[]{:S(2)}) %collective-permute-start) | collective-permute-done | bytes 2097184 | tf_op jit(solution)/shard_map/ppermute | solution.py:628
  100.1 20.9 %collective-permute-done.2 = bf16[256,2048]{1,0:T(8,128)(2,1)S(1)} collective-permute-done((bf16[256,2048]{1,0:T(8,128)(2,1)S(1)}, bf16[256,2048]{1,0:T(8,128)(2,1)S(1)}, u32[]{:S(2)}, u32[]{:S(2)}) %collective-permute-start.2) | collective-permute-done | bytes 1048608 | tf_op jit(solution)/shard_map/ppermute | solution.py:628
  137.4 5.2 fusion.30
  159.5 19.8 %attend.1 = bf16[4,2,256,512]{3,2,1,0:T(8,128)(2,1)S(1)} custom-call(s32[4]{0:T(128)S(1)} %iota_xor_fusion.where, bf16[4,2,256,1536]{3,2,1,0:T(8,128)(2,1)} %bitcast.160), custom_call_target="tpu_custom_call" | custom-call | bytes 62914560 | tf_op jit(solution)/shard_map/attend/pallas_call | solution.py:253
  185.2 21.2 %collective-permute-done.5 = bf16[256,2048]{1,0:T(8,128)(2,1)} collective-permute-done((bf16[256,2048]{1,0:T(8,128)(2,1)S(1)}, bf16[256,2048]{1,0:T(8,128)(2,1)}, u32[]{:S(2)}, u32[]{:S(2)}) %collective-permute-start.5) | collective-permute-done | bytes 1048608 | tf_op jit(solution)/shard_map/ppermute | solution.py:628
  231.4 14.4 %collective-permute-done.12 = bf16[256,2048]{1,0:T(8,128)(2,1)S(1)} collective-permute-done((bf16[256,2048]{1,0:T(8,128)(2,1)S(1)}, bf16[256,2048]{1,0:T(8,128)(2,1)S(1)}, u32[]{:S(2)}, u32[]{:S(2)}) %collective-permute-start.12) | collective-permute-done | bytes 1048608 | tf_op jit(solution)/shard_map/ppermute | solution.py:628
  247.3 22.3 %collective-permute-done.4 = bf16[256,2048]{1,0:T(8,128)(2,1)S(1)} collective-permute-done((bf16[256,2048]{1,0:T(8,128)(2,1)S(1)}, bf16[256,2048]{1,0:T(8,128)(2,1)S(1)}, u32[]{:S(2)}, u32[]{:S(2)}) %collective-permute-start.4) | collective-permute-done | bytes 1048608 | tf_op jit(solution)/shard_map/ppermute | solution.py:628
  269.7 20.4 %collective-permute-done.6 = bf16[256,2048]{1,0:T(8,128)(2,1)S(1)} collective-permute-done((bf16[256,2048]{1,0:T(8,128)(2,1)S(1)}, bf16[256,2048]{1,0:T(8,128)(2,1)S(1)}, u32[]{:S(2)}, u32[]{:S(2)}) %collective-permute-start.6) | collective-permute-done | bytes 1048608 | tf_op jit(solution)/shard_map/ppermute | solution.py:628
  297.0 155.9 %forward_back.1 = (bf16[8,256,2048]{2,1,0:T(8,128)(2,1)}, bf16[8,256,2048]{2,1,0:T(8,128)(2,1)}, bf16[8,256,2048]{2,1,0:T(8,128)(2,1)}, bf16[8,256,2048]{2,1,0:T(8,128)(2,1)}, bf16[6,256,2048]{2,1,0:T(8,128)(2,1)}) custom-call(bf16[512,2048]{1,0:T(8,128)(2,1)} %add_convert_fusion.mine, bf16[8,256,2048]{2,1,0:T(8,128)(2,1)} %copy-done.36, ...), custom_call_target="tpu_custom_call" | custom-call | flops 68719476736 | bytes 419430400 | tf_op jit(solution)/shard_map/forward_back/pallas_call | solution.py:525
  452.9 23.8 %convolution_bitcast_fusion = bf16[2048,2048]{1,0:T(8,128)(2,1)} fusion(bf16[8,256,2048]{2,1,0:T(8,128)(2,1)} %get-tuple-element.51, bf16[8,256,2048]{2,1,0:T(8,128)(2,1)} %copy-done.36), kind=kOutput, calls=%fused_computation | convolution fusion | flops 17179869184 | bytes 25165824 | tf_op jit(solution)/shard_map/dot_general | solution.py:34
  476.8 4.4 fusion.45
  488.4 20.5 %fusion.63 = bf16[2048,2048]{1,0:T(8,128)(2,1)} fusion(bf16[2048,2048]{1,0:T(8,128)(2,1)S(1)} %bitcast.204, bf16[2048,2048]{1,0:T(8,128)(2,1)S(1)} %bitcast.207), kind=kOutput, calls=%fused_computation.164 | convolution fusion | flops 17179869184 | bytes 25165824 | tf_op jit(solution)/shard_map/dot_general | solution.py:34
  510.7 43.5 %collective-permute-done.14 = bf16[512,2048]{1,0:T(8,128)(2,1)S(1)} collective-permute-done((bf16[512,2048]{1,0:T(8,128)(2,1)S(1)}, bf16[512,2048]{1,0:T(8,128)(2,1)S(1)}, u32[]{:S(2)}, u32[]{:S(2)}) %collective-permute-start.14) | collective-permute-done | bytes 2097184 | tf_op jit(solution)/shard_map/ppermute | solution.py:628
  562.2 14.3 %collective-permute-done.16 = bf16[256,2048]{1,0:T(8,128)(2,1)S(1)} collective-permute-done((bf16[256,2048]{1,0:T(8,128)(2,1)S(1)}, bf16[256,2048]{1,0:T(8,128)(2,1)S(1)}, u32[]{:S(2)}, u32[]{:S(2)}) %collective-permute-start.16) | collective-permute-done | bytes 1048608 | tf_op jit(solution)/shard_map/ppermute | solution.py:628
  581.9 7.5 pad_maximum_fusion
  589.4 71.5 %attend_back.1 = (bf16[4,2,256,1536]{3,2,1,0:T(8,128)(2,1)}, bf16[6,256,2048]{2,1,0:T(8,128)(2,1)}) custom-call(bf16[4,2,256,1536]{3,2,1,0:T(8,128)(2,1)} %bitcast.161, bf16[4,2,256,512]{3,2,1,0:T(8,128)(2,1)S(1)} %bitcast.154, bf16[8,256,2048]{2,1,0:T(8,128)(2,1)} %get-tuple-element.48.terms), custom_call_target="tpu_custom_call" | custom-call | bytes 251658240 | tf_op jit(solution)/shard_map/attend_back/pallas_call | solution.py:396
  660.8 4.2 add_bitcast_fusion.1
  669.4 19.2 %fusion.64 = bf16[2048,1536]{1,0:T(8,128)(2,1)} fusion(bf16[2048,2048]{1,0:T(8,128)(2,1)} %pad_maximum_fusion, bf16[2048,1536]{1,0:T(8,128)(2,1)} %bitcast.200), kind=kOutput, calls=%fused_computation.165 | convolution fusion | flops 12884901888 | bytes 20971520 | tf_op jit(solution)/shard_map/dot_general | solution.py:34
  696.7 6.0 fusion.65
  702.7 89.2 %send_back.1 = (bf16[6,256,2048]{2,1,0:T(8,128)(2,1)S(1)}, bf16[4,64,2048]{2,1,0:T(8,128)(2,1)S(1)}) custom-call(bf16[8,256,1536]{2,1,0:T(8,128)(2,1)} %bitcast.201, bf16[2048,1536]{1,0:T(8,128)(2,1)} %bitcast.193, bf16[4,64,2048]{2,1,0:T(8,128)(2,1)S(1)} %copy-done.3), custom_call_target="tpu_custom_call" | custom-call | flops 12884901888 | bytes 251658240 | tf_op jit(solution)/shard_map/send_back/pallas_call | solution.py:597
  794.5 6.1 fusion.49
  807.7 7.0 fusion.35
  816.2 17.7 %closing.1 = (f32[8,128]{1,0:T(8,128)}, f32[64,6144]{1,0:T(8,128)}) custom-call(f32[4,8,8,128]{3,2,1,0:T(8,128)} %copy.42, bf16[4,64,1536]{2,1,0:T(8,128)(2,1)} %reduce-scatter.9.cloned.1.call-done.pieces), custom_call_target="tpu_custom_call" | custom-call | tf_op jit(solution)/shard_map/closing/pallas_call | solution.py:199
  (270 shorter events, 137.3 us)
Async XLA Ops:
  7.2 117.3 %all-gather.4.cloned.1.call-start = ((), (), s32[]{:S(2)}) async-start(), calls=%async_computation.4 | async-start | bytes 7077888 | tf_op jit(solution)/shard_map/all_gather | solution.py:666
  48.6 159.8 %all-gather.6.cloned.1.call-start = ((), (), s32[]{:S(2)}) async-start(), calls=%async_computation.5 | async-start | bytes 9437184 | tf_op jit(solution)/shard_map/all_gather | solution.py:666
  48.6 47.7 %collective-permute-start = (bf16[512,2048]{1,0:T(8,128)(2,1)S(1)}, bf16[512,2048]{1,0:T(8,128)(2,1)S(1)}, u32[]{:S(2)}, u32[]{:S(2)}) collective-permute-start(bf16[512,2048]{1,0:T(8,128)(2,1)S(1)} %bitcast.155), channel_id=1, source_target_pairs={{0,8},{8,0},{16,24},{24,16},{1,9},{9,1},{17,25},{25,17},{2,10},{10... | collective-permute-start | bytes 6291464 | tf_op jit(solution)/shard_map/ppermute | solution.py:628
  49.7 47.9 %collective-permute-start.1 = (bf16[512,2048]{1,0:T(8,128)(2,1)S(1)}, bf16[512,2048]{1,0:T(8,128)(2,1)S(1)}, u32[]{:S(2)}, u32[]{:S(2)}) collective-permute-start(bf16[512,2048]{1,0:T(8,128)(2,1)S(1)} %bitcast.156), channel_id=1, source_target_pairs={{0,16},{8,24},{16,0},{24,8},{1,17},{9,25},{17,1},{25,9},{2,18},{10... | collective-permute-start | bytes 6291464 | tf_op jit(solution)/shard_map/ppermute | solution.py:628
  96.4 24.5 %collective-permute-start.2 = (bf16[256,2048]{1,0:T(8,128)(2,1)S(1)}, bf16[256,2048]{1,0:T(8,128)(2,1)S(1)}, u32[]{:S(2)}, u32[]{:S(2)}) collective-permute-start(bf16[256,2048]{1,0:T(8,128)(2,1)S(1)} %slice.234), channel_id=1, source_target_pairs={{0,16},{8,24},{16,0},{24,8},{1,17},{9,25},{17,1},{25,9},{2,18},{10... | collective-permute-start | bytes 3145736 | tf_op jit(solution)/shard_map/ppermute | solution.py:628
  99.0 24.4 %collective-permute-start.3 = (bf16[256,2048]{1,0:T(8,128)(2,1)S(1)}, bf16[256,2048]{1,0:T(8,128)(2,1)S(1)}, u32[]{:S(2)}, u32[]{:S(2)}) collective-permute-start(bf16[256,2048]{1,0:T(8,128)(2,1)S(1)} %slice.235), channel_id=1, source_target_pairs={{0,8},{8,0},{16,24},{24,16},{1,9},{9,1},{17,25},{25,17},{2,10},{10... | collective-permute-start | bytes 3145736 | tf_op jit(solution)/shard_map/ppermute | solution.py:628
  124.5 172.6 %all-gather.8.cloned.1.call-start = ((), (), s32[]{:S(2)}) async-start(), calls=%async_computation.6 | async-start | bytes 9437184 | tf_op jit(solution)/shard_map/all_gather | solution.py:719
  130.1 55.1 %collective-permute-start.10 = (bf16[512,2048]{1,0:T(8,128)(2,1)S(1)}, bf16[512,2048]{1,0:T(8,128)(2,1)}, u32[]{:S(2)}, u32[]{:S(2)}) collective-permute-start(bf16[512,2048]{1,0:T(8,128)(2,1)S(1)} %fusion.38), channel_id=1, source_target_pairs={{0,8},{8,0},{16,24},{24,16},{1,9},{9,1},{17,25},{25,17},{2,10},{10... | collective-permute-start | bytes 6291464 | tf_op jit(solution)/shard_map/ppermute | solution.py:628
  131.3 53.9 %collective-permute-start.11 = (bf16[512,2048]{1,0:T(8,128)(2,1)S(1)}, bf16[512,2048]{1,0:T(8,128)(2,1)}, u32[]{:S(2)}, u32[]{:S(2)}) collective-permute-start(bf16[512,2048]{1,0:T(8,128)(2,1)S(1)} %fusion.38), channel_id=1, source_target_pairs={{0,16},{8,24},{16,0},{24,8},{1,17},{9,25},{17,1},{25,9},{2,18},{10... | collective-permute-start | bytes 6291464 | tf_op jit(solution)/shard_map/ppermute | solution.py:628
  183.4 23.0 %collective-permute-start.5 = (bf16[256,2048]{1,0:T(8,128)(2,1)S(1)}, bf16[256,2048]{1,0:T(8,128)(2,1)}, u32[]{:S(2)}, u32[]{:S(2)}) collective-permute-start(bf16[256,2048]{1,0:T(8,128)(2,1)S(1)} %get-tuple-element.91), channel_id=1, source_target_pairs={{0,8},{8,0},{16,24},{24,16},{1,9},{9,1},{17,25},{25,17},{2,10},{10... | collective-permute-start | bytes 3145736 | tf_op jit(solution)/shard_map/ppermute | solution.py:628
  184.4 22.5 %collective-permute-start.7 = (bf16[256,2048]{1,0:T(8,128)(2,1)S(1)}, bf16[256,2048]{1,0:T(8,128)(2,1)}, u32[]{:S(2)}, u32[]{:S(2)}) collective-permute-start(bf16[256,2048]{1,0:T(8,128)(2,1)S(1)} %get-tuple-element.92), channel_id=1, source_target_pairs={{0,16},{8,24},{16,0},{24,8},{1,17},{9,25},{17,1},{25,9},{2,18},{10... | collective-permute-start | bytes 3145736 | tf_op jit(solution)/shard_map/ppermute | solution.py:628
  208.4 370.6 %reduce-scatter.5.cloned.1.call-start = ((), (), s32[]{:S(2)}) async-start(), calls=%async_computation.7 | async-start | bytes 9437184 | tf_op jit(solution)/shard_map/reduce_scatter | solution.py:677
  219.7 26.1 %collective-permute-start.12 = (bf16[256,2048]{1,0:T(8,128)(2,1)S(1)}, bf16[256,2048]{1,0:T(8,128)(2,1)S(1)}, u32[]{:S(2)}, u32[]{:S(2)}) collective-permute-start(bf16[256,2048]{1,0:T(8,128)(2,1)S(1)} %slice.248), channel_id=1, source_target_pairs={{0,16},{8,24},{16,0},{24,8},{1,17},{9,25},{17,1},{25,9},{2,18},{10... | collective-permute-start | bytes 3145736 | tf_op jit(solution)/shard_map/ppermute | solution.py:628
  221.1 26.1 %collective-permute-start.13 = (bf16[256,2048]{1,0:T(8,128)(2,1)S(1)}, bf16[256,2048]{1,0:T(8,128)(2,1)S(1)}, u32[]{:S(2)}, u32[]{:S(2)}) collective-permute-start(bf16[256,2048]{1,0:T(8,128)(2,1)S(1)} %slice.251), channel_id=1, source_target_pairs={{0,8},{8,0},{16,24},{24,16},{1,9},{9,1},{17,25},{25,17},{2,10},{10... | collective-permute-start | bytes 3145736 | tf_op jit(solution)/shard_map/ppermute | solution.py:628
  225.3 44.4 %collective-permute-start.4 = (bf16[256,2048]{1,0:T(8,128)(2,1)S(1)}, bf16[256,2048]{1,0:T(8,128)(2,1)S(1)}, u32[]{:S(2)}, u32[]{:S(2)}) collective-permute-start(bf16[256,2048]{1,0:T(8,128)(2,1)S(1)} %slice.238), channel_id=1, source_target_pairs={{0,8},{8,0},{16,24},{24,16},{1,9},{9,1},{17,25},{25,17},{2,10},{10... | collective-permute-start | bytes 3145736 | tf_op jit(solution)/shard_map/ppermute | solution.py:628
  226.0 64.4 %collective-permute-start.9 = (bf16[256,2048]{1,0:T(8,128)(2,1)S(1)}, bf16[256,2048]{1,0:T(8,128)(2,1)S(1)}, u32[]{:S(2)}, u32[]{:S(2)}) collective-permute-start(bf16[256,2048]{1,0:T(8,128)(2,1)S(1)} %slice.245), channel_id=1, source_target_pairs={{0,16},{8,24},{16,0},{24,8},{1,17},{9,25},{17,1},{25,9},{2,18},{10... | collective-permute-start | bytes 3145736 | tf_op jit(solution)/shard_map/ppermute | solution.py:628
  228.3 61.7 %collective-permute-start.6 = (bf16[256,2048]{1,0:T(8,128)(2,1)S(1)}, bf16[256,2048]{1,0:T(8,128)(2,1)S(1)}, u32[]{:S(2)}, u32[]{:S(2)}) collective-permute-start(bf16[256,2048]{1,0:T(8,128)(2,1)S(1)} %add_convert_fusion.2), channel_id=1, source_target_pairs={{0,16},{8,24},{16,0},{24,8},{1,17},{9,25},{17,1},{25,9},{2,18},{10... | collective-permute-start | bytes 3145736 | tf_op jit(solution)/shard_map/ppermute | solution.py:628
  245.8 45.3 %collective-permute-start.8 = (bf16[256,2048]{1,0:T(8,128)(2,1)S(1)}, bf16[256,2048]{1,0:T(8,128)(2,1)S(1)}, u32[]{:S(2)}, u32[]{:S(2)}) collective-permute-start(bf16[256,2048]{1,0:T(8,128)(2,1)S(1)} %add_convert_fusion.1), channel_id=1, source_target_pairs={{0,8},{8,0},{16,24},{24,16},{1,9},{9,1},{17,25},{25,17},{2,10},{10... | collective-permute-start | bytes 3145736 | tf_op jit(solution)/shard_map/ppermute | solution.py:628
  476.8 192.6 %reduce-scatter.7.cloned.1.call-start = ((), (), s32[]{:S(2)}) async-start(), calls=%async_computation.8 | async-start | bytes 9437184 | tf_op jit(solution)/shard_map/reduce_scatter | solution.py:671
  508.9 45.3 %collective-permute-start.14 = (bf16[512,2048]{1,0:T(8,128)(2,1)S(1)}, bf16[512,2048]{1,0:T(8,128)(2,1)S(1)}, u32[]{:S(2)}, u32[]{:S(2)}) collective-permute-start(bf16[512,2048]{1,0:T(8,128)(2,1)S(1)} %get-tuple-element.54), channel_id=1, source_target_pairs={{0,8},{8,0},{16,24},{24,16},{1,9},{9,1},{17,25},{25,17},{2,10},{10... | collective-permute-start | bytes 6291464 | tf_op jit(solution)/shard_map/ppermute | solution.py:628
  509.6 44.8 %collective-permute-start.15 = (bf16[512,2048]{1,0:T(8,128)(2,1)S(1)}, bf16[512,2048]{1,0:T(8,128)(2,1)S(1)}, u32[]{:S(2)}, u32[]{:S(2)}) collective-permute-start(bf16[512,2048]{1,0:T(8,128)(2,1)S(1)} %get-tuple-element.54), channel_id=1, source_target_pairs={{0,16},{8,24},{16,0},{24,8},{1,17},{9,25},{17,1},{25,9},{2,18},{10... | collective-permute-start | bytes 6291464 | tf_op jit(solution)/shard_map/ppermute | solution.py:628
  554.4 22.2 %collective-permute-start.16 = (bf16[256,2048]{1,0:T(8,128)(2,1)S(1)}, bf16[256,2048]{1,0:T(8,128)(2,1)S(1)}, u32[]{:S(2)}, u32[]{:S(2)}) collective-permute-start(bf16[256,2048]{1,0:T(8,128)(2,1)S(1)} %slice.252), channel_id=1, source_target_pairs={{0,16},{8,24},{16,0},{24,8},{1,17},{9,25},{17,1},{25,9},{2,18},{10... | collective-permute-start | bytes 3145736 | tf_op jit(solution)/shard_map/ppermute | solution.py:628
  581.8 212.6 %reduce-scatter.9.cloned.1.call-start = ((), (), s32[]{:S(2)}) async-start(), calls=%async_computation.9 | async-start | bytes 7077888 | tf_op jit(solution)/shard_map/reduce_scatter | solution.py:671
  688.7 146.5 %reduce-scatter.11.cloned.1.call-start = ((), (), s32[]{:S(2)}) async-start(), calls=%async_computation.10 | async-start | bytes 2359296 | tf_op jit(solution)/shard_map/reduce_scatter | solution.py:677
  (51 other events, 456.7 us)
Sparse Core Ops, SparseCore 0:
  48.7 65.8 all-gather.3
  124.6 83.7 all-gather.5
  210.0 80.6 all-gather.7
  476.9 86.4 reduce-scatter.4
  582.0 87.4 reduce-scatter.6
  688.8 68.1 reduce-scatter.8
  794.6 35.2 reduce-scatter.10

commit v7 on v6

--- a/solution.py
+++ b/solution.py
@@ -747,7 +747,7 @@
         projected_back = projected_back.reshape(total, -1)
         result = middle + over_plan([down_terms[0], down_terms[1]] + [result_terms[spot] for spot in range(2, landings(seq))])
         outputs = (result * live).astype(BF).reshape(slots, block, model)
-        in_sum = rows_product(after(normed, (summed_up, outputs)), projected_back)
+        in_sum = rows_product(after(normed, outputs), projected_back)
         summed_in = scatter_columns(in_sum)
         one_terms, swapped_up = send_back(seq, plan, after(projected_back, in_sum), matrix_in, summed_up)
         upward_delta = jnp.concatenate([swapped_up[step] for step in range(seq)], axis=1).astype(F32)

time: 855 us -> 842 us (0.985)
    unnamed x121 -> x125, local copies, waits for them, and re-layouts: 30 us -> 29.7 us
  transfers between devices with their start and end apart: 25 -> 25, of which waited for: 13 -> 12; matrix products, arithmetic and copies ran while one was open for 17% -> 18% of each run, Pallas kernels for 23% -> 23%
where the time goes in v7:
time: 842 us; the launch traced here: 834 us
  Pallas kernels  383 us (45%)
  waiting for transfers between devices  207 us (25%)
  matrix products  89.6 us (11%)
  other arithmetic  71.5 us (8%)
  local copies, waits for them, and re-layouts  45.5 us (5%)
  starting transfers between devices  21.5 us (3%)
  between operations  16.4 us (2%)
    ppermute x18, waiting for transfers between devices, shift(): return lax.ppermute(values, 'seq', pairs)  205 us
    pallas_call x1, Pallas kernels, forward_back(): pl.pallas_call(functools.partial(forward_back_kernel, seq, math.gcd(512,...  156 us
    pallas_call x1, Pallas kernels, send_back(): pl.pallas_call(functools.partial(send_back_kernel, seq, plan, math.gcd(51...  88.2 us
    pallas_call x1, Pallas kernels, attend_back(): pl.pallas_call(functools.partial(attend_back_kernel, scaling, plan), out_...  70.9 us
    dot_general x4, matrix products, rows_product(): lax.dot_general(left, right, (((0,), (0,)), ((), ())), preferred_element_...  65.5 us
    pallas_call x1, Pallas kernels, opening(): pl.pallas_call(functools.partial(opening_kernel, seq, dp), out_shape=(jax...  32.8 us
    unnamed x125, local copies, waits for them, and re-layouts  29.7 us
    ppermute x18, starting transfers between devices, shift(): return lax.ppermute(values, 'seq', pairs)  21.3 us
  transfers between devices with their start and end apart: 25, of which 12 were waited for; matrix products, arithmetic and copies ran while one was open for 18% of the time, Pallas kernels for 23%

profile of v7, /device:TPU:0, one launch (start us, length us, event | category | flops | bytes accessed | tf_op | source)
XLA Modules:
  0.0 834.4 jit_solution(6883151620289554309)
XLA Ops:
  15.7 32.8 %opening.1 = (bf16[4,64,1536]{2,1,0:T(8,128)(2,1)}, bf16[4,64,2048]{2,1,0:T(8,128)(2,1)}, f32[8,4,8,128]{3,2,1,0:T(8,128)}, bf16[8,64,2048]{2,1,0:T(8,128)(2,1)}) custom-call(bf16[4,64,1536]{2,1,0:T(8,128)(2,1)} %reshape.346.pieces, bf16[4,64,2048]{2,1,0:T(8,128)(2,1)} %bitcast.166, f32[8,128]{1,0:T(8,128)} %bitcast_convert_fusion.small, bf16[64,2048]{1,0:T(8,128)(2,1)} %shard.1), custom_call_target="tpu_custom_call" | custom-call | tf_op jit(solution)/shard_map/opening/pallas_call | solution.py:132
  50.8 45.5 %collective-permute-done = bf16[512,2048]{1,0:T(8,128)(2,1)S(1)} collective-permute-done((bf16[512,2048]{1,0:T(8,128)(2,1)S(1)}, bf16[512,2048]{1,0:T(8,128)(2,1)S(1)}, u32[]{:S(2)}, u32[]{:S(2)}) %collective-permute-start) | collective-permute-done | bytes 2097184 | tf_op jit(solution)/shard_map/ppermute | solution.py:628
  100.1 20.9 %collective-permute-done.2 = bf16[256,2048]{1,0:T(8,128)(2,1)S(1)} collective-permute-done((bf16[256,2048]{1,0:T(8,128)(2,1)S(1)}, bf16[256,2048]{1,0:T(8,128)(2,1)S(1)}, u32[]{:S(2)}, u32[]{:S(2)}) %collective-permute-start.2) | collective-permute-done | bytes 1048608 | tf_op jit(solution)/shard_map/ppermute | solution.py:628
  137.4 5.2 fusion.30
  159.4 19.8 %attend.1 = bf16[4,2,256,512]{3,2,1,0:T(8,128)(2,1)S(1)} custom-call(s32[4]{0:T(128)S(1)} %iota_xor_fusion.where, bf16[4,2,256,1536]{3,2,1,0:T(8,128)(2,1)} %bitcast.160), custom_call_target="tpu_custom_call" | custom-call | bytes 62914560 | tf_op jit(solution)/shard_map/attend/pallas_call | solution.py:253
  185.1 21.2 %collective-permute-done.5 = bf16[256,2048]{1,0:T(8,128)(2,1)} collective-permute-done((bf16[256,2048]{1,0:T(8,128)(2,1)S(1)}, bf16[256,2048]{1,0:T(8,128)(2,1)}, u32[]{:S(2)}, u32[]{:S(2)}) %collective-permute-start.5) | collective-permute-done | bytes 1048608 | tf_op jit(solution)/shard_map/ppermute | solution.py:628
  231.4 14.4 %collective-permute-done.12 = bf16[256,2048]{1,0:T(8,128)(2,1)S(1)} collective-permute-done((bf16[256,2048]{1,0:T(8,128)(2,1)S(1)}, bf16[256,2048]{1,0:T(8,128)(2,1)S(1)}, u32[]{:S(2)}, u32[]{:S(2)}) %collective-permute-start.12) | collective-permute-done | bytes 1048608 | tf_op jit(solution)/shard_map/ppermute | solution.py:628
  247.3 22.3 %collective-permute-done.4 = bf16[256,2048]{1,0:T(8,128)(2,1)S(1)} collective-permute-done((bf16[256,2048]{1,0:T(8,128)(2,1)S(1)}, bf16[256,2048]{1,0:T(8,128)(2,1)S(1)}, u32[]{:S(2)}, u32[]{:S(2)}) %collective-permute-start.4) | collective-permute-done | bytes 1048608 | tf_op jit(solution)/shard_map/ppermute | solution.py:628
  269.6 20.4 %collective-permute-done.6 = bf16[256,2048]{1,0:T(8,128)(2,1)S(1)} collective-permute-done((bf16[256,2048]{1,0:T(8,128)(2,1)S(1)}, bf16[256,2048]{1,0:T(8,128)(2,1)S(1)}, u32[]{:S(2)}, u32[]{:S(2)}) %collective-permute-start.6) | collective-permute-done | bytes 1048608 | tf_op jit(solution)/shard_map/ppermute | solution.py:628
  297.1 156.0 %forward_back.1 = (bf16[8,256,2048]{2,1,0:T(8,128)(2,1)}, bf16[8,256,2048]{2,1,0:T(8,128)(2,1)}, bf16[8,256,2048]{2,1,0:T(8,128)(2,1)}, bf16[8,256,2048]{2,1,0:T(8,128)(2,1)}, bf16[6,256,2048]{2,1,0:T(8,128)(2,1)}) custom-call(bf16[512,2048]{1,0:T(8,128)(2,1)} %add_convert_fusion.mine, bf16[8,256,2048]{2,1,0:T(8,128)(2,1)} %copy-done.36, ...), custom_call_target="tpu_custom_call" | custom-call | flops 68719476736 | bytes 419430400 | tf_op jit(solution)/shard_map/forward_back/pallas_call | solution.py:525
  453.1 23.8 %convolution_bitcast_fusion = bf16[2048,2048]{1,0:T(8,128)(2,1)} fusion(bf16[8,256,2048]{2,1,0:T(8,128)(2,1)} %get-tuple-element.51, bf16[8,256,2048]{2,1,0:T(8,128)(2,1)} %copy-done.36), kind=kOutput, calls=%fused_computation | convolution fusion | flops 17179869184 | bytes 25165824 | tf_op jit(solution)/shard_map/dot_general | solution.py:34
  477.0 4.7 fusion.45
  488.5 20.6 %fusion.63 = bf16[2048,2048]{1,0:T(8,128)(2,1)} fusion(bf16[2048,2048]{1,0:T(8,128)(2,1)S(1)} %bitcast.206, bf16[2048,2048]{1,0:T(8,128)(2,1)S(1)} %bitcast.209), kind=kOutput, calls=%fused_computation.164 | convolution fusion | flops 17179869184 | bytes 25165824 | tf_op jit(solution)/shard_map/dot_general | solution.py:34
  510.9 43.5 %collective-permute-done.14 = bf16[512,2048]{1,0:T(8,128)(2,1)S(1)} collective-permute-done((bf16[512,2048]{1,0:T(8,128)(2,1)S(1)}, bf16[512,2048]{1,0:T(8,128)(2,1)S(1)}, u32[]{:S(2)}, u32[]{:S(2)}) %collective-permute-start.14) | collective-permute-done | bytes 2097184 | tf_op jit(solution)/shard_map/ppermute | solution.py:628
  562.5 14.3 %collective-permute-done.16 = bf16[256,2048]{1,0:T(8,128)(2,1)S(1)} collective-permute-done((bf16[256,2048]{1,0:T(8,128)(2,1)S(1)}, bf16[256,2048]{1,0:T(8,128)(2,1)S(1)}, u32[]{:S(2)}, u32[]{:S(2)}) %collective-permute-start.16) | collective-permute-done | bytes 1048608 | tf_op jit(solution)/shard_map/ppermute | solution.py:628
  582.1 5.4 pad_maximum_fusion
  587.6 70.9 %attend_back.1 = (bf16[4,2,256,1536]{3,2,1,0:T(8,128)(2,1)}, bf16[6,256,2048]{2,1,0:T(8,128)(2,1)}) custom-call(bf16[4,2,256,1536]{3,2,1,0:T(8,128)(2,1)} %bitcast.161, bf16[4,2,256,512]{3,2,1,0:T(8,128)(2,1)S(1)} %bitcast.154, bf16[8,256,2048]{2,1,0:T(8,128)(2,1)} %get-tuple-element.48.terms), custom_call_target="tpu_custom_call" | custom-call | bytes 251658240 | tf_op jit(solution)/shard_map/attend_back/pallas_call | solution.py:396
  658.5 4.2 add_bitcast_fusion.1
  665.5 15.1 %fusion.64 = bf16[2048,1536]{1,0:T(8,128)(2,1)} fusion(bf16[2048,2048]{1,0:T(8,128)(2,1)S(1)} %pad_maximum_fusion, bf16[2048,1536]{1,0:T(8,128)(2,1)S(1)} %bitcast.203), kind=kOutput, calls=%fused_computation.165 | convolution fusion | flops 12884901888 | bytes 20971520 | tf_op jit(solution)/shard_map/dot_general | solution.py:34
  688.5 6.0 fusion.65
  695.8 88.2 %send_back.1 = (bf16[6,256,2048]{2,1,0:T(8,128)(2,1)S(1)}, bf16[4,64,2048]{2,1,0:T(8,128)(2,1)S(1)}) custom-call(bf16[8,256,1536]{2,1,0:T(8,128)(2,1)} %bitcast.200, bf16[2048,1536]{1,0:T(8,128)(2,1)} %bitcast.193, bf16[4,64,2048]{2,1,0:T(8,128)(2,1)S(1)} %copy-done.3), custom_call_target="tpu_custom_call" | custom-call | flops 12884901888 | bytes 251658240 | tf_op jit(solution)/shard_map/send_back/pallas_call | solution.py:597
  786.7 6.1 fusion.49
  799.2 15.2 %closing.1 = (f32[8,128]{1,0:T(8,128)}, f32[64,6144]{1,0:T(8,128)}) custom-call(f32[4,8,8,128]{3,2,1,0:T(8,128)} %copy.42, bf16[4,64,1536]{2,1,0:T(8,128)(2,1)} %reduce-scatter.9.cloned.1.call-done.pieces), custom_call_target="tpu_custom_call" | custom-call | tf_op jit(solution)/shard_map/closing/pallas_call | solution.py:199
  815.8 7.0 fusion.35
  (275 shorter events, 134.6 us)
Async XLA Ops:
  7.2 117.3 %all-gather.4.cloned.1.call-start = ((), (), s32[]{:S(2)}) async-start(), calls=%async_computation.4 | async-start | bytes 7077888 | tf_op jit(solution)/shard_map/all_gather | solution.py:666
  48.6 159.8 %all-gather.6.cloned.1.call-start = ((), (), s32[]{:S(2)}) async-start(), calls=%async_computation.5 | async-start | bytes 9437184 | tf_op jit(solution)/shard_map/all_gather | solution.py:666
  48.6 47.7 %collective-permute-start = (bf16[512,2048]{1,0:T(8,128)(2,1)S(1)}, bf16[512,2048]{1,0:T(8,128)(2,1)S(1)}, u32[]{:S(2)}, u32[]{:S(2)}) collective-permute-start(bf16[512,2048]{1,0:T(8,128)(2,1)S(1)} %bitcast.155), channel_id=1, source_target_pairs={{0,8},{8,0},{16,24},{24,16},{1,9},{9,1},{17,25},{25,17},{2,10},{10... | collective-permute-start | bytes 6291464 | tf_op jit(solution)/shard_map/ppermute | solution.py:628
  49.7 47.9 %collective-permute-start.1 = (bf16[512,2048]{1,0:T(8,128)(2,1)S(1)}, bf16[512,2048]{1,0:T(8,128)(2,1)S(1)}, u32[]{:S(2)}, u32[]{:S(2)}) collective-permute-start(bf16[512,2048]{1,0:T(8,128)(2,1)S(1)} %bitcast.156), channel_id=1, source_target_pairs={{0,16},{8,24},{16,0},{24,8},{1,17},{9,25},{17,1},{25,9},{2,18},{10... | collective-permute-start | bytes 6291464 | tf_op jit(solution)/shard_map/ppermute | solution.py:628
  96.4 24.5 %collective-permute-start.2 = (bf16[256,2048]{1,0:T(8,128)(2,1)S(1)}, bf16[256,2048]{1,0:T(8,128)(2,1)S(1)}, u32[]{:S(2)}, u32[]{:S(2)}) collective-permute-start(bf16[256,2048]{1,0:T(8,128)(2,1)S(1)} %slice.234), channel_id=1, source_target_pairs={{0,16},{8,24},{16,0},{24,8},{1,17},{9,25},{17,1},{25,9},{2,18},{10... | collective-permute-start | bytes 3145736 | tf_op jit(solution)/shard_map/ppermute | solution.py:628
  99.0 24.4 %collective-permute-start.3 = (bf16[256,2048]{1,0:T(8,128)(2,1)S(1)}, bf16[256,2048]{1,0:T(8,128)(2,1)S(1)}, u32[]{:S(2)}, u32[]{:S(2)}) collective-permute-start(bf16[256,2048]{1,0:T(8,128)(2,1)S(1)} %slice.235), channel_id=1, source_target_pairs={{0,8},{8,0},{16,24},{24,16},{1,9},{9,1},{17,25},{25,17},{2,10},{10... | collective-permute-start | bytes 3145736 | tf_op jit(solution)/shard_map/ppermute | solution.py:628
  124.5 172.6 %all-gather.8.cloned.1.call-start = ((), (), s32[]{:S(2)}) async-start(), calls=%async_computation.6 | async-start | bytes 9437184 | tf_op jit(solution)/shard_map/all_gather | solution.py:719
  130.1 55.1 %collective-permute-start.10 = (bf16[512,2048]{1,0:T(8,128)(2,1)S(1)}, bf16[512,2048]{1,0:T(8,128)(2,1)}, u32[]{:S(2)}, u32[]{:S(2)}) collective-permute-start(bf16[512,2048]{1,0:T(8,128)(2,1)S(1)} %fusion.38), channel_id=1, source_target_pairs={{0,8},{8,0},{16,24},{24,16},{1,9},{9,1},{17,25},{25,17},{2,10},{10... | collective-permute-start | bytes 6291464 | tf_op jit(solution)/shard_map/ppermute | solution.py:628
  131.3 53.8 %collective-permute-start.11 = (bf16[512,2048]{1,0:T(8,128)(2,1)S(1)}, bf16[512,2048]{1,0:T(8,128)(2,1)}, u32[]{:S(2)}, u32[]{:S(2)}) collective-permute-start(bf16[512,2048]{1,0:T(8,128)(2,1)S(1)} %fusion.38), channel_id=1, source_target_pairs={{0,16},{8,24},{16,0},{24,8},{1,17},{9,25},{17,1},{25,9},{2,18},{10... | collective-permute-start | bytes 6291464 | tf_op jit(solution)/shard_map/ppermute | solution.py:628
  183.3 23.0 %collective-permute-start.5 = (bf16[256,2048]{1,0:T(8,128)(2,1)S(1)}, bf16[256,2048]{1,0:T(8,128)(2,1)}, u32[]{:S(2)}, u32[]{:S(2)}) collective-permute-start(bf16[256,2048]{1,0:T(8,128)(2,1)S(1)} %get-tuple-element.91), channel_id=1, source_target_pairs={{0,8},{8,0},{16,24},{24,16},{1,9},{9,1},{17,25},{25,17},{2,10},{10... | collective-permute-start | bytes 3145736 | tf_op jit(solution)/shard_map/ppermute | solution.py:628
  184.2 22.6 %collective-permute-start.7 = (bf16[256,2048]{1,0:T(8,128)(2,1)S(1)}, bf16[256,2048]{1,0:T(8,128)(2,1)}, u32[]{:S(2)}, u32[]{:S(2)}) collective-permute-start(bf16[256,2048]{1,0:T(8,128)(2,1)S(1)} %get-tuple-element.92), channel_id=1, source_target_pairs={{0,16},{8,24},{16,0},{24,8},{1,17},{9,25},{17,1},{25,9},{2,18},{10... | collective-permute-start | bytes 3145736 | tf_op jit(solution)/shard_map/ppermute | solution.py:628
  208.4 370.9 %reduce-scatter.5.cloned.1.call-start = ((), (), s32[]{:S(2)}) async-start(), calls=%async_computation.7 | async-start | bytes 9437184 | tf_op jit(solution)/shard_map/reduce_scatter | solution.py:677
  219.7 26.1 %collective-permute-start.12 = (bf16[256,2048]{1,0:T(8,128)(2,1)S(1)}, bf16[256,2048]{1,0:T(8,128)(2,1)S(1)}, u32[]{:S(2)}, u32[]{:S(2)}) collective-permute-start(bf16[256,2048]{1,0:T(8,128)(2,1)S(1)} %slice.248), channel_id=1, source_target_pairs={{0,16},{8,24},{16,0},{24,8},{1,17},{9,25},{17,1},{25,9},{2,18},{10... | collective-permute-start | bytes 3145736 | tf_op jit(solution)/shard_map/ppermute | solution.py:628
  221.2 26.1 %collective-permute-start.13 = (bf16[256,2048]{1,0:T(8,128)(2,1)S(1)}, bf16[256,2048]{1,0:T(8,128)(2,1)S(1)}, u32[]{:S(2)}, u32[]{:S(2)}) collective-permute-start(bf16[256,2048]{1,0:T(8,128)(2,1)S(1)} %slice.251), channel_id=1, source_target_pairs={{0,8},{8,0},{16,24},{24,16},{1,9},{9,1},{17,25},{25,17},{2,10},{10... | collective-permute-start | bytes 3145736 | tf_op jit(solution)/shard_map/ppermute | solution.py:628
  225.3 44.4 %collective-permute-start.4 = (bf16[256,2048]{1,0:T(8,128)(2,1)S(1)}, bf16[256,2048]{1,0:T(8,128)(2,1)S(1)}, u32[]{:S(2)}, u32[]{:S(2)}) collective-permute-start(bf16[256,2048]{1,0:T(8,128)(2,1)S(1)} %slice.238), channel_id=1, source_target_pairs={{0,8},{8,0},{16,24},{24,16},{1,9},{9,1},{17,25},{25,17},{2,10},{10... | collective-permute-start | bytes 3145736 | tf_op jit(solution)/shard_map/ppermute | solution.py:628
  226.0 64.4 %collective-permute-start.9 = (bf16[256,2048]{1,0:T(8,128)(2,1)S(1)}, bf16[256,2048]{1,0:T(8,128)(2,1)S(1)}, u32[]{:S(2)}, u32[]{:S(2)}) collective-permute-start(bf16[256,2048]{1,0:T(8,128)(2,1)S(1)} %slice.245), channel_id=1, source_target_pairs={{0,16},{8,24},{16,0},{24,8},{1,17},{9,25},{17,1},{25,9},{2,18},{10... | collective-permute-start | bytes 3145736 | tf_op jit(solution)/shard_map/ppermute | solution.py:628
  228.3 61.7 %collective-permute-start.6 = (bf16[256,2048]{1,0:T(8,128)(2,1)S(1)}, bf16[256,2048]{1,0:T(8,128)(2,1)S(1)}, u32[]{:S(2)}, u32[]{:S(2)}) collective-permute-start(bf16[256,2048]{1,0:T(8,128)(2,1)S(1)} %add_convert_fusion.2), channel_id=1, source_target_pairs={{0,16},{8,24},{16,0},{24,8},{1,17},{9,25},{17,1},{25,9},{2,18},{10... | collective-permute-start | bytes 3145736 | tf_op jit(solution)/shard_map/ppermute | solution.py:628
  245.7 45.4 %collective-permute-start.8 = (bf16[256,2048]{1,0:T(8,128)(2,1)S(1)}, bf16[256,2048]{1,0:T(8,128)(2,1)S(1)}, u32[]{:S(2)}, u32[]{:S(2)}) collective-permute-start(bf16[256,2048]{1,0:T(8,128)(2,1)S(1)} %add_convert_fusion.1), channel_id=1, source_target_pairs={{0,8},{8,0},{16,24},{24,16},{1,9},{9,1},{17,25},{25,17},{2,10},{10... | collective-permute-start | bytes 3145736 | tf_op jit(solution)/shard_map/ppermute | solution.py:628
  476.9 217.6 %reduce-scatter.7.cloned.1.call-start = ((), (), s32[]{:S(2)}) async-start(), calls=%async_computation.8 | async-start | bytes 9437184 | tf_op jit(solution)/shard_map/reduce_scatter | solution.py:671
  509.1 45.3 %collective-permute-start.14 = (bf16[512,2048]{1,0:T(8,128)(2,1)S(1)}, bf16[512,2048]{1,0:T(8,128)(2,1)S(1)}, u32[]{:S(2)}, u32[]{:S(2)}) collective-permute-start(bf16[512,2048]{1,0:T(8,128)(2,1)S(1)} %get-tuple-element.54), channel_id=1, source_target_pairs={{0,8},{8,0},{16,24},{24,16},{1,9},{9,1},{17,25},{25,17},{2,10},{10... | collective-permute-start | bytes 6291464 | tf_op jit(solution)/shard_map/ppermute | solution.py:628
  509.9 44.7 %collective-permute-start.15 = (bf16[512,2048]{1,0:T(8,128)(2,1)S(1)}, bf16[512,2048]{1,0:T(8,128)(2,1)S(1)}, u32[]{:S(2)}, u32[]{:S(2)}) collective-permute-start(bf16[512,2048]{1,0:T(8,128)(2,1)S(1)} %get-tuple-element.54), channel_id=1, source_target_pairs={{0,16},{8,24},{16,0},{24,8},{1,17},{9,25},{17,1},{25,9},{2,18},{10... | collective-permute-start | bytes 6291464 | tf_op jit(solution)/shard_map/ppermute | solution.py:628
  554.5 22.3 %collective-permute-start.16 = (bf16[256,2048]{1,0:T(8,128)(2,1)S(1)}, bf16[256,2048]{1,0:T(8,128)(2,1)S(1)}, u32[]{:S(2)}, u32[]{:S(2)}) collective-permute-start(bf16[256,2048]{1,0:T(8,128)(2,1)S(1)} %slice.252), channel_id=1, source_target_pairs={{0,16},{8,24},{16,0},{24,8},{1,17},{9,25},{17,1},{25,9},{2,18},{10... | collective-permute-start | bytes 3145736 | tf_op jit(solution)/shard_map/ppermute | solution.py:628
  582.1 204.6 %reduce-scatter.9.cloned.1.call-start = ((), (), s32[]{:S(2)}) async-start(), calls=%async_computation.9 | async-start | bytes 7077888 | tf_op jit(solution)/shard_map/reduce_scatter | solution.py:671
  680.7 143.6 %reduce-scatter.11.cloned.1.call-start = ((), (), s32[]{:S(2)}) async-start(), calls=%async_computation.10 | async-start | bytes 2359296 | tf_op jit(solution)/shard_map/reduce_scatter | solution.py:677
  (53 other events, 460.3 us)
Sparse Core Ops, SparseCore 0:
  48.7 65.8 all-gather.3
  124.6 83.7 all-gather.5
  210.0 80.5 all-gather.7
  477.0 86.1 reduce-scatter.4
  582.2 87.1 reduce-scatter.6
  680.8 66.9 reduce-scatter.8
  786.8 33.2 reduce-scatter.10

commit v8 on v7

--- a/solution.py
+++ b/solution.py
@@ -523,7 +523,7 @@
     whole = lambda shape: pl.BlockSpec(shape, lambda step: (0, 0), pipeline_mode=pl.Buffered(1))
     shape = lambda columns: jax.ShapeDtypeStruct((steps, rows, columns), BF)
     return pl.pallas_call(
-        functools.partial(forward_back_kernel, seq, math.gcd(512, math.gcd(width, model))),
+        functools.partial(forward_back_kernel, seq, math.gcd(1024, math.gcd(width, model))),
         out_shape=[shape(model), shape(width), shape(width), shape(model)]
         + [jax.ShapeDtypeStruct((landings(seq), rows, model), BF)],
         grid=(steps,),

time: 842 us -> 841 us (level)
  no operation moved by 1% of the time
where the time goes in v8:
time: 841 us; the launch traced here: 834 us
  Pallas kernels  382 us (45%)
  waiting for transfers between devices  207 us (25%)
  matrix products  89.6 us (11%)
  other arithmetic  71.6 us (9%)
  local copies, waits for them, and re-layouts  45.5 us (5%)
  starting transfers between devices  21.5 us (3%)
  between operations  16.4 us (2%)
    ppermute x18, waiting for transfers between devices, shift(): return lax.ppermute(values, 'seq', pairs)  205 us
    pallas_call x1, Pallas kernels, forward_back(): pl.pallas_call(functools.partial(forward_back_kernel, seq, math.gcd(1024,...  155 us
    pallas_call x1, Pallas kernels, send_back(): pl.pallas_call(functools.partial(send_back_kernel, seq, plan, math.gcd(51...  88.2 us
    pallas_call x1, Pallas kernels, attend_back(): pl.pallas_call(functools.partial(attend_back_kernel, scaling, plan), out_...  70.9 us
    dot_general x4, matrix products, rows_product(): lax.dot_general(left, right, (((0,), (0,)), ((), ())), preferred_element_...  65.5 us
    pallas_call x1, Pallas kernels, opening(): pl.pallas_call(functools.partial(opening_kernel, seq, dp), out_shape=(jax...  32.8 us
    unnamed x125, local copies, waits for them, and re-layouts  29.7 us
    ppermute x18, starting transfers between devices, shift(): return lax.ppermute(values, 'seq', pairs)  21.2 us
  transfers between devices with their start and end apart: 25, of which 12 were waited for; matrix products, arithmetic and copies ran while one was open for 18% of the time, Pallas kernels for 23%

profile of v8, /device:TPU:0, one launch (start us, length us, event | category | flops | bytes accessed | tf_op | source)
XLA Modules:
  0.0 833.6 jit_solution(11443573618817343050)
XLA Ops:
  15.7 32.8 %opening.1 = (bf16[4,64,1536]{2,1,0:T(8,128)(2,1)}, bf16[4,64,2048]{2,1,0:T(8,128)(2,1)}, f32[8,4,8,128]{3,2,1,0:T(8,128)}, bf16[8,64,2048]{2,1,0:T(8,128)(2,1)}) custom-call(bf16[4,64,1536]{2,1,0:T(8,128)(2,1)} %reshape.346.pieces, bf16[4,64,2048]{2,1,0:T(8,128)(2,1)} %bitcast.166, f32[8,128]{1,0:T(8,128)} %bitcast_convert_fusion.small, bf16[64,2048]{1,0:T(8,128)(2,1)} %shard.1), custom_call_target="tpu_custom_call" | custom-call | tf_op jit(solution)/shard_map/opening/pallas_call | solution.py:132
  50.8 45.5 %collective-permute-done = bf16[512,2048]{1,0:T(8,128)(2,1)S(1)} collective-permute-done((bf16[512,2048]{1,0:T(8,128)(2,1)S(1)}, bf16[512,2048]{1,0:T(8,128)(2,1)S(1)}, u32[]{:S(2)}, u32[]{:S(2)}) %collective-permute-start) | collective-permute-done | bytes 2097184 | tf_op jit(solution)/shard_map/ppermute | solution.py:628
  100.1 20.9 %collective-permute-done.2 = bf16[256,2048]{1,0:T(8,128)(2,1)S(1)} collective-permute-done((bf16[256,2048]{1,0:T(8,128)(2,1)S(1)}, bf16[256,2048]{1,0:T(8,128)(2,1)S(1)}, u32[]{:S(2)}, u32[]{:S(2)}) %collective-permute-start.2) | collective-permute-done | bytes 1048608 | tf_op jit(solution)/shard_map/ppermute | solution.py:628
  137.4 5.2 fusion.30
  159.4 19.8 %attend.1 = bf16[4,2,256,512]{3,2,1,0:T(8,128)(2,1)S(1)} custom-call(s32[4]{0:T(128)S(1)} %iota_xor_fusion.where, bf16[4,2,256,1536]{3,2,1,0:T(8,128)(2,1)} %bitcast.160), custom_call_target="tpu_custom_call" | custom-call | bytes 62914560 | tf_op jit(solution)/shard_map/attend/pallas_call | solution.py:253
  185.1 21.2 %collective-permute-done.5 = bf16[256,2048]{1,0:T(8,128)(2,1)} collective-permute-done((bf16[256,2048]{1,0:T(8,128)(2,1)S(1)}, bf16[256,2048]{1,0:T(8,128)(2,1)}, u32[]{:S(2)}, u32[]{:S(2)}) %collective-permute-start.5) | collective-permute-done | bytes 1048608 | tf_op jit(solution)/shard_map/ppermute | solution.py:628
  231.4 14.4 %collective-permute-done.12 = bf16[256,2048]{1,0:T(8,128)(2,1)S(1)} collective-permute-done((bf16[256,2048]{1,0:T(8,128)(2,1)S(1)}, bf16[256,2048]{1,0:T(8,128)(2,1)S(1)}, u32[]{:S(2)}, u32[]{:S(2)}) %collective-permute-start.12) | collective-permute-done | bytes 1048608 | tf_op jit(solution)/shard_map/ppermute | solution.py:628
  247.3 22.3 %collective-permute-done.4 = bf16[256,2048]{1,0:T(8,128)(2,1)S(1)} collective-permute-done((bf16[256,2048]{1,0:T(8,128)(2,1)S(1)}, bf16[256,2048]{1,0:T(8,128)(2,1)S(1)}, u32[]{:S(2)}, u32[]{:S(2)}) %collective-permute-start.4) | collective-permute-done | bytes 1048608 | tf_op jit(solution)/shard_map/ppermute | solution.py:628
  269.6 20.4 %collective-permute-done.6 = bf16[256,2048]{1,0:T(8,128)(2,1)S(1)} collective-permute-done((bf16[256,2048]{1,0:T(8,128)(2,1)S(1)}, bf16[256,2048]{1,0:T(8,128)(2,1)S(1)}, u32[]{:S(2)}, u32[]{:S(2)}) %collective-permute-start.6) | collective-permute-done | bytes 1048608 | tf_op jit(solution)/shard_map/ppermute | solution.py:628
  297.1 155.2 %forward_back.1 = (bf16[8,256,2048]{2,1,0:T(8,128)(2,1)}, bf16[8,256,2048]{2,1,0:T(8,128)(2,1)}, bf16[8,256,2048]{2,1,0:T(8,128)(2,1)}, bf16[8,256,2048]{2,1,0:T(8,128)(2,1)}, bf16[6,256,2048]{2,1,0:T(8,128)(2,1)}) custom-call(bf16[512,2048]{1,0:T(8,128)(2,1)} %add_convert_fusion.mine, bf16[8,256,2048]{2,1,0:T(8,128)(2,1)} %copy-done.36, ...), custom_call_target="tpu_custom_call" | custom-call | flops 68719476736 | bytes 419430400 | tf_op jit(solution)/shard_map/forward_back/pallas_call | solution.py:525
  452.3 23.8 %convolution_bitcast_fusion = bf16[2048,2048]{1,0:T(8,128)(2,1)} fusion(bf16[8,256,2048]{2,1,0:T(8,128)(2,1)} %get-tuple-element.51, bf16[8,256,2048]{2,1,0:T(8,128)(2,1)} %copy-done.36), kind=kOutput, calls=%fused_computation | convolution fusion | flops 17179869184 | bytes 25165824 | tf_op jit(solution)/shard_map/dot_general | solution.py:34
  476.2 4.7 fusion.45
  487.7 20.6 %fusion.63 = bf16[2048,2048]{1,0:T(8,128)(2,1)} fusion(bf16[2048,2048]{1,0:T(8,128)(2,1)S(1)} %bitcast.206, bf16[2048,2048]{1,0:T(8,128)(2,1)S(1)} %bitcast.209), kind=kOutput, calls=%fused_computation.164 | convolution fusion | flops 17179869184 | bytes 25165824 | tf_op jit(solution)/shard_map/dot_general | solution.py:34
  510.1 43.5 %collective-permute-done.14 = bf16[512,2048]{1,0:T(8,128)(2,1)S(1)} collective-permute-done((bf16[512,2048]{1,0:T(8,128)(2,1)S(1)}, bf16[512,2048]{1,0:T(8,128)(2,1)S(1)}, u32[]{:S(2)}, u32[]{:S(2)}) %collective-permute-start.14) | collective-permute-done | bytes 2097184 | tf_op jit(solution)/shard_map/ppermute | solution.py:628
  561.7 14.3 %collective-permute-done.16 = bf16[256,2048]{1,0:T(8,128)(2,1)S(1)} collective-permute-done((bf16[256,2048]{1,0:T(8,128)(2,1)S(1)}, bf16[256,2048]{1,0:T(8,128)(2,1)S(1)}, u32[]{:S(2)}, u32[]{:S(2)}) %collective-permute-start.16) | collective-permute-done | bytes 1048608 | tf_op jit(solution)/shard_map/ppermute | solution.py:628
  581.3 5.4 pad_maximum_fusion
  586.8 70.9 %attend_back.1 = (bf16[4,2,256,1536]{3,2,1,0:T(8,128)(2,1)}, bf16[6,256,2048]{2,1,0:T(8,128)(2,1)}) custom-call(bf16[4,2,256,1536]{3,2,1,0:T(8,128)(2,1)} %bitcast.161, bf16[4,2,256,512]{3,2,1,0:T(8,128)(2,1)S(1)} %bitcast.154, bf16[8,256,2048]{2,1,0:T(8,128)(2,1)} %get-tuple-element.48.terms), custom_call_target="tpu_custom_call" | custom-call | bytes 251658240 | tf_op jit(solution)/shard_map/attend_back/pallas_call | solution.py:396
  657.7 4.2 add_bitcast_fusion.1
  664.7 15.1 %fusion.64 = bf16[2048,1536]{1,0:T(8,128)(2,1)} fusion(bf16[2048,2048]{1,0:T(8,128)(2,1)S(1)} %pad_maximum_fusion, bf16[2048,1536]{1,0:T(8,128)(2,1)S(1)} %bitcast.203), kind=kOutput, calls=%fused_computation.165 | convolution fusion | flops 12884901888 | bytes 20971520 | tf_op jit(solution)/shard_map/dot_general | solution.py:34
  687.7 6.0 fusion.65
  695.0 88.2 %send_back.1 = (bf16[6,256,2048]{2,1,0:T(8,128)(2,1)S(1)}, bf16[4,64,2048]{2,1,0:T(8,128)(2,1)S(1)}) custom-call(bf16[8,256,1536]{2,1,0:T(8,128)(2,1)} %bitcast.200, bf16[2048,1536]{1,0:T(8,128)(2,1)} %bitcast.193, bf16[4,64,2048]{2,1,0:T(8,128)(2,1)S(1)} %copy-done.3), custom_call_target="tpu_custom_call" | custom-call | flops 12884901888 | bytes 251658240 | tf_op jit(solution)/shard_map/send_back/pallas_call | solution.py:597
  785.9 6.1 fusion.49
  798.4 15.2 %closing.1 = (f32[8,128]{1,0:T(8,128)}, f32[64,6144]{1,0:T(8,128)}) custom-call(f32[4,8,8,128]{3,2,1,0:T(8,128)} %copy.42, bf16[4,64,1536]{2,1,0:T(8,128)(2,1)} %reduce-scatter.9.cloned.1.call-done.pieces), custom_call_target="tpu_custom_call" | custom-call | tf_op jit(solution)/shard_map/closing/pallas_call | solution.py:199
  815.0 6.9 fusion.35
  (275 shorter events, 134.5 us)
Async XLA Ops:
  7.2 117.3 %all-gather.4.cloned.1.call-start = ((), (), s32[]{:S(2)}) async-start(), calls=%async_computation.4 | async-start | bytes 7077888 | tf_op jit(solution)/shard_map/all_gather | solution.py:666
  48.6 159.8 %all-gather.6.cloned.1.call-start = ((), (), s32[]{:S(2)}) async-start(), calls=%async_computation.5 | async-start | bytes 9437184 | tf_op jit(solution)/shard_map/all_gather | solution.py:666
  48.6 47.7 %collective-permute-start = (bf16[512,2048]{1,0:T(8,128)(2,1)S(1)}, bf16[512,2048]{1,0:T(8,128)(2,1)S(1)}, u32[]{:S(2)}, u32[]{:S(2)}) collective-permute-start(bf16[512,2048]{1,0:T(8,128)(2,1)S(1)} %bitcast.155), channel_id=1, source_target_pairs={{0,8},{8,0},{16,24},{24,16},{1,9},{9,1},{17,25},{25,17},{2,10},{10... | collective-permute-start | bytes 6291464 | tf_op jit(solution)/shard_map/ppermute | solution.py:628
  49.7 47.9 %collective-permute-start.1 = (bf16[512,2048]{1,0:T(8,128)(2,1)S(1)}, bf16[512,2048]{1,0:T(8,128)(2,1)S(1)}, u32[]{:S(2)}, u32[]{:S(2)}) collective-permute-start(bf16[512,2048]{1,0:T(8,128)(2,1)S(1)} %bitcast.156), channel_id=1, source_target_pairs={{0,16},{8,24},{16,0},{24,8},{1,17},{9,25},{17,1},{25,9},{2,18},{10... | collective-permute-start | bytes 6291464 | tf_op jit(solution)/shard_map/ppermute | solution.py:628
  96.4 24.5 %collective-permute-start.2 = (bf16[256,2048]{1,0:T(8,128)(2,1)S(1)}, bf16[256,2048]{1,0:T(8,128)(2,1)S(1)}, u32[]{:S(2)}, u32[]{:S(2)}) collective-permute-start(bf16[256,2048]{1,0:T(8,128)(2,1)S(1)} %slice.234), channel_id=1, source_target_pairs={{0,16},{8,24},{16,0},{24,8},{1,17},{9,25},{17,1},{25,9},{2,18},{10... | collective-permute-start | bytes 3145736 | tf_op jit(solution)/shard_map/ppermute | solution.py:628
  99.0 24.4 %collective-permute-start.3 = (bf16[256,2048]{1,0:T(8,128)(2,1)S(1)}, bf16[256,2048]{1,0:T(8,128)(2,1)S(1)}, u32[]{:S(2)}, u32[]{:S(2)}) collective-permute-start(bf16[256,2048]{1,0:T(8,128)(2,1)S(1)} %slice.235), channel_id=1, source_target_pairs={{0,8},{8,0},{16,24},{24,16},{1,9},{9,1},{17,25},{25,17},{2,10},{10... | collective-permute-start | bytes 3145736 | tf_op jit(solution)/shard_map/ppermute | solution.py:628
  124.5 172.6 %all-gather.8.cloned.1.call-start = ((), (), s32[]{:S(2)}) async-start(), calls=%async_computation.6 | async-start | bytes 9437184 | tf_op jit(solution)/shard_map/all_gather | solution.py:719
  130.1 55.1 %collective-permute-start.10 = (bf16[512,2048]{1,0:T(8,128)(2,1)S(1)}, bf16[512,2048]{1,0:T(8,128)(2,1)}, u32[]{:S(2)}, u32[]{:S(2)}) collective-permute-start(bf16[512,2048]{1,0:T(8,128)(2,1)S(1)} %fusion.38), channel_id=1, source_target_pairs={{0,8},{8,0},{16,24},{24,16},{1,9},{9,1},{17,25},{25,17},{2,10},{10... | collective-permute-start | bytes 6291464 | tf_op jit(solution)/shard_map/ppermute | solution.py:628
  131.3 53.8 %collective-permute-start.11 = (bf16[512,2048]{1,0:T(8,128)(2,1)S(1)}, bf16[512,2048]{1,0:T(8,128)(2,1)}, u32[]{:S(2)}, u32[]{:S(2)}) collective-permute-start(bf16[512,2048]{1,0:T(8,128)(2,1)S(1)} %fusion.38), channel_id=1, source_target_pairs={{0,16},{8,24},{16,0},{24,8},{1,17},{9,25},{17,1},{25,9},{2,18},{10... | collective-permute-start | bytes 6291464 | tf_op jit(solution)/shard_map/ppermute | solution.py:628
  183.3 23.0 %collective-permute-start.5 = (bf16[256,2048]{1,0:T(8,128)(2,1)S(1)}, bf16[256,2048]{1,0:T(8,128)(2,1)}, u32[]{:S(2)}, u32[]{:S(2)}) collective-permute-start(bf16[256,2048]{1,0:T(8,128)(2,1)S(1)} %get-tuple-element.91), channel_id=1, source_target_pairs={{0,8},{8,0},{16,24},{24,16},{1,9},{9,1},{17,25},{25,17},{2,10},{10... | collective-permute-start | bytes 3145736 | tf_op jit(solution)/shard_map/ppermute | solution.py:628
  184.2 22.6 %collective-permute-start.7 = (bf16[256,2048]{1,0:T(8,128)(2,1)S(1)}, bf16[256,2048]{1,0:T(8,128)(2,1)}, u32[]{:S(2)}, u32[]{:S(2)}) collective-permute-start(bf16[256,2048]{1,0:T(8,128)(2,1)S(1)} %get-tuple-element.92), channel_id=1, source_target_pairs={{0,16},{8,24},{16,0},{24,8},{1,17},{9,25},{17,1},{25,9},{2,18},{10... | collective-permute-start | bytes 3145736 | tf_op jit(solution)/shard_map/ppermute | solution.py:628
  208.4 370.1 %reduce-scatter.5.cloned.1.call-start = ((), (), s32[]{:S(2)}) async-start(), calls=%async_computation.7 | async-start | bytes 9437184 | tf_op jit(solution)/shard_map/reduce_scatter | solution.py:677
  219.7 26.1 %collective-permute-start.12 = (bf16[256,2048]{1,0:T(8,128)(2,1)S(1)}, bf16[256,2048]{1,0:T(8,128)(2,1)S(1)}, u32[]{:S(2)}, u32[]{:S(2)}) collective-permute-start(bf16[256,2048]{1,0:T(8,128)(2,1)S(1)} %slice.248), channel_id=1, source_target_pairs={{0,16},{8,24},{16,0},{24,8},{1,17},{9,25},{17,1},{25,9},{2,18},{10... | collective-permute-start | bytes 3145736 | tf_op jit(solution)/shard_map/ppermute | solution.py:628
  221.2 26.1 %collective-permute-start.13 = (bf16[256,2048]{1,0:T(8,128)(2,1)S(1)}, bf16[256,2048]{1,0:T(8,128)(2,1)S(1)}, u32[]{:S(2)}, u32[]{:S(2)}) collective-permute-start(bf16[256,2048]{1,0:T(8,128)(2,1)S(1)} %slice.251), channel_id=1, source_target_pairs={{0,8},{8,0},{16,24},{24,16},{1,9},{9,1},{17,25},{25,17},{2,10},{10... | collective-permute-start | bytes 3145736 | tf_op jit(solution)/shard_map/ppermute | solution.py:628
  225.3 44.4 %collective-permute-start.4 = (bf16[256,2048]{1,0:T(8,128)(2,1)S(1)}, bf16[256,2048]{1,0:T(8,128)(2,1)S(1)}, u32[]{:S(2)}, u32[]{:S(2)}) collective-permute-start(bf16[256,2048]{1,0:T(8,128)(2,1)S(1)} %slice.238), channel_id=1, source_target_pairs={{0,8},{8,0},{16,24},{24,16},{1,9},{9,1},{17,25},{25,17},{2,10},{10... | collective-permute-start | bytes 3145736 | tf_op jit(solution)/shard_map/ppermute | solution.py:628
  226.0 64.4 %collective-permute-start.9 = (bf16[256,2048]{1,0:T(8,128)(2,1)S(1)}, bf16[256,2048]{1,0:T(8,128)(2,1)S(1)}, u32[]{:S(2)}, u32[]{:S(2)}) collective-permute-start(bf16[256,2048]{1,0:T(8,128)(2,1)S(1)} %slice.245), channel_id=1, source_target_pairs={{0,16},{8,24},{16,0},{24,8},{1,17},{9,25},{17,1},{25,9},{2,18},{10... | collective-permute-start | bytes 3145736 | tf_op jit(solution)/shard_map/ppermute | solution.py:628
  228.3 61.7 %collective-permute-start.6 = (bf16[256,2048]{1,0:T(8,128)(2,1)S(1)}, bf16[256,2048]{1,0:T(8,128)(2,1)S(1)}, u32[]{:S(2)}, u32[]{:S(2)}) collective-permute-start(bf16[256,2048]{1,0:T(8,128)(2,1)S(1)} %add_convert_fusion.2), channel_id=1, source_target_pairs={{0,16},{8,24},{16,0},{24,8},{1,17},{9,25},{17,1},{25,9},{2,18},{10... | collective-permute-start | bytes 3145736 | tf_op jit(solution)/shard_map/ppermute | solution.py:628
  245.7 45.4 %collective-permute-start.8 = (bf16[256,2048]{1,0:T(8,128)(2,1)S(1)}, bf16[256,2048]{1,0:T(8,128)(2,1)S(1)}, u32[]{:S(2)}, u32[]{:S(2)}) collective-permute-start(bf16[256,2048]{1,0:T(8,128)(2,1)S(1)} %add_convert_fusion.1), channel_id=1, source_target_pairs={{0,8},{8,0},{16,24},{24,16},{1,9},{9,1},{17,25},{25,17},{2,10},{10... | collective-permute-start | bytes 3145736 | tf_op jit(solution)/shard_map/ppermute | solution.py:628
  476.1 217.6 %reduce-scatter.7.cloned.1.call-start = ((), (), s32[]{:S(2)}) async-start(), calls=%async_computation.8 | async-start | bytes 9437184 | tf_op jit(solution)/shard_map/reduce_scatter | solution.py:671
  508.3 45.3 %collective-permute-start.14 = (bf16[512,2048]{1,0:T(8,128)(2,1)S(1)}, bf16[512,2048]{1,0:T(8,128)(2,1)S(1)}, u32[]{:S(2)}, u32[]{:S(2)}) collective-permute-start(bf16[512,2048]{1,0:T(8,128)(2,1)S(1)} %get-tuple-element.54), channel_id=1, source_target_pairs={{0,8},{8,0},{16,24},{24,16},{1,9},{9,1},{17,25},{25,17},{2,10},{10... | collective-permute-start | bytes 6291464 | tf_op jit(solution)/shard_map/ppermute | solution.py:628
  509.1 44.7 %collective-permute-start.15 = (bf16[512,2048]{1,0:T(8,128)(2,1)S(1)}, bf16[512,2048]{1,0:T(8,128)(2,1)S(1)}, u32[]{:S(2)}, u32[]{:S(2)}) collective-permute-start(bf16[512,2048]{1,0:T(8,128)(2,1)S(1)} %get-tuple-element.54), channel_id=1, source_target_pairs={{0,16},{8,24},{16,0},{24,8},{1,17},{9,25},{17,1},{25,9},{2,18},{10... | collective-permute-start | bytes 6291464 | tf_op jit(solution)/shard_map/ppermute | solution.py:628
  553.7 22.3 %collective-permute-start.16 = (bf16[256,2048]{1,0:T(8,128)(2,1)S(1)}, bf16[256,2048]{1,0:T(8,128)(2,1)S(1)}, u32[]{:S(2)}, u32[]{:S(2)}) collective-permute-start(bf16[256,2048]{1,0:T(8,128)(2,1)S(1)} %slice.252), channel_id=1, source_target_pairs={{0,16},{8,24},{16,0},{24,8},{1,17},{9,25},{17,1},{25,9},{2,18},{10... | collective-permute-start | bytes 3145736 | tf_op jit(solution)/shard_map/ppermute | solution.py:628
  581.3 204.6 %reduce-scatter.9.cloned.1.call-start = ((), (), s32[]{:S(2)}) async-start(), calls=%async_computation.9 | async-start | bytes 7077888 | tf_op jit(solution)/shard_map/reduce_scatter | solution.py:671
  679.9 143.6 %reduce-scatter.11.cloned.1.call-start = ((), (), s32[]{:S(2)}) async-start(), calls=%async_computation.10 | async-start | bytes 2359296 | tf_op jit(solution)/shard_map/reduce_scatter | solution.py:677
  (53 other events, 460.3 us)
Sparse Core Ops, SparseCore 0:
  48.7 65.8 all-gather.3
  124.6 83.7 all-gather.5
  210.0 80.5 all-gather.7
  476.2 86.1 reduce-scatter.4
  581.4 87.1 reduce-scatter.6
  680.0 66.9 reduce-scatter.8
  786.0 33.4 reduce-scatter.10

commit v9 on v8

--- a/solution.py
+++ b/solution.py
@@ -595,7 +595,7 @@
     rows = left.shape[1]
     inside, anywhere = pl.BlockSpec(memory_space=pltpu.VMEM), pl.BlockSpec(memory_space=pl.ANY)
     return pl.pallas_call(
-        functools.partial(send_back_kernel, seq, plan, math.gcd(512, model)),
+        functools.partial(send_back_kernel, seq, plan, math.gcd(1024, model)),
         out_shape=[
             jax.ShapeDtypeStruct((landings(seq), rows, model), BF),
             jax.ShapeDtypeStruct(pieces.shape, pieces.dtype),

time: 841 us -> 841 us (level)
  no operation moved by 1% of the time
where the time goes in v9:
time: 841 us; the launch traced here: 833 us
  Pallas kernels  381 us (45%)
  waiting for transfers between devices  207 us (25%)
  matrix products  89.6 us (11%)
  other arithmetic  72 us (9%)
  local copies, waits for them, and re-layouts  45.6 us (5%)
  starting transfers between devices  21.4 us (3%)
  between operations  16.1 us (2%)
    ppermute x18, waiting for transfers between devices, shift(): return lax.ppermute(values, 'seq', pairs)  205 us
    pallas_call x1, Pallas kernels, forward_back(): pl.pallas_call(functools.partial(forward_back_kernel, seq, math.gcd(1024,...  155 us
    pallas_call x1, Pallas kernels, send_back(): pl.pallas_call(functools.partial(send_back_kernel, seq, plan, math.gcd(10...  87.4 us
    pallas_call x1, Pallas kernels, attend_back(): pl.pallas_call(functools.partial(attend_back_kernel, scaling, plan), out_...  70.9 us
    dot_general x4, matrix products, rows_product(): lax.dot_general(left, right, (((0,), (0,)), ((), ())), preferred_element_...  65.5 us
    pallas_call x1, Pallas kernels, opening(): pl.pallas_call(functools.partial(opening_kernel, seq, dp), out_shape=(jax...  32.8 us
    unnamed x125, local copies, waits for them, and re-layouts  29.8 us
    ppermute x18, starting transfers between devices, shift(): return lax.ppermute(values, 'seq', pairs)  21.2 us
  transfers between devices with their start and end apart: 25, of which 12 were waited for; matrix products, arithmetic and copies ran while one was open for 18% of the time, Pallas kernels for 23%

profile of v9, /device:TPU:0, one launch (start us, length us, event | category | flops | bytes accessed | tf_op | source)
XLA Modules:
  0.0 832.9 jit_solution(4742623576146384012)
XLA Ops:
  15.7 32.8 %opening.1 = (bf16[4,64,1536]{2,1,0:T(8,128)(2,1)}, bf16[4,64,2048]{2,1,0:T(8,128)(2,1)}, f32[8,4,8,128]{3,2,1,0:T(8,128)}, bf16[8,64,2048]{2,1,0:T(8,128)(2,1)}) custom-call(bf16[4,64,1536]{2,1,0:T(8,128)(2,1)} %reshape.346.pieces, bf16[4,64,2048]{2,1,0:T(8,128)(2,1)} %bitcast.166, f32[8,128]{1,0:T(8,128)} %bitcast_convert_fusion.small, bf16[64,2048]{1,0:T(8,128)(2,1)} %shard.1), custom_call_target="tpu_custom_call" | custom-call | tf_op jit(solution)/shard_map/opening/pallas_call | solution.py:132
  50.8 45.5 %collective-permute-done = bf16[512,2048]{1,0:T(8,128)(2,1)S(1)} collective-permute-done((bf16[512,2048]{1,0:T(8,128)(2,1)S(1)}, bf16[512,2048]{1,0:T(8,128)(2,1)S(1)}, u32[]{:S(2)}, u32[]{:S(2)}) %collective-permute-start) | collective-permute-done | bytes 2097184 | tf_op jit(solution)/shard_map/ppermute | solution.py:628
  100.1 20.9 %collective-permute-done.2 = bf16[256,2048]{1,0:T(8,128)(2,1)S(1)} collective-permute-done((bf16[256,2048]{1,0:T(8,128)(2,1)S(1)}, bf16[256,2048]{1,0:T(8,128)(2,1)S(1)}, u32[]{:S(2)}, u32[]{:S(2)}) %collective-permute-start.2) | collective-permute-done | bytes 1048608 | tf_op jit(solution)/shard_map/ppermute | solution.py:628
  137.4 5.2 fusion.30
  159.4 19.8 %attend.1 = bf16[4,2,256,512]{3,2,1,0:T(8,128)(2,1)S(1)} custom-call(s32[4]{0:T(128)S(1)} %iota_xor_fusion.where, bf16[4,2,256,1536]{3,2,1,0:T(8,128)(2,1)} %bitcast.160), custom_call_target="tpu_custom_call" | custom-call | bytes 62914560 | tf_op jit(solution)/shard_map/attend/pallas_call | solution.py:253
  185.1 21.2 %collective-permute-done.5 = bf16[256,2048]{1,0:T(8,128)(2,1)} collective-permute-done((bf16[256,2048]{1,0:T(8,128)(2,1)S(1)}, bf16[256,2048]{1,0:T(8,128)(2,1)}, u32[]{:S(2)}, u32[]{:S(2)}) %collective-permute-start.5) | collective-permute-done | bytes 1048608 | tf_op jit(solution)/shard_map/ppermute | solution.py:628
  231.4 14.4 %collective-permute-done.12 = bf16[256,2048]{1,0:T(8,128)(2,1)S(1)} collective-permute-done((bf16[256,2048]{1,0:T(8,128)(2,1)S(1)}, bf16[256,2048]{1,0:T(8,128)(2,1)S(1)}, u32[]{:S(2)}, u32[]{:S(2)}) %collective-permute-start.12) | collective-permute-done | bytes 1048608 | tf_op jit(solution)/shard_map/ppermute | solution.py:628
  247.3 22.3 %collective-permute-done.4 = bf16[256,2048]{1,0:T(8,128)(2,1)S(1)} collective-permute-done((bf16[256,2048]{1,0:T(8,128)(2,1)S(1)}, bf16[256,2048]{1,0:T(8,128)(2,1)S(1)}, u32[]{:S(2)}, u32[]{:S(2)}) %collective-permute-start.4) | collective-permute-done | bytes 1048608 | tf_op jit(solution)/shard_map/ppermute | solution.py:628
  269.7 20.4 %collective-permute-done.6 = bf16[256,2048]{1,0:T(8,128)(2,1)S(1)} collective-permute-done((bf16[256,2048]{1,0:T(8,128)(2,1)S(1)}, bf16[256,2048]{1,0:T(8,128)(2,1)S(1)}, u32[]{:S(2)}, u32[]{:S(2)}) %collective-permute-start.6) | collective-permute-done | bytes 1048608 | tf_op jit(solution)/shard_map/ppermute | solution.py:628
  297.1 155.1 %forward_back.1 = (bf16[8,256,2048]{2,1,0:T(8,128)(2,1)}, bf16[8,256,2048]{2,1,0:T(8,128)(2,1)}, bf16[8,256,2048]{2,1,0:T(8,128)(2,1)}, bf16[8,256,2048]{2,1,0:T(8,128)(2,1)}, bf16[6,256,2048]{2,1,0:T(8,128)(2,1)}) custom-call(bf16[512,2048]{1,0:T(8,128)(2,1)} %add_convert_fusion.mine, bf16[8,256,2048]{2,1,0:T(8,128)(2,1)} %copy-done.36, ...), custom_call_target="tpu_custom_call" | custom-call | flops 68719476736 | bytes 419430400 | tf_op jit(solution)/shard_map/forward_back/pallas_call | solution.py:525
  452.2 23.8 %convolution_bitcast_fusion = bf16[2048,2048]{1,0:T(8,128)(2,1)} fusion(bf16[8,256,2048]{2,1,0:T(8,128)(2,1)} %get-tuple-element.51, bf16[8,256,2048]{2,1,0:T(8,128)(2,1)} %copy-done.36), kind=kOutput, calls=%fused_computation | convolution fusion | flops 17179869184 | bytes 25165824 | tf_op jit(solution)/shard_map/dot_general | solution.py:34
  476.1 4.6 fusion.45
  487.7 20.6 %fusion.63 = bf16[2048,2048]{1,0:T(8,128)(2,1)} fusion(bf16[2048,2048]{1,0:T(8,128)(2,1)S(1)} %bitcast.206, bf16[2048,2048]{1,0:T(8,128)(2,1)S(1)} %bitcast.209), kind=kOutput, calls=%fused_computation.164 | convolution fusion | flops 17179869184 | bytes 25165824 | tf_op jit(solution)/shard_map/dot_general | solution.py:34
  510.1 43.5 %collective-permute-done.14 = bf16[512,2048]{1,0:T(8,128)(2,1)S(1)} collective-permute-done((bf16[512,2048]{1,0:T(8,128)(2,1)S(1)}, bf16[512,2048]{1,0:T(8,128)(2,1)S(1)}, u32[]{:S(2)}, u32[]{:S(2)}) %collective-permute-start.14) | collective-permute-done | bytes 2097184 | tf_op jit(solution)/shard_map/ppermute | solution.py:628
  561.5 14.4 %collective-permute-done.16 = bf16[256,2048]{1,0:T(8,128)(2,1)S(1)} collective-permute-done((bf16[256,2048]{1,0:T(8,128)(2,1)S(1)}, bf16[256,2048]{1,0:T(8,128)(2,1)S(1)}, u32[]{:S(2)}, u32[]{:S(2)}) %collective-permute-start.16) | collective-permute-done | bytes 1048608 | tf_op jit(solution)/shard_map/ppermute | solution.py:628
  581.2 5.4 pad_maximum_fusion
  586.6 70.9 %attend_back.1 = (bf16[4,2,256,1536]{3,2,1,0:T(8,128)(2,1)}, bf16[6,256,2048]{2,1,0:T(8,128)(2,1)}) custom-call(bf16[4,2,256,1536]{3,2,1,0:T(8,128)(2,1)} %bitcast.161, bf16[4,2,256,512]{3,2,1,0:T(8,128)(2,1)S(1)} %bitcast.154, bf16[8,256,2048]{2,1,0:T(8,128)(2,1)} %get-tuple-element.48.terms), custom_call_target="tpu_custom_call" | custom-call | bytes 251658240 | tf_op jit(solution)/shard_map/attend_back/pallas_call | solution.py:396
  657.6 4.2 add_bitcast_fusion.1
  664.6 15.1 %fusion.64 = bf16[2048,1536]{1,0:T(8,128)(2,1)} fusion(bf16[2048,2048]{1,0:T(8,128)(2,1)S(1)} %pad_maximum_fusion, bf16[2048,1536]{1,0:T(8,128)(2,1)S(1)} %bitcast.203), kind=kOutput, calls=%fused_computation.165 | convolution fusion | flops 12884901888 | bytes 20971520 | tf_op jit(solution)/shard_map/dot_general | solution.py:34
  687.6 6.0 fusion.65
  694.8 87.4 %send_back.1 = (bf16[6,256,2048]{2,1,0:T(8,128)(2,1)S(1)}, bf16[4,64,2048]{2,1,0:T(8,128)(2,1)S(1)}) custom-call(bf16[8,256,1536]{2,1,0:T(8,128)(2,1)} %bitcast.200, bf16[2048,1536]{1,0:T(8,128)(2,1)} %bitcast.193, bf16[4,64,2048]{2,1,0:T(8,128)(2,1)S(1)} %copy-done.3), custom_call_target="tpu_custom_call" | custom-call | flops 12884901888 | bytes 251658240 | tf_op jit(solution)/shard_map/send_back/pallas_call | solution.py:597
  785.0 6.1 fusion.49
  797.9 15.2 %closing.1 = (f32[8,128]{1,0:T(8,128)}, f32[64,6144]{1,0:T(8,128)}) custom-call(f32[4,8,8,128]{3,2,1,0:T(8,128)} %copy.42, bf16[4,64,1536]{2,1,0:T(8,128)(2,1)} %reduce-scatter.9.cloned.1.call-done.pieces), custom_call_target="tpu_custom_call" | custom-call | tf_op jit(solution)/shard_map/closing/pallas_call | solution.py:199
  814.6 7.0 fusion.35
  (275 shorter events, 135.0 us)
Async XLA Ops:
  7.2 117.3 %all-gather.4.cloned.1.call-start = ((), (), s32[]{:S(2)}) async-start(), calls=%async_computation.4 | async-start | bytes 7077888 | tf_op jit(solution)/shard_map/all_gather | solution.py:666
  48.6 159.8 %all-gather.6.cloned.1.call-start = ((), (), s32[]{:S(2)}) async-start(), calls=%async_computation.5 | async-start | bytes 9437184 | tf_op jit(solution)/shard_map/all_gather | solution.py:666
  48.6 47.7 %collective-permute-start = (bf16[512,2048]{1,0:T(8,128)(2,1)S(1)}, bf16[512,2048]{1,0:T(8,128)(2,1)S(1)}, u32[]{:S(2)}, u32[]{:S(2)}) collective-permute-start(bf16[512,2048]{1,0:T(8,128)(2,1)S(1)} %bitcast.155), channel_id=1, source_target_pairs={{0,8},{8,0},{16,24},{24,16},{1,9},{9,1},{17,25},{25,17},{2,10},{10... | collective-permute-start | bytes 6291464 | tf_op jit(solution)/shard_map/ppermute | solution.py:628
  49.7 47.9 %collective-permute-start.1 = (bf16[512,2048]{1,0:T(8,128)(2,1)S(1)}, bf16[512,2048]{1,0:T(8,128)(2,1)S(1)}, u32[]{:S(2)}, u32[]{:S(2)}) collective-permute-start(bf16[512,2048]{1,0:T(8,128)(2,1)S(1)} %bitcast.156), channel_id=1, source_target_pairs={{0,16},{8,24},{16,0},{24,8},{1,17},{9,25},{17,1},{25,9},{2,18},{10... | collective-permute-start | bytes 6291464 | tf_op jit(solution)/shard_map/ppermute | solution.py:628
  96.4 24.5 %collective-permute-start.2 = (bf16[256,2048]{1,0:T(8,128)(2,1)S(1)}, bf16[256,2048]{1,0:T(8,128)(2,1)S(1)}, u32[]{:S(2)}, u32[]{:S(2)}) collective-permute-start(bf16[256,2048]{1,0:T(8,128)(2,1)S(1)} %slice.234), channel_id=1, source_target_pairs={{0,16},{8,24},{16,0},{24,8},{1,17},{9,25},{17,1},{25,9},{2,18},{10... | collective-permute-start | bytes 3145736 | tf_op jit(solution)/shard_map/ppermute | solution.py:628
  99.0 24.4 %collective-permute-start.3 = (bf16[256,2048]{1,0:T(8,128)(2,1)S(1)}, bf16[256,2048]{1,0:T(8,128)(2,1)S(1)}, u32[]{:S(2)}, u32[]{:S(2)}) collective-permute-start(bf16[256,2048]{1,0:T(8,128)(2,1)S(1)} %slice.235), channel_id=1, source_target_pairs={{0,8},{8,0},{16,24},{24,16},{1,9},{9,1},{17,25},{25,17},{2,10},{10... | collective-permute-start | bytes 3145736 | tf_op jit(solution)/shard_map/ppermute | solution.py:628
  124.5 172.6 %all-gather.8.cloned.1.call-start = ((), (), s32[]{:S(2)}) async-start(), calls=%async_computation.6 | async-start | bytes 9437184 | tf_op jit(solution)/shard_map/all_gather | solution.py:719
  130.1 55.0 %collective-permute-start.10 = (bf16[512,2048]{1,0:T(8,128)(2,1)S(1)}, bf16[512,2048]{1,0:T(8,128)(2,1)}, u32[]{:S(2)}, u32[]{:S(2)}) collective-permute-start(bf16[512,2048]{1,0:T(8,128)(2,1)S(1)} %fusion.38), channel_id=1, source_target_pairs={{0,8},{8,0},{16,24},{24,16},{1,9},{9,1},{17,25},{25,17},{2,10},{10... | collective-permute-start | bytes 6291464 | tf_op jit(solution)/shard_map/ppermute | solution.py:628
  131.3 53.8 %collective-permute-start.11 = (bf16[512,2048]{1,0:T(8,128)(2,1)S(1)}, bf16[512,2048]{1,0:T(8,128)(2,1)}, u32[]{:S(2)}, u32[]{:S(2)}) collective-permute-start(bf16[512,2048]{1,0:T(8,128)(2,1)S(1)} %fusion.38), channel_id=1, source_target_pairs={{0,16},{8,24},{16,0},{24,8},{1,17},{9,25},{17,1},{25,9},{2,18},{10... | collective-permute-start | bytes 6291464 | tf_op jit(solution)/shard_map/ppermute | solution.py:628
  183.3 23.0 %collective-permute-start.5 = (bf16[256,2048]{1,0:T(8,128)(2,1)S(1)}, bf16[256,2048]{1,0:T(8,128)(2,1)}, u32[]{:S(2)}, u32[]{:S(2)}) collective-permute-start(bf16[256,2048]{1,0:T(8,128)(2,1)S(1)} %get-tuple-element.91), channel_id=1, source_target_pairs={{0,8},{8,0},{16,24},{24,16},{1,9},{9,1},{17,25},{25,17},{2,10},{10... | collective-permute-start | bytes 3145736 | tf_op jit(solution)/shard_map/ppermute | solution.py:628
  184.2 22.6 %collective-permute-start.7 = (bf16[256,2048]{1,0:T(8,128)(2,1)S(1)}, bf16[256,2048]{1,0:T(8,128)(2,1)}, u32[]{:S(2)}, u32[]{:S(2)}) collective-permute-start(bf16[256,2048]{1,0:T(8,128)(2,1)S(1)} %get-tuple-element.92), channel_id=1, source_target_pairs={{0,16},{8,24},{16,0},{24,8},{1,17},{9,25},{17,1},{25,9},{2,18},{10... | collective-permute-start | bytes 3145736 | tf_op jit(solution)/shard_map/ppermute | solution.py:628
  208.4 370.0 %reduce-scatter.5.cloned.1.call-start = ((), (), s32[]{:S(2)}) async-start(), calls=%async_computation.7 | async-start | bytes 9437184 | tf_op jit(solution)/shard_map/reduce_scatter | solution.py:677
  219.7 26.1 %collective-permute-start.12 = (bf16[256,2048]{1,0:T(8,128)(2,1)S(1)}, bf16[256,2048]{1,0:T(8,128)(2,1)S(1)}, u32[]{:S(2)}, u32[]{:S(2)}) collective-permute-start(bf16[256,2048]{1,0:T(8,128)(2,1)S(1)} %slice.248), channel_id=1, source_target_pairs={{0,16},{8,24},{16,0},{24,8},{1,17},{9,25},{17,1},{25,9},{2,18},{10... | collective-permute-start | bytes 3145736 | tf_op jit(solution)/shard_map/ppermute | solution.py:628
  221.2 26.1 %collective-permute-start.13 = (bf16[256,2048]{1,0:T(8,128)(2,1)S(1)}, bf16[256,2048]{1,0:T(8,128)(2,1)S(1)}, u32[]{:S(2)}, u32[]{:S(2)}) collective-permute-start(bf16[256,2048]{1,0:T(8,128)(2,1)S(1)} %slice.251), channel_id=1, source_target_pairs={{0,8},{8,0},{16,24},{24,16},{1,9},{9,1},{17,25},{25,17},{2,10},{10... | collective-permute-start | bytes 3145736 | tf_op jit(solution)/shard_map/ppermute | solution.py:628
  225.3 44.4 %collective-permute-start.4 = (bf16[256,2048]{1,0:T(8,128)(2,1)S(1)}, bf16[256,2048]{1,0:T(8,128)(2,1)S(1)}, u32[]{:S(2)}, u32[]{:S(2)}) collective-permute-start(bf16[256,2048]{1,0:T(8,128)(2,1)S(1)} %slice.238), channel_id=1, source_target_pairs={{0,8},{8,0},{16,24},{24,16},{1,9},{9,1},{17,25},{25,17},{2,10},{10... | collective-permute-start | bytes 3145736 | tf_op jit(solution)/shard_map/ppermute | solution.py:628
  226.0 64.4 %collective-permute-start.9 = (bf16[256,2048]{1,0:T(8,128)(2,1)S(1)}, bf16[256,2048]{1,0:T(8,128)(2,1)S(1)}, u32[]{:S(2)}, u32[]{:S(2)}) collective-permute-start(bf16[256,2048]{1,0:T(8,128)(2,1)S(1)} %slice.245), channel_id=1, source_target_pairs={{0,16},{8,24},{16,0},{24,8},{1,17},{9,25},{17,1},{25,9},{2,18},{10... | collective-permute-start | bytes 3145736 | tf_op jit(solution)/shard_map/ppermute | solution.py:628
  228.3 61.7 %collective-permute-start.6 = (bf16[256,2048]{1,0:T(8,128)(2,1)S(1)}, bf16[256,2048]{1,0:T(8,128)(2,1)S(1)}, u32[]{:S(2)}, u32[]{:S(2)}) collective-permute-start(bf16[256,2048]{1,0:T(8,128)(2,1)S(1)} %add_convert_fusion.2), channel_id=1, source_target_pairs={{0,16},{8,24},{16,0},{24,8},{1,17},{9,25},{17,1},{25,9},{2,18},{10... | collective-permute-start | bytes 3145736 | tf_op jit(solution)/shard_map/ppermute | solution.py:628
  245.8 45.4 %collective-permute-start.8 = (bf16[256,2048]{1,0:T(8,128)(2,1)S(1)}, bf16[256,2048]{1,0:T(8,128)(2,1)S(1)}, u32[]{:S(2)}, u32[]{:S(2)}) collective-permute-start(bf16[256,2048]{1,0:T(8,128)(2,1)S(1)} %add_convert_fusion.1), channel_id=1, source_target_pairs={{0,8},{8,0},{16,24},{24,16},{1,9},{9,1},{17,25},{25,17},{2,10},{10... | collective-permute-start | bytes 3145736 | tf_op jit(solution)/shard_map/ppermute | solution.py:628
  476.0 217.6 %reduce-scatter.7.cloned.1.call-start = ((), (), s32[]{:S(2)}) async-start(), calls=%async_computation.8 | async-start | bytes 9437184 | tf_op jit(solution)/shard_map/reduce_scatter | solution.py:671
  508.3 45.3 %collective-permute-start.14 = (bf16[512,2048]{1,0:T(8,128)(2,1)S(1)}, bf16[512,2048]{1,0:T(8,128)(2,1)S(1)}, u32[]{:S(2)}, u32[]{:S(2)}) collective-permute-start(bf16[512,2048]{1,0:T(8,128)(2,1)S(1)} %get-tuple-element.54), channel_id=1, source_target_pairs={{0,8},{8,0},{16,24},{24,16},{1,9},{9,1},{17,25},{25,17},{2,10},{10... | collective-permute-start | bytes 6291464 | tf_op jit(solution)/shard_map/ppermute | solution.py:628
  508.9 44.8 %collective-permute-start.15 = (bf16[512,2048]{1,0:T(8,128)(2,1)S(1)}, bf16[512,2048]{1,0:T(8,128)(2,1)S(1)}, u32[]{:S(2)}, u32[]{:S(2)}) collective-permute-start(bf16[512,2048]{1,0:T(8,128)(2,1)S(1)} %get-tuple-element.54), channel_id=1, source_target_pairs={{0,16},{8,24},{16,0},{24,8},{1,17},{9,25},{17,1},{25,9},{2,18},{10... | collective-permute-start | bytes 6291464 | tf_op jit(solution)/shard_map/ppermute | solution.py:628
  553.7 22.2 %collective-permute-start.16 = (bf16[256,2048]{1,0:T(8,128)(2,1)S(1)}, bf16[256,2048]{1,0:T(8,128)(2,1)S(1)}, u32[]{:S(2)}, u32[]{:S(2)}) collective-permute-start(bf16[256,2048]{1,0:T(8,128)(2,1)S(1)} %slice.252), channel_id=1, source_target_pairs={{0,16},{8,24},{16,0},{24,8},{1,17},{9,25},{17,1},{25,9},{2,18},{10... | collective-permute-start | bytes 3145736 | tf_op jit(solution)/shard_map/ppermute | solution.py:628
  581.2 203.8 %reduce-scatter.9.cloned.1.call-start = ((), (), s32[]{:S(2)}) async-start(), calls=%async_computation.9 | async-start | bytes 7077888 | tf_op jit(solution)/shard_map/reduce_scatter | solution.py:671
  679.7 143.3 %reduce-scatter.11.cloned.1.call-start = ((), (), s32[]{:S(2)}) async-start(), calls=%async_computation.10 | async-start | bytes 2359296 | tf_op jit(solution)/shard_map/reduce_scatter | solution.py:677
  (53 other events, 459.8 us)
Sparse Core Ops, SparseCore 0:
  48.7 65.8 all-gather.3
  124.6 83.7 all-gather.5
  210.0 80.5 all-gather.7
  476.2 86.2 reduce-scatter.4
  581.3 87.1 reduce-scatter.6
  679.9 66.9 reduce-scatter.8
  785.1 33.3 reduce-scatter.10
